TPU v7x, 32 devices: a whole 2x2x4 slice. The times are simulated.
32 devices in a mesh: node: 16 (over z, x, core), tp: 2 (over y).
Axes of the slice: x: 2, y: 2, z: 4, core: 2. Of those that a mesh axis runs over, the one named last changes fastest.
Arguments:
- query_rows: bfloat16 [4096, 8192], P('node', 'tp'), may hold values from -6 to 6
- key_rows: bfloat16 [4096, 1024], P('node', 'tp'), may hold values from -5 to 5
- value_rows: bfloat16 [4096, 1024], P('node', 'tp'), may hold values from -6 to 6
- out_weight: bfloat16 [8192, 4096], P('tp'), may hold values from -0.0625 to 0.0625
- out_grad: bfloat16 [4096, 4096], P(('node', 'tp')), may hold values from -6 to 6
- owner_slot: int32 [16], replicated, may hold values from 0 to 15, each once
Outputs:
- projected: bfloat16 [4096, 4096], P(('node', 'tp'))
- query_grad: bfloat16 [4096, 8192], P('node', 'tp')
- key_grad: bfloat16 [4096, 1024], P('node', 'tp')
- value_grad: bfloat16 [4096, 1024], P('node', 'tp')
Inputs may be any that keep to these rules, and one draw needn't show every extreme that they name: `owner_slot`: every slot holds exactly one tree node.
All inputs are finite; a program needn't handle non-finite values.
Results may differ from a plain program's by a relative error of at most 0.017.
Values may be sent and summed in bfloat16 or wider, within the bound.
No kernel may reach another device: no remote copies, remote signals or barrier semaphores. Data moves between devices by JAX's collectives and lax.ppermute only.
A program may use at most 256 MiB of HBM per device.

v0:
```python
import jax
import jax.numpy as jnp
from jax import lax
from jax.sharding import PartitionSpec as P

HEAD_DIM = 128
NODE_LEN = 256
CHAIN = 8
LEAVES = 8


masked_score = -1e30


def local(query_rows, key_rows, value_rows, out_weight, out_grad, owner_slot):
    node_count = owner_slot.shape[0]
    tree_nodes = CHAIN + LEAVES
    local_rows = query_rows.shape[0]
    slots_here = local_rows // NODE_LEN
    kv_width = key_rows.shape[1]
    kv_heads = kv_width // HEAD_DIM
    head_group = query_rows.shape[1] // kv_width
    score_scale = HEAD_DIM ** (-0.5)
    first_slot = lax.axis_index("node") * slots_here
    numbers = jnp.arange(node_count, dtype=jnp.int32)
    matches = (owner_slot[:, None] == numbers[None, :]).astype(jnp.int32)
    node_of_slot = jnp.sum(matches * numbers[:, None], axis=0)
    packed = jnp.concatenate([key_rows, value_rows], axis=1).reshape(
        slots_here, NODE_LEN, 2 * kv_width
    )
    chain_steps = jnp.arange(CHAIN, dtype=jnp.int32)
    stored = lax.all_gather(packed, "node", axis=0, tiled=True)
    upstream_all = lax.dot_general(
        lax.all_gather(out_grad, "tp", axis=0, tiled=True),
        out_weight,
        (((1,), (1,)), ((), ())),
        preferred_element_type=jnp.float32,
    ).astype(jnp.bfloat16)
    positions = jnp.arange(NODE_LEN, dtype=jnp.int32)
    causal = positions[None, :] <= positions[:, None]
    query_blocks = query_rows.reshape(slots_here, NODE_LEN, kv_heads, head_group, HEAD_DIM)
    upstream_blocks = upstream_all.reshape(slots_here, NODE_LEN, kv_heads, head_group, HEAD_DIM)
    grad_store = jnp.zeros((stored.shape[0], NODE_LEN, 2 * kv_width), jnp.float32)
    tree_node = node_of_slot[first_slot + 0]
    node_depth = jnp.minimum(tree_node % tree_nodes, CHAIN)
    lineage = owner_slot[tree_node // tree_nodes * tree_nodes + chain_steps]
    own_block = packed[0]
    queries = query_blocks[0]
    upstream = upstream_blocks[0]

    def block_data(block_no):
        far_block = lax.dynamic_index_in_dim(
            stored, lineage[jnp.minimum(block_no, CHAIN - 1)], 0, keepdims=False
        )
        chosen = jnp.where(block_no < node_depth, far_block, own_block)
        keys_here = chosen[:, :kv_width].reshape(NODE_LEN, kv_heads, HEAD_DIM)
        values_here = chosen[:, kv_width:].reshape(NODE_LEN, kv_heads, HEAD_DIM)
        return (keys_here, values_here)

    def scan_stats(block_no, running):
        row_max, row_sum, score_store = running
        keys_here = block_data(block_no)[0]
        scores = (
            jnp.einsum("rkgd,skd->kgrs", queries, keys_here, preferred_element_type=jnp.float32)
            * score_scale
        )
        allowed = jnp.logical_or(block_no < node_depth, causal)
        scores = jnp.where(allowed[None, None], scores, masked_score)
        score_store = lax.dynamic_update_index_in_dim(score_store, scores, block_no, 0)
        new_max = jnp.maximum(row_max, jnp.max(scores, axis=-1))
        row_sum = row_sum * jnp.exp(row_max - new_max) + jnp.sum(
            jnp.exp(scores - new_max[..., None]), axis=-1
        )
        return (new_max, row_sum, score_store)

    start_max = jnp.full((kv_heads, head_group, NODE_LEN), masked_score, jnp.float32)
    start_sum = jnp.zeros((kv_heads, head_group, NODE_LEN), jnp.float32)
    empty_scores = jnp.zeros((CHAIN + 1, kv_heads, head_group, NODE_LEN, NODE_LEN), jnp.float32)
    row_max, row_sum, score_store = lax.fori_loop(
        0, node_depth + 1, scan_stats, (start_max, start_sum, empty_scores)
    )

    def block_probability(block_no):
        scores = lax.dynamic_index_in_dim(score_store, block_no, 0, keepdims=False)
        return jnp.exp(scores - row_max[..., None]) / row_sum[..., None]

    def forward_block(block_no, running_sum):
        values_here = block_data(block_no)[1]
        weights = block_probability(block_no).astype(jnp.bfloat16)
        return running_sum + jnp.einsum(
            "kgrs,skd->rkgd", weights, values_here, preferred_element_type=jnp.float32
        )

    zero_rows = jnp.zeros((NODE_LEN, kv_heads, head_group, HEAD_DIM), jnp.float32)
    attended = lax.fori_loop(0, node_depth + 1, forward_block, zero_rows).astype(jnp.bfloat16)
    correction = jnp.transpose(
        jnp.sum(upstream.astype(jnp.float32) * attended.astype(jnp.float32), axis=-1), (1, 2, 0)
    )

    def backward_block(block_no, running):
        query_sum, grad_rows, own_grad = running
        keys_here, values_here = block_data(block_no)
        probability = block_probability(block_no)
        weights = probability.astype(jnp.bfloat16)
        d_prob = jnp.einsum(
            "rkgd,skd->kgrs", upstream, values_here, preferred_element_type=jnp.float32
        )
        d_score = (probability * (d_prob - correction[..., None]) * score_scale).astype(
            jnp.bfloat16
        )
        query_sum = query_sum + jnp.einsum(
            "kgrs,skd->rkgd", d_score, keys_here, preferred_element_type=jnp.float32
        )
        key_part = jnp.einsum(
            "kgrs,rkgd->skd", d_score, queries, preferred_element_type=jnp.float32
        ).reshape(NODE_LEN, kv_width)
        value_part = jnp.einsum(
            "kgrs,rkgd->skd", weights, upstream, preferred_element_type=jnp.float32
        ).reshape(NODE_LEN, kv_width)
        block_grad = jnp.concatenate([key_part, value_part], axis=1)
        is_far = block_no < node_depth
        target = lineage[jnp.minimum(block_no, CHAIN - 1)]
        current = lax.dynamic_index_in_dim(grad_rows, target, 0, keepdims=False)
        grad_rows = lax.dynamic_update_index_in_dim(
            grad_rows, current + jnp.where(is_far, block_grad, 0.0), target, 0
        )
        own_grad = jnp.where(is_far, own_grad, block_grad)
        return (query_sum, grad_rows, own_grad)

    own_start = jnp.zeros((NODE_LEN, 2 * kv_width), jnp.float32)
    query_sum, grad_store, own_grad = lax.fori_loop(
        0, node_depth + 1, backward_block, (zero_rows, grad_store, own_start)
    )
    query_parts = query_sum.astype(jnp.bfloat16)
    own_parts = [own_grad]
    attended_all = attended.reshape(local_rows, query_rows.shape[1])
    projected = lax.psum_scatter(
        jnp.dot(attended_all, out_weight, preferred_element_type=jnp.float32).astype(jnp.bfloat16),
        "tp",
        scatter_dimension=0,
        tiled=True,
    )
    own_all = jnp.stack(own_parts)
    received = lax.psum_scatter(
        grad_store.astype(jnp.bfloat16), "node", scatter_dimension=0, tiled=True
    ).astype(jnp.float32)
    total_grad = own_all + received
    key_grad = total_grad[:, :, :kv_width].reshape(local_rows, kv_width).astype(jnp.bfloat16)
    value_grad = total_grad[:, :, kv_width:].reshape(local_rows, kv_width).astype(jnp.bfloat16)
    query_grad = query_parts.reshape(local_rows, query_rows.shape[1])
    return (projected, query_grad, key_grad, value_grad)


def solution(mesh):
    in_specs = (
        P("node", "tp"),
        P("node", "tp"),
        P("node", "tp"),
        P("tp", None),
        P(("node", "tp"), None),
        P(),
    )
    out_specs = (P(("node", "tp"), None), P("node", "tp"), P("node", "tp"), P("node", "tp"))
    return jax.shard_map(local, mesh=mesh, in_specs=in_specs, out_specs=out_specs, check_vma=False)
```

profile of v0, /device:TPU:0, one launch (start us, length us, event | category | flops | bytes accessed | tf_op | source)
XLA Modules:
  0.0 1025.8 jit_solution(9078785451027870556)
XLA Ops:
  17.3 3.4 copy.67
  20.8 2.7 copy.70
  23.4 22.0 %all-gather.4.cloned.1.call-done = bf16[256,4096]{1,0:T(8,128)(2,1)} async-done(((bf16[128,4096]{1,0:T(8,128)(2,1)}), bf16[256,4096]{1,0:T(8,128)(2,1)}) %all-gather.4.cloned.1.call-update) | async-done | bytes 2097168 | tf_op jit(solution)/shard_map/all_gather | solution.py:34
  45.4 17.7 %convolution_convert_fusion.1 = bf16[256,4096]{1,0:T(8,128)(2,1)} fusion(bf16[256,4096]{1,0:T(8,128)(2,1)} %all-gather.4.cloned.1.call-done, bf16[4096,4096]{1,0:T(8,128)(2,1)} %param.15), kind=kOutput, calls=%fused_computation.38 | convolution fusion | flops 8590983168 | bytes 37748736 | tf_op jit(solution)/shard_map/dot_general | solution.py:33
  63.1 4.1 copy.96
  67.1 56.0 %all-gather.6.cloned.1.call-done = bf16[4096,1024]{1,0:T(8,128)(2,1)} async-done(((bf16[256,1024]{1,0:T(8,128)(2,1)}), bf16[4096,1024]{1,0:T(8,128)(2,1)}) %all-gather.6.cloned.1.call-update) | async-done | bytes 8388624 | tf_op jit(solution)/shard_map/all_gather | solution.py:32
  123.1 12.3 %copy.71 = bf16[16,256,1024]{1,2,0:T(8,128)(2,1)} copy(bf16[16,256,1024]{2,1,0:T(8,128)(2,1)} %bitcast.200) | data formatting | bytes 16777216 | tf_op jit(solution)/shard_map/while | solution.py:95
  135.3 23.6 %broadcast_in_dim.56 = f32[9,4,8,256,256]{3,4,2,1,0:T(8,128)} broadcast(f32[]{:T(128)} %constant.106.clone.1), dimensions={} | broadcast | bytes 75497472 | tf_op jit(solution)/shard_map/broadcast_in_dim | solution.py:78
  159.0 75.6 %while.41 = (s32[]{:T(128)}, f32[4,8,256]{2,1,0:T(8,128)S(1)}, f32[4,8,256]{2,1,0:T(8,128)S(1)}, f32[9,4,8,256,256]{3,4,2,1,0:T(8,128)}, s32[]{:T(128)}, /*index...) while((s32[]{:T(128)}, f32[4,8,256]{2,1,0:T(8,128)S(1)}, ...), condition=%wide.region_4.5_spmd.clone, body=%wide.region_1.4_spmd.clone.sunk | while | flops 556023808 | bytes 71991616 | solution.py:79
  162.7 4.8 fusion.76
  167.5 8.4 bitcast_dynamic-update-slice_fusion.2
  176.0 1.9 exponential_reduce_fusion.2
  181.6 4.8 fusion.76
  186.4 8.5 bitcast_dynamic-update-slice_fusion.2
  194.9 1.9 exponential_reduce_fusion.2
  200.5 4.8 fusion.76
  205.3 8.4 bitcast_dynamic-update-slice_fusion.2
  213.7 1.9 exponential_reduce_fusion.2
  219.4 4.8 fusion.76
  224.2 8.4 bitcast_dynamic-update-slice_fusion.2
  232.6 1.9 exponential_reduce_fusion.2
  234.5 2.5 broadcast_in_dim.53.clone
  237.0 109.0 %while.39 = (s32[]{:T(128)}, f32[256,4,8,128]{0,3,2,1:T(8,128)}, s32[]{:T(128)}, s32[]{:T(128)}, s32[8]{0:T(128)S(1)}, /*index=5*/bf16[16,256,1024]{1,2,0:T(8,12...) while((s32[]{:T(128)}, f32[256,4,8,128]{0,3,2,1:T(8,128)}, ...), condition=%wide.region_6.7_spmd, body=%wide.region_5.6_spmd.sunk | while | flops 544342016 | bytes 52494628 | solution.py:95
  240.7 7.5 constant_dynamic-slice_fusion.4
  248.2 8.7 copy.105
  256.9 7.4 bitcast_add_fusion.5
  268.0 7.5 constant_dynamic-slice_fusion.4
  275.4 8.7 copy.105
  284.1 7.4 bitcast_add_fusion.5
  295.2 7.5 constant_dynamic-slice_fusion.4
  302.7 8.7 copy.105
  311.4 7.4 bitcast_add_fusion.5
  322.4 7.5 constant_dynamic-slice_fusion.4
  329.9 8.7 copy.105
  338.6 7.4 bitcast_add_fusion.5
  346.0 4.2 multiply_reduce_fusion
  350.2 7.9 broadcast_in_dim.57.clone
  358.1 2.5 broadcast_in_dim.53
  361.6 124.1 %while.40 = (s32[]{:T(128)}, f32[256,4,8,128]{0,3,2,1:T(8,128)}, f32[16,256,1024]{2,1,0:T(8,128)}, f32[256,1024]{0,1:T(8,128)}, s32[]{:T(128)}, /*index=5*/s32[]...) while((s32[]{:T(128)}, f32[256,4,8,128]{0,3,2,1:T(8,128)}, ...), condition=%wide.region_10.11_spmd, body=%wide.region_9.10_spmd.sunk | while | flops 2168979456 | bytes 92438992 | solution.py:131
  365.3 5.6 fusion.69
  370.9 2.0 copy-done.1
  376.1 5.7 fusion.70
  384.1 6.4 bitcast_add_fusion.6
  390.6 2.4 maximum_select_fusion.3
  396.6 5.6 fusion.69
  402.2 2.0 copy-done.1
  407.4 5.7 fusion.70
  415.5 6.4 bitcast_add_fusion.6
  421.9 2.4 maximum_select_fusion.3
  428.0 5.6 fusion.69
  433.6 2.0 copy-done.1
  438.8 5.7 fusion.70
  446.8 6.4 bitcast_add_fusion.6
  453.2 2.4 maximum_select_fusion.3
  459.3 5.6 fusion.69
  464.9 2.0 copy-done.1
  470.0 5.7 fusion.70
  478.1 6.4 bitcast_add_fusion.6
  485.7 9.1 convert_element_type.48
  496.4 16.7 %convolution_convert_fusion = bf16[256,4096]{1,0:T(8,128)(2,1)} fusion(bf16[256,4096]{0,1:T(8,128)(2,1)S(1)} %bitcast.198, bf16[4096,4096]{1,0:T(8,128)(2,1)} %param.15), kind=kOutput, calls=%fused_computation.37 | convolution fusion | flops 8590983168 | bytes 37748736 | tf_op jit(solution)/shard_map/dot_general | solution.py:138
  514.7 2.5 convert_element_type.47
  517.2 2.9 copy.93
  520.1 464.8 %reduce-scatter.5.cloned.1.call-done = bf16[1,256,1024]{2,1,0:T(8,128)(2,1)} async-done(((bf16[16,256,1024]{2,1,0:T(8,128)(2,1)}), bf16[1,256,1024]{2,1,0:T(8,128)(2,1)}) %reduce-scatter.5.cloned.1.call-update) | async-done | bytes 524304 | tf_op jit(solution)/shard_map/reduce_scatter | solution.py:144
  987.0 32.3 %reduce-scatter.3.cloned.1.call-done = bf16[128,4096]{1,0:T(8,128)(2,1)} async-done(((bf16[256,4096]{1,0:T(8,128)(2,1)}), bf16[128,4096]{1,0:T(8,128)(2,1)}) %reduce-scatter.3.cloned.1.call-update) | async-done | bytes 1048592 | tf_op jit(solution)/shard_map/reduce_scatter | solution.py:137
  (147 shorter events, 57.4 us)
Async XLA Ops:
  7.2 38.2 %all-gather.4.cloned.1.call-start = ((), (), s32[]{:S(2)}) async-start(), calls=%async_computation.3 | async-start | bytes 3145728 | tf_op jit(solution)/shard_map/all_gather | solution.py:34
  7.9 115.2 %all-gather.6.cloned.1.call-start = ((), (), s32[]{:S(2)}) async-start(), calls=%async_computation.5 | async-start | bytes 8912896 | tf_op jit(solution)/shard_map/all_gather | solution.py:32
  9.9 0.8 copy-start.10
  10.7 974.2 %reduce-scatter.5.cloned.1.call-start = ((), (), s32[]{:S(2)}) async-start(), calls=%async_computation.4 | async-start | bytes 8912896 | tf_op jit(solution)/shard_map/reduce_scatter | solution.py:144
  20.8 42.3 %copy-start.2 = (bf16[256,4096]{0,1:T(8,128)(2,1)}, bf16[256,4096]{0,1:T(8,128)(2,1)S(1)}, u32[]{:S(2)}) copy-start(bf16[256,4096]{0,1:T(8,128)(2,1)S(1)} %copy.67) | copy-start | bytes 6291460
  135.3 23.7 %copy-start.5 = (bf16[256,4,8,128]{3,0,2,1:T(8,128)(2,1)S(1)}, bf16[256,4,8,128]{3,0,2,1:T(8,128)(2,1)}, u32[]{:S(2)}) copy-start(bf16[256,4,8,128]{3,0,2,1:T(8,128)(2,1)} %copy.70) | copy-start | bytes 6291460
  167.5 8.4 copy-start
  186.4 8.5 copy-start
  205.3 8.4 copy-start
  224.2 8.4 copy-start
  237.0 109.0 %copy-start.9 = (bf16[256,4096]{0,1:T(8,128)(2,1)S(1)}, bf16[256,4096]{0,1:T(8,128)(2,1)}, u32[]{:S(2)}) copy-start(bf16[256,4096]{0,1:T(8,128)(2,1)} %copy.96) | copy-start | bytes 6291460
  350.2 11.4 %copy-start.3 = (bf16[256,4096]{0,1:T(8,128)(2,1)S(1)}, bf16[256,4096]{0,1:T(8,128)(2,1)}, u32[]{:S(2)}) copy-start(bf16[256,4096]{0,1:T(8,128)(2,1)} %copy-done.2) | copy-start | bytes 6291460
  370.9 2.1 copy-start.1
  381.8 0.8 copy-start.6
  383.0 7.5 copy-start.7
  384.1 8.8 copy-start.4
  402.2 2.1 copy-start.1
  413.1 0.8 copy-start.6
  414.3 7.6 copy-start.7
  415.5 8.8 copy-start.4
  433.6 2.1 copy-start.1
  444.4 0.8 copy-start.6
  445.7 7.5 copy-start.7
  446.8 8.8 copy-start.4
  464.9 2.1 copy-start.1
  475.7 0.8 copy-start.6
  477.0 7.6 copy-start.7
  478.1 7.6 copy-start.4
  494.8 1.6 copy-start.8
  494.8 524.4 %reduce-scatter.3.cloned.1.call-start = ((), (), s32[]{:S(2)}) async-start(), calls=%async_computation.2 | async-start | bytes 3145728 | tf_op jit(solution)/shard_map/reduce_scatter | solution.py:137
Sparse Core Ops, SparseCore 0:
  9.5 35.8 all-gather.3
  48.1 74.8 all-gather.5
  495.0 489.9 reduce-scatter.4
  987.6 31.5 reduce-scatter.2
where the time goes:
time: 1030 us
  waiting for transfers between devices  576 us (56%)
  local copies, waits for them, and re-layouts  176 us (17%)
  matrix products  160 us (16%)
  other arithmetic  72.5 us (7%)
  loops' own time  24.2 us (2%)
  between operations  16.5 us (2%)
    reduce_scatter x1, waiting for transfers between devices, local(): lax.psum_scatter(grad_store.astype(jnp.bfloat16), 'node', scatter_dimensi...  465 us
    dynamic_slice x8, local copies, waits for them, and re-layouts, block_probability(): scores = lax.dynamic_index_in_dim(score_store, block_no, 0, keepdims=False)  64.7 us
    all_gather x1, waiting for transfers between devices, local(): stored = lax.all_gather(packed, 'node', axis=0, tiled=True)  56 us
    dynamic_update_slice x4, other arithmetic, scan_stats(): lax.dynamic_update_index_in_dim(score_store, scores, block_no, 0)  33.8 us
    reduce_scatter x1, waiting for transfers between devices, local(): lax.psum_scatter(jnp.dot(attended_all, out_weight, preferred_element_type...  32.3 us
    dot_general x4, matrix products, forward_block(): jnp.einsum('kgrs,skd->rkgd', weights, values_here, preferred_element_type...  29.6 us
    dot_general x4, matrix products, backward_block(): jnp.einsum('kgrs,skd->rkgd', d_score, keys_here, preferred_element_type=j...  25.8 us
    broadcast_in_dim x1, local copies, waits for them, and re-layouts, local(): jnp.zeros((CHAIN + 1, kv_heads, head_group, NODE_LEN, NODE_LEN), jnp.floa...  23.6 us
  transfers between devices with their start and end apart: 4, of which 4 were waited for; matrix products, arithmetic and copies ran while one was open for 6% of the time, Pallas kernels for 0%

commit v1 on v0

v1 whole, which is shorter than its diff:
```python
import functools

import jax
import jax.numpy as jnp
from jax import lax
from jax.experimental import pallas as pl
from jax.experimental.pallas import tpu as pltpu
from jax.sharding import PartitionSpec as P

HEAD_DIM = 128
NODE_LEN = 256
CHAIN = 8
LEAVES = 8
GROUP = 4

masked_score = -1e30
score_scale = HEAD_DIM ** (-0.5)
log2_e = 1.4426950408889634


def dot(a, b):
    return jnp.dot(a, b, preferred_element_type=jnp.float32)


def dot_nt(a, b):
    return lax.dot_general(a, b, (((1,), (1,)), ((), ())), preferred_element_type=jnp.float32)


def attend(
    lineage, depth_ref, q_ref, up_ref, far_ref, own_ref,
    att_ref, dq_ref, far_grad, own_grad,
    s_ref, p_ref, qs, ups, q_t, up_t, m_ref, l_ref, acc_ref, corr_ref, grad_t,
):
    step = pl.program_id(0)
    depth = depth_ref[0]
    heads = q_ref.shape[1] // HEAD_DIM
    rows = heads * NODE_LEN
    half = HEAD_DIM
    factor = score_scale * log2_e

    def head_rows(h):
        return pl.ds(h * NODE_LEN, NODE_LEN)

    def head_columns(h):
        return pl.ds(h * HEAD_DIM, HEAD_DIM)

    for h in range(heads):
        qs[head_rows(h), :] = q_ref[:, head_columns(h)]
        ups[head_rows(h), :] = up_ref[:, head_columns(h)]

    def fold_max(s):
        return jnp.maximum(s[:, :half], s[:, half:])

    s = dot_nt(qs[...], own_ref[:, :half])
    row = lax.broadcasted_iota(jnp.int32, (rows, NODE_LEN), 0) % NODE_LEN
    col = lax.broadcasted_iota(jnp.int32, (rows, NODE_LEN), 1)
    s = jnp.where(col <= row, s, masked_score)
    s_ref[CHAIN] = s
    m_ref[...] = fold_max(s)

    def score_block(b, carry):
        s = dot_nt(qs[...], far_ref[lineage[b], :, :half])
        s_ref[b] = s
        m_ref[...] = jnp.maximum(m_ref[...], fold_max(s))
        return carry

    lax.fori_loop(0, depth, score_block, 0)
    m_ref[...] = jnp.broadcast_to(jnp.max(m_ref[...], axis=1, keepdims=True), (rows, half))

    def weigh(b, values):
        top = m_ref[...]
        s = s_ref[b]
        p_low = jnp.exp2((s[:, :half] - top) * factor)
        p_high = jnp.exp2((s[:, half:] - top) * factor)
        p = jnp.concatenate([p_low, p_high], axis=1).astype(jnp.bfloat16)
        p_ref[b] = p
        return p_low + p_high, dot(p, values)

    part_sum, part = weigh(CHAIN, own_ref[:, half:])
    l_ref[...] = part_sum
    acc_ref[...] = part

    def forward_block(b, carry):
        part_sum, part = weigh(b, far_ref[lineage[b], :, half:])
        l_ref[...] += part_sum
        acc_ref[...] += part
        return carry

    lax.fori_loop(0, depth, forward_block, 0)
    inverse = 1.0 / jnp.broadcast_to(jnp.sum(l_ref[...], axis=1, keepdims=True), (rows, half))
    l_ref[...] = inverse
    attended = (acc_ref[...] * inverse).astype(jnp.bfloat16)
    upstream = ups[...].astype(jnp.float32)
    corr_ref[...] = jnp.broadcast_to(
        jnp.sum(upstream * attended.astype(jnp.float32), axis=1, keepdims=True), (rows, half)
    )
    for h in range(heads):
        att_ref[:, head_columns(h)] = attended[h * NODE_LEN : (h + 1) * NODE_LEN, :]
    q_scaled = qs[...].astype(jnp.float32) * (inverse * score_scale)
    q_t[...] = q_scaled.T.astype(jnp.bfloat16)
    up_t[...] = (upstream * inverse).T.astype(jnp.bfloat16)

    @pl.when(step == 0)
    def _():
        grad_t[...] = jnp.zeros_like(grad_t)

    def backward(b, keys, values):
        corr = corr_ref[...]
        p = p_ref[b]
        d_prob = dot_nt(ups[...], values)
        centred = jnp.concatenate([d_prob[:, :half] - corr, d_prob[:, half:] - corr], axis=1)
        d_score = (p.astype(jnp.float32) * centred).astype(jnp.bfloat16)
        grad_t[b, :half, :] += dot(q_t[...], d_score)
        grad_t[b, half:, :] += dot(up_t[...], p)
        return dot(d_score, keys)

    acc_ref[...] = backward(CHAIN, own_ref[:, :half], own_ref[:, half:])

    def backward_block(b, carry):
        slot = lineage[b]
        acc_ref[...] += backward(b, far_ref[slot, :, :half], far_ref[slot, :, half:])
        return carry

    lax.fori_loop(0, depth, backward_block, 0)
    query_grad = (acc_ref[...] * (l_ref[...] * score_scale)).astype(jnp.bfloat16)
    for h in range(heads):
        dq_ref[:, head_columns(h)] = query_grad[h * NODE_LEN : (h + 1) * NODE_LEN, :]

    @pl.when(step == pl.num_programs(0) - 1)
    def _():
        far_grad[...] = jnp.zeros_like(far_grad)
        own_grad[...] = grad_t[CHAIN].T

        def emit(b, carry):
            far_grad[lineage[b]] = grad_t[b].T.astype(jnp.bfloat16)
            return carry

        lax.fori_loop(0, depth, emit, 0)


def attention(kv_head, head_group, lineage, depth, query_rows, upstream, far, own):
    group = min(GROUP, head_group)
    steps = head_group // group
    slots = far.shape[0]
    width = group * HEAD_DIM
    rows = group * NODE_LEN
    first = kv_head * steps

    def heads_in(j, *_):
        return (0, first + j)

    def heads_out(j, *_):
        return (0, j)

    def whole2(j, *_):
        return (0, 0)

    def whole3(j, *_):
        return (0, 0, 0)

    pair = 2 * HEAD_DIM
    blocks = (CHAIN + 1) * head_group
    out_rows = jax.ShapeDtypeStruct((NODE_LEN, head_group * HEAD_DIM), jnp.bfloat16)
    return pl.pallas_call(
        attend,
        grid_spec=pltpu.PrefetchScalarGridSpec(
            num_scalar_prefetch=2,
            grid=(steps,),
            in_specs=[
                pl.BlockSpec((NODE_LEN, width), heads_in),
                pl.BlockSpec((NODE_LEN, width), heads_in),
                pl.BlockSpec((slots, NODE_LEN, pair), whole3),
                pl.BlockSpec((NODE_LEN, pair), whole2),
            ],
            out_specs=[
                pl.BlockSpec((NODE_LEN, width), heads_out),
                pl.BlockSpec((NODE_LEN, width), heads_out),
                pl.BlockSpec((slots, NODE_LEN, pair), whole3),
                pl.BlockSpec((NODE_LEN, pair), whole2),
            ],
            scratch_shapes=[
                pltpu.VMEM((CHAIN + 1, rows, NODE_LEN), jnp.float32),
                pltpu.VMEM((CHAIN + 1, rows, NODE_LEN), jnp.bfloat16),
                pltpu.VMEM((rows, HEAD_DIM), jnp.bfloat16),
                pltpu.VMEM((rows, HEAD_DIM), jnp.bfloat16),
                pltpu.VMEM((HEAD_DIM, rows), jnp.bfloat16),
                pltpu.VMEM((HEAD_DIM, rows), jnp.bfloat16),
                pltpu.VMEM((rows, HEAD_DIM), jnp.float32),
                pltpu.VMEM((rows, HEAD_DIM), jnp.float32),
                pltpu.VMEM((rows, HEAD_DIM), jnp.float32),
                pltpu.VMEM((rows, HEAD_DIM), jnp.float32),
                pltpu.VMEM((CHAIN + 1, pair, NODE_LEN), jnp.float32),
            ],
        ),
        out_shape=[
            out_rows,
            out_rows,
            jax.ShapeDtypeStruct((slots, NODE_LEN, pair), jnp.bfloat16),
            jax.ShapeDtypeStruct((NODE_LEN, pair), jnp.float32),
        ],
        compiler_params=pltpu.CompilerParams(
            dimension_semantics=("arbitrary",), vmem_limit_bytes=48 * 1024 * 1024
        ),
        cost_estimate=pl.CostEstimate(
            flops=12 * blocks * NODE_LEN * NODE_LEN * HEAD_DIM,
            bytes_accessed=16 * 1024 * 1024,
            transcendentals=blocks * NODE_LEN * NODE_LEN,
        ),
    )(lineage, depth, query_rows, upstream, far, own)


def exchange_sum(part, tp):
    rows = part.shape[0] // tp
    if tp != 2:
        return lax.psum_scatter(part, "tp", scatter_dimension=0, tiled=True)
    me = lax.axis_index("tp")
    away = lax.dynamic_slice_in_dim(part, (1 - me) * rows, rows, 0)
    here = lax.dynamic_slice_in_dim(part, me * rows, rows, 0)
    came = lax.ppermute(away, "tp", [(0, 1), (1, 0)])
    return (here.astype(jnp.float32) + came.astype(jnp.float32)).astype(jnp.bfloat16)


def gather_rows(block, tp):
    if tp != 2:
        return lax.all_gather(block, "tp", axis=0, tiled=True)
    me = lax.axis_index("tp")
    came = lax.ppermute(block, "tp", [(0, 1), (1, 0)])
    return jnp.where(
        me == 0, jnp.concatenate([block, came], axis=0), jnp.concatenate([came, block], axis=0)
    )


def local(tp, query_rows, key_rows, value_rows, out_weight, out_grad, owner_slot):
    node_count = owner_slot.shape[0]
    tree_nodes = CHAIN + LEAVES
    kv_width = key_rows.shape[1]
    kv_heads = kv_width // HEAD_DIM
    head_group = query_rows.shape[1] // kv_width
    my_slot = lax.axis_index("node")
    numbers = jnp.arange(node_count, dtype=jnp.int32)
    tree_node = jnp.sum(jnp.where(owner_slot == my_slot, numbers, 0))
    depth = jnp.minimum(tree_node % tree_nodes, CHAIN).reshape(1)
    lineage = lax.dynamic_slice_in_dim(owner_slot, tree_node // tree_nodes * tree_nodes, CHAIN)

    out_grad_rows = gather_rows(out_grad, tp)
    own, far = [], []
    for k in range(kv_heads):
        columns = slice(k * HEAD_DIM, (k + 1) * HEAD_DIM)
        own.append(jnp.concatenate([key_rows[:, columns], value_rows[:, columns]], axis=1))
        far.append(lax.all_gather(own[k], "node", axis=0, tiled=False))
    upstream = dot_nt(out_grad_rows, out_weight).astype(jnp.bfloat16)

    attended, query_grad, key_grad, value_grad = [], [], [], []
    for k in range(kv_heads):
        att, dq, far_part, own_part = attention(
            k, head_group, lineage, depth, query_rows, upstream, far[k], own[k]
        )
        attended.append(att)
        query_grad.append(dq)
        came = lax.psum_scatter(far_part, "node", scatter_dimension=0, tiled=False)
        total = (own_part + came.astype(jnp.float32)).astype(jnp.bfloat16)
        key_grad.append(total[:, :HEAD_DIM])
        value_grad.append(total[:, HEAD_DIM:])

    projected = exchange_sum(
        dot(jnp.concatenate(attended, axis=1), out_weight).astype(jnp.bfloat16), tp
    )
    return (
        projected,
        jnp.concatenate(query_grad, axis=1),
        jnp.concatenate(key_grad, axis=1),
        jnp.concatenate(value_grad, axis=1),
    )


def solution(mesh):
    in_specs = (
        P("node", "tp"),
        P("node", "tp"),
        P("node", "tp"),
        P("tp", None),
        P(("node", "tp"), None),
        P(),
    )
    out_specs = (P(("node", "tp"), None), P("node", "tp"), P("node", "tp"), P("node", "tp"))
    return jax.shard_map(
        functools.partial(local, mesh.shape["tp"]),
        mesh=mesh, in_specs=in_specs, out_specs=out_specs, check_vma=False,
    )
```

time: 1030 us -> 451 us (0.44)
  waiting for transfers between devices: 576 us -> 330 us
  local copies, waits for them, and re-layouts: 176 us -> 10.2 us
  matrix products: 160 us -> 33.1 us
  other arithmetic: 72.5 us -> 12.5 us
  Pallas kernels: 0 us -> 42.7 us
  loops' own time: 24.2 us -> 0 us
    reduce_scatter x2 -> x4, waiting for transfers between devices: 497 us -> 196 us  [local(): came = lax.psum_scatter(far_part, 'node', scatter_dimension=0, tiled=False)]
    dot_general x26 -> x2, matrix products: 160 us -> 33.1 us  [the longest x1 17 us: dot(): return jnp.dot(a, b, preferred_element_type=jnp.float32)]
    dynamic_slice x29 -> x2, local copies, waits for them, and re-layouts: 78.8 us -> 2.55 us  [the longest x1 2.48 us: exchange_sum(): away = lax.dynamic_slice_in_dim(part, (1 - me) * rows, rows, 0)]
    pallas_call x0 -> x4, Pallas kernels: none -> 42.7 us  [attention(): pl.pallas_call(attend, grid_spec=pltpu.PrefetchScalarGridSpec(num_scalar_...]
    ppermute x0 -> x2, waiting for transfers between devices: none -> 40.8 us  [the longest x1 21.7 us: exchange_sum(): came = lax.ppermute(away, 'tp', [(0, 1), (1, 0)])]
    broadcast_in_dim x7 -> x0, local copies, waits for them, and re-layouts: 37.5 us -> none  [the longest x1 23.6 us: local(): jnp.zeros((CHAIN + 1, kv_heads, head_group, NODE_LEN, NODE_LEN), jnp.floa...]
    dynamic_update_slice x4 -> x0, other arithmetic: 33.8 us -> none  [scan_stats(): lax.dynamic_update_index_in_dim(score_store, scores, block_no, 0)]
    while x48 -> x0, local copies, waits for them, and re-layouts: 30.5 us -> none  [the longest x2 13.5 us: local(): lax.fori_loop(0, node_depth + 1, forward_block, zero_rows)]
  transfers between devices with their start and end apart: 4 -> 10, of which waited for: 4 -> 10; matrix products, arithmetic and copies ran while one was open for 6% -> 10% of each run, Pallas kernels for 0% -> 9%
where the time goes in v1:
time: 451 us; the launch traced here: 450 us
  waiting for transfers between devices  330 us (73%)
  Pallas kernels  42.7 us (9%)
  matrix products  33.1 us (7%)
  between operations  16.9 us (4%)
  other arithmetic  12.5 us (3%)
  local copies, waits for them, and re-layouts  10.2 us (2%)
  starting transfers between devices  4.87 us (1%)
    reduce_scatter x4, waiting for transfers between devices, local(): came = lax.psum_scatter(far_part, 'node', scatter_dimension=0, tiled=False)  196 us
    all_gather x4, waiting for transfers between devices, local(): far.append(lax.all_gather(own[k], 'node', axis=0, tiled=False))  92.8 us
    pallas_call x4, Pallas kernels, attention(): pl.pallas_call(attend, grid_spec=pltpu.PrefetchScalarGridSpec(num_scalar_...  42.7 us
    ppermute x1, waiting for transfers between devices, exchange_sum(): came = lax.ppermute(away, 'tp', [(0, 1), (1, 0)])  21.7 us
    ppermute x1, waiting for transfers between devices, gather_rows(): came = lax.ppermute(block, 'tp', [(0, 1), (1, 0)])  19.1 us
    dot_general x1, matrix products, dot(): return jnp.dot(a, b, preferred_element_type=jnp.float32)  17 us
    dot_general x1, matrix products, dot_nt(): lax.dot_general(a, b, (((1,), (1,)), ((), ())), preferred_element_type=jn...  16.1 us
  transfers between devices with their start and end apart: 10, of which 10 were waited for; matrix products, arithmetic and copies ran while one was open for 10% of the time, Pallas kernels for 9%

profile of v1, /device:TPU:0, one launch (start us, length us, event | category | flops | bytes accessed | tf_op | source)
XLA Modules:
  0.0 450.0 jit_solution(15054805726282174758)
XLA Ops:
  7.2 0.0 copy-start.15
  7.2 0.0 copy-start.16
  7.2 0.0 all-gather.9.cloned.1.call-start
  7.2 1.2 fusion.20
  8.4 0.7 pad_maximum_fusion.3.own_ref
  9.1 0.0 all-gather.9.cloned.1.call-update
  9.1 0.0 all-gather.11.cloned.1.call-start
  9.2 0.7 pad_maximum_fusion.4.own_ref
  9.8 0.0 all-gather.11.cloned.1.call-update
  9.9 0.0 all-gather.13.cloned.1.call-start
  9.9 0.7 pad_maximum_fusion.5.own_ref
  10.6 0.0 all-gather.13.cloned.1.call-update
  10.6 0.0 all-gather.15.cloned.1.call-start
  10.7 0.0 copy-done.15
  10.7 3.0 collective-permute-start
  13.7 0.7 pad_maximum_fusion.6.own_ref
  14.4 0.0 all-gather.15.cloned.1.call-update
  14.4 0.0 reduce-scatter.5.cloned.1.call-start
  14.5 0.0 copy-done.16
  14.5 0.6 fusion.17
  17.7 0.1 dynamic_slice.9.lineage
  17.8 19.1 %collective-permute-done = bf16[128,4096]{1,0:T(8,128)(2,1)S(1)} collective-permute-done((bf16[128,4096]{1,0:T(8,128)(2,1)S(1)}, bf16[128,4096]{1,0:T(8,128)(2,1)S(1)}, u32[]{:S(2)}, u32[]{:S(2)}) %collective-permute-start) | collective-permute-done | bytes 1048608 | tf_op jit(solution)/shard_map/ppermute | solution.py:227
  36.9 16.1 %convolution_convert_fusion.1.up_ref = bf16[256,4096]{1,0:T(8,128)(2,1)} fusion(bf16[4096,4096]{1,0:T(8,128)(2,1)} %param.9, bf16[128,4096]{1,0:T(8,128)(2,1)S(1)} %collective-permute-done, bf16[128,4096]{1,0:T(8,128)(2,1)S(1)} %copy-done.15, pred[]{:T(512)S(6)} %eq.13), kind=kOutput, calls=%fused_computation.1 | convolution fusion | flops 8600420352 | bytes 37748736 | tf_op jit(solution)/shard_map/dot_general | solution.py:26
  53.0 1.3 all-gather.9.cloned.1.call-done
  54.3 0.0 copy-done.3
  54.3 1.6 copy-done.4
  55.9 10.6 %shard_map.93 = (bf16[256,1024]{1,0:T(8,128)(2,1)S(1)}, bf16[256,1024]{1,0:T(8,128)(2,1)S(1)}, bf16[16,256,256]{2,1,0:T(8,128)(2,1)}, f32[256,256]{1,0:T(8,128)S(1)}) custom-call(s32[8]{0:T(128)S(1)} %dynamic_slice.9.lineage, s32[1]{0:T(128)} %bitcast.depth_ref, bf16[256,4096]{1,0:T(8,128)(2,1)S(1)} %copy-done.4, ...), custom_call_target="tpu_custom_call" | custom-call | flops 7247757312 | bytes 16777216 | tf_op jit(solution)/shard_map/pallas_call | solution.py:164
  66.6 0.0 reduce-scatter.5.cloned.1.call-update
  66.6 0.0 reduce-scatter.7.cloned.1.call-start
  66.6 30.6 %all-gather.11.cloned.1.call-done = bf16[4096,256]{1,0:T(8,128)(2,1)} async-done(((bf16[256,256]{1,0:T(8,128)(2,1)}), bf16[4096,256]{1,0:T(8,128)(2,1)}) %all-gather.11.cloned.1.call-update) | async-done | bytes 2097168 | tf_op jit(solution)/shard_map/all_gather | solution.py:250
  97.3 0.0 copy-done.8
  97.3 0.0 copy-done.2
  97.3 1.6 copy-done.5
  98.9 10.7 %shard_map.94 = (bf16[256,1024]{1,0:T(8,128)(2,1)S(1)}, bf16[256,1024]{1,0:T(8,128)(2,1)S(1)}, bf16[16,256,256]{2,1,0:T(8,128)(2,1)}, f32[256,256]{1,0:T(8,128)S(1)}) custom-call(s32[8]{0:T(128)S(1)} %dynamic_slice.9.lineage, s32[1]{0:T(128)} %bitcast.depth_ref, bf16[256,4096]{1,0:T(8,128)(2,1)S(1)} %copy-done.5, ...), custom_call_target="tpu_custom_call" | custom-call | flops 7247757312 | bytes 16777216 | tf_op jit(solution)/shard_map/pallas_call | solution.py:164
  109.5 0.0 reduce-scatter.7.cloned.1.call-update
  109.6 0.2 reduce-scatter.9.cloned.1.call-start
  109.8 30.4 %all-gather.13.cloned.1.call-done = bf16[4096,256]{1,0:T(8,128)(2,1)} async-done(((bf16[256,256]{1,0:T(8,128)(2,1)}), bf16[4096,256]{1,0:T(8,128)(2,1)}) %all-gather.13.cloned.1.call-update) | async-done | bytes 2097168 | tf_op jit(solution)/shard_map/all_gather | solution.py:250
  140.2 0.0 copy-done.10
  140.2 1.6 copy-done.6
  141.8 10.7 %shard_map.95 = (bf16[256,1024]{1,0:T(8,128)(2,1)S(1)}, bf16[256,1024]{1,0:T(8,128)(2,1)S(1)}, bf16[16,256,256]{2,1,0:T(8,128)(2,1)}, f32[256,256]{1,0:T(8,128)S(1)}) custom-call(s32[8]{0:T(128)S(1)} %dynamic_slice.9.lineage, s32[1]{0:T(128)} %bitcast.depth_ref, bf16[256,4096]{1,0:T(8,128)(2,1)S(1)} %copy-done.6, ...), custom_call_target="tpu_custom_call" | custom-call | flops 7247757312 | bytes 16777216 | tf_op jit(solution)/shard_map/pallas_call | solution.py:164
  152.5 0.0 reduce-scatter.9.cloned.1.call-update
  152.6 0.0 reduce-scatter.11.cloned.1.call-start
  152.6 30.4 %all-gather.15.cloned.1.call-done = bf16[4096,256]{1,0:T(8,128)(2,1)} async-done(((bf16[256,256]{1,0:T(8,128)(2,1)}), bf16[4096,256]{1,0:T(8,128)(2,1)}) %all-gather.15.cloned.1.call-update) | async-done | bytes 2097168 | tf_op jit(solution)/shard_map/all_gather | solution.py:250
  183.0 0.0 copy-done
  183.0 1.6 copy-done.7
  184.6 10.7 %shard_map.96 = (bf16[256,1024]{1,0:T(8,128)(2,1)S(1)}, bf16[256,1024]{1,0:T(8,128)(2,1)S(1)}, bf16[16,256,256]{2,1,0:T(8,128)(2,1)}, f32[256,256]{1,0:T(8,128)S(1)}) custom-call(s32[8]{0:T(128)S(1)} %dynamic_slice.9.lineage, s32[1]{0:T(128)} %bitcast.depth_ref, bf16[256,4096]{1,0:T(8,128)(2,1)S(1)} %copy-done.7, ...), custom_call_target="tpu_custom_call" | custom-call | flops 7247757312 | bytes 16777216 | tf_op jit(solution)/shard_map/pallas_call | solution.py:164
  195.3 0.0 copy-done.11
  195.3 17.0 %convolution_convert_fusion = bf16[256,4096]{1,0:T(8,128)(2,1)} fusion(bf16[4096,4096]{1,0:T(8,128)(2,1)} %param.9, bf16[256,1024]{1,0:T(8,128)(2,1)S(1)} %get-tuple-element.23, bf16[256,1024]{1,0:T(8,128)(2,1)S(1)} %copy-done.13, bf16[256,1024]{1,0:T(8,128)(2,1)S(1)} %copy-done.11, bf16[256,1024]{1,0:T(8,128)(2,1)S(1)} %copy-done.9), kind=kOutput, calls=%fused_computation | convolution fusion | flops 8599371776 | bytes 37748736 | tf_op jit(solution)/shard_map/dot_general | solution.py:22
  212.3 2.5 constant_dynamic-slice_fusion
  214.8 1.3 collective-permute-start.1
  216.1 0.0 reduce-scatter.11.cloned.1.call-update
  216.1 1.5 pad_maximum_fusion
  217.6 21.7 %collective-permute-done.1 = bf16[128,4096]{1,0:T(8,128)(2,1)} collective-permute-done((bf16[128,4096]{1,0:T(8,128)(2,1)}, bf16[128,4096]{1,0:T(8,128)(2,1)}, u32[]{:S(2)}, u32[]{:S(2)}) %collective-permute-start.1) | collective-permute-done | bytes 1048608 | tf_op jit(solution)/shard_map/ppermute | solution.py:219
  239.3 2.5 add_convert_fusion
  241.8 5.2 %reduce-scatter.5.cloned.1.call-done = bf16[1,256,256]{2,1,0:T(8,128)(2,1)} async-done(((bf16[16,256,256]{2,1,0:T(8,128)(2,1)}), bf16[1,256,256]{2,1,0:T(8,128)(2,1)}) %reduce-scatter.5.cloned.1.call-update) | async-done | bytes 131088 | tf_op jit(solution)/shard_map/reduce_scatter | solution.py:260
  247.0 0.9 fusion.16
  247.9 63.7 %reduce-scatter.7.cloned.1.call-done = bf16[1,256,256]{2,1,0:T(8,128)(2,1)} async-done(((bf16[16,256,256]{2,1,0:T(8,128)(2,1)}), bf16[1,256,256]{2,1,0:T(8,128)(2,1)}) %reduce-scatter.7.cloned.1.call-update) | async-done | bytes 131088 | tf_op jit(solution)/shard_map/reduce_scatter | solution.py:260
  311.6 0.9 fusion.15
  312.5 63.4 %reduce-scatter.9.cloned.1.call-done = bf16[1,256,256]{2,1,0:T(8,128)(2,1)} async-done(((bf16[16,256,256]{2,1,0:T(8,128)(2,1)}), bf16[1,256,256]{2,1,0:T(8,128)(2,1)}) %reduce-scatter.9.cloned.1.call-update) | async-done | bytes 131088 | tf_op jit(solution)/shard_map/reduce_scatter | solution.py:260
  376.0 0.9 fusion.14
  376.9 63.8 %reduce-scatter.11.cloned.1.call-done = bf16[1,256,256]{2,1,0:T(8,128)(2,1)} async-done(((bf16[16,256,256]{2,1,0:T(8,128)(2,1)}), bf16[1,256,256]{2,1,0:T(8,128)(2,1)}) %reduce-scatter.11.cloned.1.call-update) | async-done | bytes 131088 | tf_op jit(solution)/shard_map/reduce_scatter | solution.py:260
  440.7 0.9 fusion.13
  441.7 0.7 pad_maximum_fusion.2
  442.4 0.7 pad_maximum_fusion.1
  (24 shorter events, 0.1 us)
Async XLA Ops:
  7.2 3.5 copy-start.15
  7.2 7.3 %copy-start.16 = (s32[16]{0:T(128)S(1)}, s32[16]{0:T(128)}, u32[]{:S(2)}) copy-start(s32[16]{0:T(128)} %param.11) | copy-start | bytes 196
  7.2 47.1 %all-gather.9.cloned.1.call-start = ((), (), s32[]{:S(2)}) async-start(), calls=%async_computation.8 | async-start | bytes 2228224 | tf_op jit(solution)/shard_map/all_gather | solution.py:250
  9.1 88.2 %all-gather.11.cloned.1.call-start = ((), (), s32[]{:S(2)}) async-start(), calls=%async_computation.9 | async-start | bytes 2228224 | tf_op jit(solution)/shard_map/all_gather | solution.py:250
  9.9 130.4 %all-gather.13.cloned.1.call-start = ((), (), s32[]{:S(2)}) async-start(), calls=%async_computation.10 | async-start | bytes 2228224 | tf_op jit(solution)/shard_map/all_gather | solution.py:250
  10.6 172.4 %all-gather.15.cloned.1.call-start = ((), (), s32[]{:S(2)}) async-start(), calls=%async_computation.11 | async-start | bytes 2228224 | tf_op jit(solution)/shard_map/all_gather | solution.py:250
  10.7 26.2 %collective-permute-start = (bf16[128,4096]{1,0:T(8,128)(2,1)S(1)}, bf16[128,4096]{1,0:T(8,128)(2,1)S(1)}, u32[]{:S(2)}, u32[]{:S(2)}) collective-permute-start(bf16[128,4096]{1,0:T(8,128)(2,1)S(1)} %copy-done.15), channel_id=1, source_target_pairs={{0,1},{1,0},{2,3},{3,2},{4,5},{5,4},{6,7},{7,6},{8,9},{9,8},{10,11... | collective-permute-start | bytes 3145736 | tf_op jit(solution)/shard_map/ppermute | solution.py:227
  14.4 232.6 %reduce-scatter.5.cloned.1.call-start = ((), (), s32[]{:S(2)}) async-start(), calls=%async_computation.4 | async-start | bytes 2228224 | tf_op jit(solution)/shard_map/reduce_scatter | solution.py:260
  17.8 36.5 %copy-start.3 = (bf16[256,256]{1,0:T(8,128)(2,1)S(1)}, bf16[256,256]{1,0:T(8,128)(2,1)}, u32[]{:S(2)}) copy-start(bf16[256,256]{1,0:T(8,128)(2,1)} %pad_maximum_fusion.3.own_ref) | copy-start | bytes 393220
  54.3 1.6 copy-start.4
  66.6 30.7 %copy-start.8 = (bf16[256,1024]{1,0:T(8,128)(2,1)}, bf16[256,1024]{1,0:T(8,128)(2,1)S(1)}, u32[]{:S(2)}) copy-start(bf16[256,1024]{1,0:T(8,128)(2,1)S(1)} %get-tuple-element.20) | copy-start | bytes 1572868
  66.6 30.7 %copy-start.2 = (bf16[256,256]{1,0:T(8,128)(2,1)S(1)}, bf16[256,256]{1,0:T(8,128)(2,1)}, u32[]{:S(2)}) copy-start(bf16[256,256]{1,0:T(8,128)(2,1)} %pad_maximum_fusion.4.own_ref) | copy-start | bytes 393220
  66.6 245.0 %reduce-scatter.7.cloned.1.call-start = ((), (), s32[]{:S(2)}) async-start(), calls=%async_computation.5 | async-start | bytes 2228224 | tf_op jit(solution)/shard_map/reduce_scatter | solution.py:260
  97.3 1.6 copy-start.5
  109.5 30.7 %copy-start.10 = (bf16[256,1024]{1,0:T(8,128)(2,1)}, bf16[256,1024]{1,0:T(8,128)(2,1)S(1)}, u32[]{:S(2)}) copy-start(bf16[256,1024]{1,0:T(8,128)(2,1)S(1)} %get-tuple-element.21) | copy-start | bytes 1572868
  109.5 30.7 %copy-start.1 = (bf16[256,256]{1,0:T(8,128)(2,1)S(1)}, bf16[256,256]{1,0:T(8,128)(2,1)}, u32[]{:S(2)}) copy-start(bf16[256,256]{1,0:T(8,128)(2,1)} %pad_maximum_fusion.5.own_ref) | copy-start | bytes 393220
  109.6 266.4 %reduce-scatter.9.cloned.1.call-start = ((), (), s32[]{:S(2)}) async-start(), calls=%async_computation.6 | async-start | bytes 2228224 | tf_op jit(solution)/shard_map/reduce_scatter | solution.py:260
  140.2 1.6 copy-start.6
  152.5 30.4 %copy-start.12 = (bf16[256,1024]{1,0:T(8,128)(2,1)}, bf16[256,1024]{1,0:T(8,128)(2,1)S(1)}, u32[]{:S(2)}) copy-start(bf16[256,1024]{1,0:T(8,128)(2,1)S(1)} %get-tuple-element.22) | copy-start | bytes 1572868
  152.5 30.4 %copy-start = (bf16[256,256]{1,0:T(8,128)(2,1)S(1)}, bf16[256,256]{1,0:T(8,128)(2,1)}, u32[]{:S(2)}) copy-start(bf16[256,256]{1,0:T(8,128)(2,1)} %pad_maximum_fusion.6.own_ref) | copy-start | bytes 393220
  152.6 288.2 %reduce-scatter.11.cloned.1.call-start = ((), (), s32[]{:S(2)}) async-start(), calls=%async_computation.7 | async-start | bytes 2228224 | tf_op jit(solution)/shard_map/reduce_scatter | solution.py:260
  183.0 1.6 copy-start.7
  184.6 10.7 %copy-start.9 = (bf16[256,1024]{1,0:T(8,128)(2,1)S(1)}, bf16[256,1024]{1,0:T(8,128)(2,1)}, u32[]{:S(2)}) copy-start(bf16[256,1024]{1,0:T(8,128)(2,1)} %copy-done.8) | copy-start | bytes 1572868
  184.6 10.7 %copy-start.11 = (bf16[256,1024]{1,0:T(8,128)(2,1)S(1)}, bf16[256,1024]{1,0:T(8,128)(2,1)}, u32[]{:S(2)}) copy-start(bf16[256,1024]{1,0:T(8,128)(2,1)} %copy-done.10) | copy-start | bytes 1572868
  184.6 10.7 %copy-start.13 = (bf16[256,1024]{1,0:T(8,128)(2,1)S(1)}, bf16[256,1024]{1,0:T(8,128)(2,1)}, u32[]{:S(2)}) copy-start(bf16[256,1024]{1,0:T(8,128)(2,1)} %copy-done.12) | copy-start | bytes 1572868
  214.8 24.6 %collective-permute-start.1 = (bf16[128,4096]{1,0:T(8,128)(2,1)}, bf16[128,4096]{1,0:T(8,128)(2,1)}, u32[]{:S(2)}, u32[]{:S(2)}) collective-permute-start(bf16[128,4096]{1,0:T(8,128)(2,1)} %constant_dynamic-slice_fusion), channel_id=1, source_target_pairs={{0,1},{1,0},{2,3},{3,2},{4,5},{5,4},{6,7},{7,6},{8,9},{9,8},{10,11... | collective-permute-start | bytes 3145736 | tf_op jit(solution)/shard_map/ppermute | solution.py:219
  216.1 23.2 %copy-start.14 = (bf16[256,4096]{1,0:T(8,128)(2,1)S(1)}, bf16[256,4096]{1,0:T(8,128)(2,1)}, u32[]{:S(2)}) copy-start(bf16[256,4096]{1,0:T(8,128)(2,1)} %convolution_convert_fusion) | copy-start | bytes 6291460
Sparse Core Ops, SparseCore 0:
  10.2 44.0 all-gather.8
  57.1 40.1 all-gather.10
  100.0 40.1 all-gather.12
  142.8 40.0 all-gather.14
  186.5 60.3 reduce-scatter.4
  251.0 60.5 reduce-scatter.6
  315.3 60.5 reduce-scatter.8
  380.2 60.5 reduce-scatter.10

commit v2 on v1

--- a/solution.py
+++ b/solution.py
@@ -27,12 +27,15 @@
 
 
 def attend(
-    lineage, depth_ref, q_ref, up_ref, far_ref, own_ref,
-    att_ref, dq_ref, far_grad, own_grad,
-    s_ref, p_ref, qs, ups, q_t, up_t, m_ref, l_ref, acc_ref, corr_ref, grad_t,
+    lineage, place, q_ref, up_ref, own_ref, near_0, near_1, near_2, near_3, *rest,
 ):
-    step = pl.program_id(0)
-    depth = depth_ref[0]
+    (
+    att_ref, dq_ref, keep_ref, cross_ref, away_ref, own_grad, token,
+    far_ref, s_ref, p_ref, qs, ups, q_t, up_t, m_ref, l_ref, acc_ref, corr_ref, grad_t,
+    ) = rest[-19:]
+    step = pl.program_id(1)
+    depth = place[0]
+    me = place[1]
     heads = q_ref.shape[1] // HEAD_DIM
     rows = heads * NODE_LEN
     half = HEAD_DIM
@@ -47,6 +50,22 @@
     for h in range(heads):
         qs[head_rows(h), :] = q_ref[:, head_columns(h)]
         ups[head_rows(h), :] = up_ref[:, head_columns(h)]
+
+    @pl.when(step == 0)
+    def _():
+        grad_t[...] = jnp.zeros_like(grad_t)
+
+        def fetch(b, carry):
+            away = lineage[b] ^ me
+            for kind, ref in enumerate((near_0, near_1, near_2, near_3)):
+
+                @pl.when(away % 4 == kind)
+                def _():
+                    far_ref[b] = ref[away // 4]
+
+            return carry
+
+        lax.fori_loop(0, depth, fetch, 0)
 
     def fold_max(s):
         return jnp.maximum(s[:, :half], s[:, half:])
@@ -59,7 +78,7 @@
     m_ref[...] = fold_max(s)
 
     def score_block(b, carry):
-        s = dot_nt(qs[...], far_ref[lineage[b], :, :half])
+        s = dot_nt(qs[...], far_ref[b, :, :half])
         s_ref[b] = s
         m_ref[...] = jnp.maximum(m_ref[...], fold_max(s))
         return carry
@@ -81,7 +100,7 @@
     acc_ref[...] = part
 
     def forward_block(b, carry):
-        part_sum, part = weigh(b, far_ref[lineage[b], :, half:])
+        part_sum, part = weigh(b, far_ref[b, :, half:])
         l_ref[...] += part_sum
         acc_ref[...] += part
         return carry
@@ -99,10 +118,6 @@
     q_scaled = qs[...].astype(jnp.float32) * (inverse * score_scale)
     q_t[...] = q_scaled.T.astype(jnp.bfloat16)
     up_t[...] = (upstream * inverse).T.astype(jnp.bfloat16)
-
-    @pl.when(step == 0)
-    def _():
-        grad_t[...] = jnp.zeros_like(grad_t)
 
     def backward(b, keys, values):
         corr = corr_ref[...]
@@ -117,8 +132,7 @@
     acc_ref[...] = backward(CHAIN, own_ref[:, :half], own_ref[:, half:])
 
     def backward_block(b, carry):
-        slot = lineage[b]
-        acc_ref[...] += backward(b, far_ref[slot, :, :half], far_ref[slot, :, half:])
+        acc_ref[...] += backward(b, far_ref[b, :, :half], far_ref[b, :, half:])
         return carry
 
     lax.fori_loop(0, depth, backward_block, 0)
@@ -126,59 +140,94 @@
     for h in range(heads):
         dq_ref[:, head_columns(h)] = query_grad[h * NODE_LEN : (h + 1) * NODE_LEN, :]
 
-    @pl.when(step == pl.num_programs(0) - 1)
+    @pl.when(step == pl.num_programs(1) - 1)
     def _():
-        far_grad[...] = jnp.zeros_like(far_grad)
+        keep_ref[...] = jnp.zeros_like(keep_ref)
+        cross_ref[...] = jnp.zeros_like(cross_ref)
+        away_ref[...] = jnp.zeros_like(away_ref)
         own_grad[...] = grad_t[CHAIN].T
+        token[...] = jnp.zeros_like(token)
 
         def emit(b, carry):
-            far_grad[lineage[b]] = grad_t[b].T.astype(jnp.bfloat16)
+            away = lineage[b] ^ me
+            block = grad_t[b].T.astype(jnp.bfloat16)
+            kind = away % 4
+            place_z = away // 4
+
+            @pl.when(kind == 0)
+            def _():
+                keep_ref[place_z, 0] = block
+
+            @pl.when(kind == 2)
+            def _():
+                cross_ref[place_z, 0] = block
+
+            @pl.when(kind % 2 == 1)
+            def _():
+                away_ref[kind // 2, place_z, 0] = block
+
             return carry
 
         lax.fori_loop(0, depth, emit, 0)
 
 
-def attention(kv_head, head_group, lineage, depth, query_rows, upstream, far, own):
+def attention(
+    first_head, chunk_head, heads, head_group, lineage, place, query_rows, upstream, own, near, after
+):
     group = min(GROUP, head_group)
     steps = head_group // group
-    slots = far.shape[0]
+    stride = near[0].shape[0]
     width = group * HEAD_DIM
     rows = group * NODE_LEN
-    first = kv_head * steps
-
-    def heads_in(j, *_):
-        return (0, first + j)
-
-    def heads_out(j, *_):
-        return (0, j)
-
-    def whole2(j, *_):
-        return (0, 0)
-
-    def whole3(j, *_):
-        return (0, 0, 0)
-
     pair = 2 * HEAD_DIM
-    blocks = (CHAIN + 1) * head_group
-    out_rows = jax.ShapeDtypeStruct((NODE_LEN, head_group * HEAD_DIM), jnp.bfloat16)
+
+    def heads_in(i, j, *_):
+        return (0, (first_head + i) * steps + j)
+
+    def heads_out(i, j, *_):
+        return (0, i * steps + j)
+
+    def near_block(i, j, *_):
+        return (0, 0, chunk_head + i)
+
+    def own_in(i, j, *_):
+        return (0, chunk_head + i)
+
+    def own_out(i, j, *_):
+        return (0, i)
+
+    def part_block(i, j, *_):
+        return (0, i, 0, 0)
+
+    def away_block(i, j, *_):
+        return (0, 0, i, 0, 0)
+
+    blocks = (CHAIN + 1) * head_group * heads
+    out_rows = jax.ShapeDtypeStruct((NODE_LEN, heads * head_group * HEAD_DIM), jnp.bfloat16)
+    part = jax.ShapeDtypeStruct((stride, heads, NODE_LEN, pair), jnp.bfloat16)
     return pl.pallas_call(
         attend,
         grid_spec=pltpu.PrefetchScalarGridSpec(
             num_scalar_prefetch=2,
-            grid=(steps,),
+            grid=(heads, steps),
             in_specs=[
                 pl.BlockSpec((NODE_LEN, width), heads_in),
                 pl.BlockSpec((NODE_LEN, width), heads_in),
-                pl.BlockSpec((slots, NODE_LEN, pair), whole3),
-                pl.BlockSpec((NODE_LEN, pair), whole2),
-            ],
+                pl.BlockSpec((NODE_LEN, pair), own_in),
+            ]
+            + [pl.BlockSpec((stride, NODE_LEN, pair), near_block)] * 4
+            + [pl.BlockSpec(memory_space=pl.ANY)] * len(after),
             out_specs=[
                 pl.BlockSpec((NODE_LEN, width), heads_out),
                 pl.BlockSpec((NODE_LEN, width), heads_out),
-                pl.BlockSpec((slots, NODE_LEN, pair), whole3),
-                pl.BlockSpec((NODE_LEN, pair), whole2),
+                pl.BlockSpec((stride, 1, NODE_LEN, pair), part_block),
+                pl.BlockSpec((stride, 1, NODE_LEN, pair), part_block),
+                pl.BlockSpec((2, stride, 1, NODE_LEN, pair), away_block),
+                pl.BlockSpec((NODE_LEN, pair), own_out),
+                pl.BlockSpec((8, HEAD_DIM), lambda i, j, *_: (0, 0)),
             ],
             scratch_shapes=[
+                pltpu.VMEM((CHAIN, NODE_LEN, pair), jnp.bfloat16),
                 pltpu.VMEM((CHAIN + 1, rows, NODE_LEN), jnp.float32),
                 pltpu.VMEM((CHAIN + 1, rows, NODE_LEN), jnp.bfloat16),
                 pltpu.VMEM((rows, HEAD_DIM), jnp.bfloat16),
@@ -195,18 +244,51 @@
         out_shape=[
             out_rows,
             out_rows,
-            jax.ShapeDtypeStruct((slots, NODE_LEN, pair), jnp.bfloat16),
-            jax.ShapeDtypeStruct((NODE_LEN, pair), jnp.float32),
+            part,
+            part,
+            jax.ShapeDtypeStruct((2, stride, heads, NODE_LEN, pair), jnp.bfloat16),
+            jax.ShapeDtypeStruct((NODE_LEN, heads * pair), jnp.float32),
+            jax.ShapeDtypeStruct((8, HEAD_DIM), jnp.float32),
         ],
         compiler_params=pltpu.CompilerParams(
-            dimension_semantics=("arbitrary",), vmem_limit_bytes=48 * 1024 * 1024
+            dimension_semantics=("arbitrary", "arbitrary"), vmem_limit_bytes=60 * 1024 * 1024
         ),
         cost_estimate=pl.CostEstimate(
             flops=12 * blocks * NODE_LEN * NODE_LEN * HEAD_DIM,
-            bytes_accessed=16 * 1024 * 1024,
+            bytes_accessed=heads * 16 * 1024 * 1024,
             transcendentals=blocks * NODE_LEN * NODE_LEN,
         ),
-    )(lineage, depth, query_rows, upstream, far, own)
+    )(lineage, place, query_rows, upstream, own, *near, *after)
+
+
+def swap(block, mask, nodes):
+    return lax.ppermute(block, "node", [(i, i ^ mask) for i in range(nodes)])
+
+
+def gather_near(own, nodes):
+    stride = nodes // 4
+    line = jnp.stack([own] + [swap(own, 4 * d, nodes) for d in range(1, stride)])
+    cross = swap(line, 2, nodes)
+    return line, swap(line, 1, nodes), cross, swap(cross, 1, nodes)
+
+
+def scatter_sum(keep, cross, away, own_part, nodes):
+    f32 = jnp.float32
+    stride = nodes // 4
+    came = swap(away, 1, nodes)
+    zero = yield [away]
+    cross = (cross.astype(f32) + (came[1].astype(f32) + zero)).astype(jnp.bfloat16)
+    keep = keep.astype(f32) + (came[0].astype(f32) + zero)
+    came = swap(cross, 2, nodes)
+    zero = yield [cross]
+    keep = keep + (came.astype(f32) + zero)
+    sent = [keep[d].astype(jnp.bfloat16) for d in range(1, stride)]
+    came = [swap(part, 4 * (d + 1), nodes) for d, part in enumerate(sent)]
+    zero = yield sent
+    total = own_part + (keep[0] + zero)
+    for part in came:
+        total = total + part.astype(f32)
+    yield [total.astype(jnp.bfloat16)]
 
 
 def exchange_sum(part, tp):
@@ -230,41 +312,61 @@
     )
 
 
-def local(tp, query_rows, key_rows, value_rows, out_weight, out_grad, owner_slot):
+def local(tp, nodes, query_rows, key_rows, value_rows, out_weight, out_grad, owner_slot):
     node_count = owner_slot.shape[0]
     tree_nodes = CHAIN + LEAVES
     kv_width = key_rows.shape[1]
     kv_heads = kv_width // HEAD_DIM
     head_group = query_rows.shape[1] // kv_width
+    pair = 2 * HEAD_DIM
     my_slot = lax.axis_index("node")
     numbers = jnp.arange(node_count, dtype=jnp.int32)
     tree_node = jnp.sum(jnp.where(owner_slot == my_slot, numbers, 0))
-    depth = jnp.minimum(tree_node % tree_nodes, CHAIN).reshape(1)
+    depth = jnp.minimum(tree_node % tree_nodes, CHAIN)
+    place = jnp.stack([depth, my_slot]).astype(jnp.int32)
     lineage = lax.dynamic_slice_in_dim(owner_slot, tree_node // tree_nodes * tree_nodes, CHAIN)
 
     out_grad_rows = gather_rows(out_grad, tp)
-    own, far = [], []
-    for k in range(kv_heads):
-        columns = slice(k * HEAD_DIM, (k + 1) * HEAD_DIM)
-        own.append(jnp.concatenate([key_rows[:, columns], value_rows[:, columns]], axis=1))
-        far.append(lax.all_gather(own[k], "node", axis=0, tiled=False))
+    wide = min(2, kv_heads)
+    own, near = [], []
+    for c in range(kv_heads // wide):
+        parts = []
+        for k in range(c * wide, (c + 1) * wide):
+            columns = slice(k * HEAD_DIM, (k + 1) * HEAD_DIM)
+            parts += [key_rows[:, columns], value_rows[:, columns]]
+        own.append(jnp.concatenate(parts, axis=1))
+        near.append(gather_near(own[c], nodes))
     upstream = dot_nt(out_grad_rows, out_weight).astype(jnp.bfloat16)
 
-    attended, query_grad, key_grad, value_grad = [], [], [], []
-    for k in range(kv_heads):
-        att, dq, far_part, own_part = attention(
-            k, head_group, lineage, depth, query_rows, upstream, far[k], own[k]
+    calls = [(0, wide)] + [(k, 1) for k in range(wide, kv_heads)]
+    attended, query_grad, sums, sent = [], [], [], []
+    for first, heads in calls:
+        c = first // wide
+        att, dq, keep, cross, away, own_part, token = attention(
+            first, first % wide, heads, head_group, lineage, place,
+            query_rows, upstream, own[c], near[c], sent,
         )
         attended.append(att)
         query_grad.append(dq)
-        came = lax.psum_scatter(far_part, "node", scatter_dimension=0, tiled=False)
-        total = (own_part + came.astype(jnp.float32)).astype(jnp.bfloat16)
-        key_grad.append(total[:, :HEAD_DIM])
-        value_grad.append(total[:, HEAD_DIM:])
-
-    projected = exchange_sum(
-        dot(jnp.concatenate(attended, axis=1), out_weight).astype(jnp.bfloat16), tp
-    )
+        own_part = jnp.stack([own_part[:, i * pair : (i + 1) * pair] for i in range(heads)])
+        zero = token[0, 0]
+        sent = [part for chain in sums for part in chain.send(zero)]
+        sums.append(scatter_sum(keep, cross, away, own_part, nodes))
+        sent += next(sums[-1])
+
+    projected = dot(jnp.concatenate(attended, axis=1), out_weight).astype(jnp.bfloat16)
+    projected = exchange_sum(projected, tp)
+    totals = [None] * len(sums)
+    left = [max(1, 3 - (len(sums) - 1 - n)) for n in range(len(sums))]
+    for turn in range(3):
+        for n in range(len(sums)):
+            if turn < left[n]:
+                totals[n] = sums[n].send(zero)[0]
+    key_grad, value_grad = [], []
+    for (first, heads), total in zip(calls, totals):
+        for i in range(heads):
+            key_grad.append(total[i, :, :HEAD_DIM])
+            value_grad.append(total[i, :, HEAD_DIM:])
     return (
         projected,
         jnp.concatenate(query_grad, axis=1),
@@ -284,6 +386,6 @@
     )
     out_specs = (P(("node", "tp"), None), P("node", "tp"), P("node", "tp"), P("node", "tp"))
     return jax.shard_map(
-        functools.partial(local, mesh.shape["tp"]),
+        functools.partial(local, mesh.shape["tp"], mesh.shape["node"]),
         mesh=mesh, in_specs=in_specs, out_specs=out_specs, check_vma=False,
     )

time: 451 us -> 299 us (0.66)
  waiting for transfers between devices: 330 us -> 72.1 us
  starting transfers between devices: 4.87 us -> 74.2 us
  Pallas kernels: 42.7 us -> 84.1 us
  between operations: 16.9 us -> 3.64 us
  other arithmetic: 12.5 us -> 22.2 us
    reduce_scatter x4 -> x0, waiting for transfers between devices: 196 us -> none  [local(): came = lax.psum_scatter(far_part, 'node', scatter_dimension=0, tiled=False)]
    all_gather x4 -> x0, waiting for transfers between devices: 92.8 us -> none  [local(): far.append(lax.all_gather(own[k], 'node', axis=0, tiled=False))]
    ppermute x0 -> x27, starting transfers between devices: none -> 72.1 us  [swap(): return lax.ppermute(block, 'node', [(i, i ^ mask) for i in range(nodes)])]
    ppermute x0 -> x27, waiting for transfers between devices: none -> 66.2 us  [swap(): return lax.ppermute(block, 'node', [(i, i ^ mask) for i in range(nodes)])]
    pallas_call x4 -> x3, Pallas kernels: 42.7 us -> 84.1 us  [attention(): pl.pallas_call(attend, grid_spec=pltpu.PrefetchScalarGridSpec(num_scalar_...]
    ppermute x1, waiting for transfers between devices: 19.1 us -> 0.01 us  [gather_rows(): came = lax.ppermute(block, 'tp', [(0, 1), (1, 0)])]
    ppermute x1, waiting for transfers between devices: 21.7 us -> 5.89 us  [exchange_sum(): came = lax.ppermute(away, 'tp', [(0, 1), (1, 0)])]
    another operation x0 -> x8, other arithmetic: none -> 9.15 us
  transfers between devices with their start and end apart: 10 -> 29, of which waited for: 10 -> 12; matrix products, arithmetic and copies ran while one was open for 10% -> 20% of each run, Pallas kernels for 9% -> 28%
where the time goes in v2:
time: 299 us
  Pallas kernels  84.1 us (28%)
  starting transfers between devices  74.2 us (25%)
  waiting for transfers between devices  72.1 us (24%)
  matrix products  36.6 us (12%)
  other arithmetic  22.2 us (7%)
  local copies, waits for them, and re-layouts  6.24 us (2%)
  between operations  3.64 us (1%)
    pallas_call x3, Pallas kernels, attention(): pl.pallas_call(attend, grid_spec=pltpu.PrefetchScalarGridSpec(num_scalar_...  84.1 us
    ppermute x27, starting transfers between devices, swap(): return lax.ppermute(block, 'node', [(i, i ^ mask) for i in range(nodes)])  72.1 us
    ppermute x27, waiting for transfers between devices, swap(): return lax.ppermute(block, 'node', [(i, i ^ mask) for i in range(nodes)])  66.2 us
    dot_general x1, matrix products, dot_nt(): lax.dot_general(a, b, (((1,), (1,)), ((), ())), preferred_element_type=jn...  20.8 us
    dot_general x1, matrix products, dot(): return jnp.dot(a, b, preferred_element_type=jnp.float32)  15.8 us
    another operation x3, other arithmetic  7.29 us
  transfers between devices with their start and end apart: 29, of which 12 were waited for; matrix products, arithmetic and copies ran while one was open for 20% of the time, Pallas kernels for 28%

profile of v2, /device:TPU:0, one launch (start us, length us, event | category | flops | bytes accessed | tf_op | source)
XLA Modules:
  0.0 299.1 jit_solution(7858156519343626604)
XLA Ops:
  0.6 1.1 fusion.48
  1.8 3.1 %collective-permute-start.1 = (bf16[256,512]{1,0:T(8,128)(2,1)S(1)}, bf16[256,512]{1,0:T(8,128)(2,1)S(1)}, u32[]{:S(2)}, u32[]{:S(2)}) collective-permute-start(bf16[256,512]{1,0:T(8,128)(2,1)S(1)} %get-tuple-element.66.own_ref), channel_id=1, source_target_pairs={{0,8},{2,10},{4,12},{6,14},{8,0},{10,2},{12,4},{14,6},{16,24},{18,... | collective-permute-start | bytes 786440 | tf_op jit(solution)/shard_map/ppermute | solution.py:265
  4.9 2.6 collective-permute-start.2
  7.5 8.6 %collective-permute-done.1 = bf16[256,512]{1,0:T(8,128)(2,1)S(1)} collective-permute-done((bf16[256,512]{1,0:T(8,128)(2,1)S(1)}, bf16[256,512]{1,0:T(8,128)(2,1)S(1)}, u32[]{:S(2)}, u32[]{:S(2)}) %collective-permute-start.1) | collective-permute-done | bytes 262176 | tf_op jit(solution)/shard_map/ppermute | solution.py:265
  16.1 10.2 %collective-permute-done.2 = bf16[256,512]{1,0:T(8,128)(2,1)S(1)} collective-permute-done((bf16[256,512]{1,0:T(8,128)(2,1)S(1)}, bf16[256,512]{1,0:T(8,128)(2,1)S(1)}, u32[]{:S(2)}, u32[]{:S(2)}) %collective-permute-start.2) | collective-permute-done | bytes 262176 | tf_op jit(solution)/shard_map/ppermute | solution.py:265
  26.3 0.1 pad_maximum_fusion.1.near_0
  26.4 1.6 collective-permute-start.5
  28.0 1.5 collective-permute-start
  29.6 4.8 %collective-permute-start.7 = (bf16[256,512]{1,0:T(8,128)(2,1)S(1)}, bf16[256,512]{1,0:T(8,128)(2,1)S(1)}, u32[]{:S(2)}, u32[]{:S(2)}) collective-permute-start(bf16[256,512]{1,0:T(8,128)(2,1)S(1)} %get-tuple-element.76.own_ref), channel_id=1, source_target_pairs={{0,8},{2,10},{4,12},{6,14},{8,0},{10,2},{12,4},{14,6},{16,24},{18,... | collective-permute-start | bytes 786440 | tf_op jit(solution)/shard_map/ppermute | solution.py:265
  34.4 1.1 collective-permute-start.8
  35.5 1.4 collective-permute-start.9
  36.9 0.6 fusion.37
  40.1 0.6 dynamic_slice.9.lineage
  40.7 0.6 pad_add_fusion.place
  41.3 1.4 collective-permute-done.7
  42.7 12.7 %collective-permute-done.8 = bf16[256,512]{1,0:T(8,128)(2,1)S(1)} collective-permute-done((bf16[256,512]{1,0:T(8,128)(2,1)S(1)}, bf16[256,512]{1,0:T(8,128)(2,1)S(1)}, u32[]{:S(2)}, u32[]{:S(2)}) %collective-permute-start.8) | collective-permute-done | bytes 262176 | tf_op jit(solution)/shard_map/ppermute | solution.py:265
  55.4 1.1 pad_maximum_fusion.2.near_0
  56.5 0.6 collective-permute-start.11
  57.2 20.8 %convolution_convert_fusion.1.up_ref = bf16[256,4096]{1,0:T(8,128)(2,1)} fusion(bf16[4096,4096]{1,0:T(8,128)(2,1)} %param.9, bf16[128,4096]{1,0:T(8,128)(2,1)} %collective-permute-done, bf16[128,4096]{1,0:T(8,128)(2,1)} %param.10, pred[]{:T(512)S(6)} %eq.13), kind=kOutput, calls=%fused_computation.1 | convolution fusion | flops 8600420352 | bytes 37748736 | tf_op jit(solution)/shard_map/dot_general | solution.py:26
  78.0 1.0 copy-done.17
  79.0 40.0 %shard_map.93 = (bf16[256,2048]{1,0:T(8,128)(2,1)}, bf16[256,2048]{1,0:T(8,128)(2,1)}, bf16[4,2,256,256]{3,2,1,0:T(8,128)(2,1)}, bf16[4,2,256,256]{3,2,1,0:T(8,1...) custom-call(s32[8]{0:T(128)} %dynamic_slice.9.lineage, s32[2]{0:T(128)} %pad_add_fusion.place, ...), custom_call_target="tpu_custom_call" | custom-call | flops 14495514624 | bytes 33554432 | tf_op jit(solution)/shard_map/pallas_call | solution.py:208
  119.1 0.5 collective-permute-start.10
  119.6 0.1 collective-permute-start.12
  119.6 6.3 %collective-permute-done.10.near_1 = bf16[4,256,512]{2,1,0:T(8,128)(2,1)} collective-permute-done((bf16[4,256,512]{2,1,0:T(8,128)(2,1)S(1)}, bf16[4,256,512]{2,1,0:T(8,128)(2,1)}, u32[]{:S(2)}, u32[]{:S(2)}) %collective-permute-start.10) | collective-permute-done | bytes 1048608 | tf_op jit(solution)/shard_map/ppermute | solution.py:265
  126.0 0.6 collective-permute-done.12.near_3
  126.5 22.0 %shard_map.94 = (bf16[256,1024]{1,0:T(8,128)(2,1)}, bf16[256,1024]{1,0:T(8,128)(2,1)}, bf16[4,1,256,256]{3,2,1,0:T(8,128)(2,1)}, bf16[4,1,256,256]{3,2,1,0:T(8,1...) custom-call(s32[8]{0:T(128)} %dynamic_slice.9.lineage, s32[2]{0:T(128)} %pad_add_fusion.place, ...), custom_call_target="tpu_custom_call" | custom-call | flops 7247757312 | bytes 16777216 | tf_op jit(solution)/shard_map/pallas_call | solution.py:208
  148.6 0.7 slice_bitcast_fusion.4
  149.4 1.3 slice.132
  150.6 2.2 fusion.11.rest_0_
  152.9 26.6 %collective-permute-start.15 = (bf16[4,2,256,256]{3,2,1,0:T(8,128)(2,1)S(1)}, bf16[4,2,256,256]{3,2,1,0:T(8,128)(2,1)}, u32[]{:S(2)}, u32[]{:S(2)}) collective-permute-start(bf16[4,2,256,256]{3,2,1,0:T(8,128)(2,1)S(1)} %fusion.11.rest_0_), channel_id=1, source_target_pairs={{0,4},{2,6},{4,0},{6,2},{8,12},{10,14},{12,8},{14,10},{16,20},{18,... | collective-permute-start | bytes 3145736 | tf_op jit(solution)/shard_map/ppermute | solution.py:265
  179.5 22.1 %shard_map.95 = (bf16[256,1024]{1,0:T(8,128)(2,1)}, bf16[256,1024]{1,0:T(8,128)(2,1)}, bf16[4,1,256,256]{3,2,1,0:T(8,128)(2,1)}, bf16[4,1,256,256]{3,2,1,0:T(8,1...) custom-call(s32[8]{0:T(128)} %dynamic_slice.9.lineage, s32[2]{0:T(128)} %pad_add_fusion.place, ...), custom_call_target="tpu_custom_call" | custom-call | flops 7247757312 | bytes 16777216 | tf_op jit(solution)/shard_map/pallas_call | solution.py:208
  201.6 1.2 slice.136
  202.8 1.8 fusion.16
  204.6 9.3 %collective-permute-start.20 = (bf16[4,1,256,256]{3,2,0,1:T(8,128)(2,1)S(1)}, bf16[4,1,256,256]{3,2,0,1:T(8,128)(2,1)}, u32[]{:S(2)}, u32[]{:S(2)}) collective-permute-start(bf16[4,1,256,256]{3,2,0,1:T(8,128)(2,1)S(1)} %fusion.16), channel_id=1, source_target_pairs={{0,4},{2,6},{4,0},{6,2},{8,12},{10,14},{12,8},{14,10},{16,20},{18,... | collective-permute-start | bytes 1572872 | tf_op jit(solution)/shard_map/ppermute | solution.py:265
  213.9 15.8 %convolution_convert_fusion = bf16[256,4096]{1,0:T(8,128)(2,1)S(1)} fusion(bf16[4096,4096]{1,0:T(8,128)(2,1)} %param.9, bf16[256,1024]{1,0:T(8,128)(2,1)} %get-tuple-element.30, bf16[256,1024]{1,0:T(8,128)(2,1)} %get-tuple-element.26, bf16[256,2048]{1,0:T(8,128)(2,1)} %get-tuple-element.24), kind=kOutput, calls=%fused_computation | convolution fusion | flops 8597274624 | bytes 37748736 | tf_op jit(solution)/shard_map/dot_general | solution.py:22
  229.8 1.5 pad_maximum_fusion
  231.3 2.1 fusion.44
  233.4 3.5 %collective-permute-start.21 = (bf16[1,256,256]{2,1,0:T(8,128)(2,1)S(1)}, bf16[1,256,256]{2,1,0:T(8,128)(2,1)S(1)}, u32[]{:S(2)}, u32[]{:S(2)}) collective-permute-start(bf16[1,256,256]{2,1,0:T(8,128)(2,1)S(1)} %get-tuple-element.55), channel_id=1, source_target_pairs={{0,8},{2,10},{4,12},{6,14},{8,0},{10,2},{12,4},{14,6},{16,24},{18,... | collective-permute-start | bytes 393224 | tf_op jit(solution)/shard_map/ppermute | solution.py:265
  237.0 1.5 collective-permute-start.22
  238.5 1.4 collective-permute-start.23
  239.9 0.1 constant_dynamic-slice_fusion
  240.0 3.6 %collective-permute-done.21 = bf16[1,256,256]{2,1,0:T(8,128)(2,1)S(1)} collective-permute-done((bf16[1,256,256]{2,1,0:T(8,128)(2,1)S(1)}, bf16[1,256,256]{2,1,0:T(8,128)(2,1)S(1)}, u32[]{:S(2)}, u32[]{:S(2)}) %collective-permute-start.21) | collective-permute-done | bytes 131104 | tf_op jit(solution)/shard_map/ppermute | solution.py:265
  243.5 0.5 collective-permute-start.14
  244.1 5.8 %collective-permute-done.22 = bf16[1,256,256]{2,1,0:T(8,128)(2,1)S(1)} collective-permute-done((bf16[1,256,256]{2,1,0:T(8,128)(2,1)S(1)}, bf16[1,256,256]{2,1,0:T(8,128)(2,1)S(1)}, u32[]{:S(2)}, u32[]{:S(2)}) %collective-permute-start.22) | collective-permute-done | bytes 131104 | tf_op jit(solution)/shard_map/ppermute | solution.py:265
  249.9 0.7 fusion.36
  250.7 3.2 %fusion.42 = (bf16[4,2,256,256]{3,2,1,0:T(8,128)(2,1)S(1)}, f32[4,2,256,256]{3,2,1,0:T(8,128)S(1)}) fusion(f32[]{:T(128)} %bitcast.15, bf16[4,2,256,256]{3,2,1,0:T(8,128)(2,1)} %collective-permute-done.15, f32[]{:T(128)} %bitcast.10, bf16[2,4,2,256,256]{4,3,2,1,0:T(8,128)(2,1)S(1)} %collective-permute-done.13, bf16[4,2,256,256]{3,2,1,0:T(8,128)(2,1)S(1)} %copy-done.4), kind=kLoop, calls=%fused_computation.86 | loop fusion | flops 4194304 | bytes 6291464 | tf_op jit(solution)/shard_map/convert.8
  253.9 2.7 collective-permute-start.16
  256.6 1.5 collective-permute-start.17
  258.1 1.4 collective-permute-start.18
  259.5 1.9 fusion.15
  261.4 1.1 collective-permute-start.25
  262.6 5.9 %collective-permute-done.14 = bf16[128,4096]{1,0:T(8,128)(2,1)S(1)} collective-permute-done((bf16[128,4096]{1,0:T(8,128)(2,1)S(1)}, bf16[128,4096]{1,0:T(8,128)(2,1)S(1)}, u32[]{:S(2)}, u32[]{:S(2)}) %collective-permute-start.14) | collective-permute-done | bytes 1048608 | tf_op jit(solution)/shard_map/ppermute | solution.py:301
  268.4 1.2 add_convert_fusion
  269.7 8.4 %collective-permute-done.17 = bf16[2,256,256]{2,1,0:T(8,128)(2,1)S(1)} collective-permute-done((bf16[2,256,256]{2,1,0:T(8,128)(2,1)S(1)}, bf16[2,256,256]{2,1,0:T(8,128)(2,1)S(1)}, u32[]{:S(2)}, u32[]{:S(2)}) %collective-permute-start.17) | collective-permute-done | bytes 262176 | tf_op jit(solution)/shard_map/ppermute | solution.py:265
  278.0 0.8 fusion.22
  278.9 2.0 fusion.46
  280.9 4.4 %collective-permute-start.26 = (bf16[1,256,256]{2,1,0:T(8,128)(2,1)S(1)}, bf16[1,256,256]{2,1,0:T(8,128)(2,1)S(1)}, u32[]{:S(2)}, u32[]{:S(2)}) collective-permute-start(bf16[1,256,256]{2,1,0:T(8,128)(2,1)S(1)} %get-tuple-element.58), channel_id=1, source_target_pairs={{0,8},{2,10},{4,12},{6,14},{8,0},{10,2},{12,4},{14,6},{16,24},{18,... | collective-permute-start | bytes 393224 | tf_op jit(solution)/shard_map/ppermute | solution.py:265
  285.3 1.5 collective-permute-start.27
  286.8 1.4 collective-permute-start.28
  288.2 1.4 collective-permute-done.26
  289.6 7.3 %collective-permute-done.27 = bf16[1,256,256]{2,1,0:T(8,128)(2,1)S(1)} collective-permute-done((bf16[1,256,256]{2,1,0:T(8,128)(2,1)S(1)}, bf16[1,256,256]{2,1,0:T(8,128)(2,1)S(1)}, u32[]{:S(2)}, u32[]{:S(2)}) %collective-permute-start.27) | collective-permute-done | bytes 131104 | tf_op jit(solution)/shard_map/ppermute | solution.py:265
  296.8 0.7 fusion.29
  297.6 0.7 pad_maximum_fusion.6
  298.3 0.7 pad_maximum_fusion.5
  (68 shorter events, 0.5 us)
Async XLA Ops:
  1.8 35.1 %copy-start.18 = (s32[16]{0:T(128)S(1)}, s32[16]{0:T(128)}, u32[]{:S(2)}) copy-start(s32[16]{0:T(128)} %param.11) | copy-start | bytes 196
  1.8 54.7 %copy-start.14 = (bf16[256,512]{1,0:T(8,128)(2,1)}, bf16[256,512]{1,0:T(8,128)(2,1)S(1)}, u32[]{:S(2)}) copy-start(bf16[256,512]{1,0:T(8,128)(2,1)S(1)} %get-tuple-element.66.own_ref) | copy-start | bytes 786436
  1.8 14.2 %collective-permute-start.1 = (bf16[256,512]{1,0:T(8,128)(2,1)S(1)}, bf16[256,512]{1,0:T(8,128)(2,1)S(1)}, u32[]{:S(2)}, u32[]{:S(2)}) collective-permute-start(bf16[256,512]{1,0:T(8,128)(2,1)S(1)} %get-tuple-element.66.own_ref), channel_id=1, source_target_pairs={{0,8},{2,10},{4,12},{6,14},{8,0},{10,2},{12,4},{14,6},{16,24},{18,... | collective-permute-start | bytes 786440 | tf_op jit(solution)/shard_map/ppermute | solution.py:265
  4.9 21.4 %collective-permute-start.2 = (bf16[256,512]{1,0:T(8,128)(2,1)S(1)}, bf16[256,512]{1,0:T(8,128)(2,1)S(1)}, u32[]{:S(2)}, u32[]{:S(2)}) collective-permute-start(bf16[256,512]{1,0:T(8,128)(2,1)S(1)} %get-tuple-element.66.own_ref), channel_id=1, source_target_pairs={{0,16},{2,18},{4,20},{6,22},{8,24},{10,26},{12,28},{14,30},{16,0},... | collective-permute-start | bytes 786440 | tf_op jit(solution)/shard_map/ppermute | solution.py:265
  7.5 18.8 %collective-permute-start.3 = (bf16[256,512]{1,0:T(8,128)(2,1)S(1)}, bf16[256,512]{1,0:T(8,128)(2,1)S(1)}, u32[]{:S(2)}, u32[]{:S(2)}) collective-permute-start(bf16[256,512]{1,0:T(8,128)(2,1)S(1)} %get-tuple-element.66.own_ref), channel_id=1, source_target_pairs={{0,24},{2,26},{4,28},{6,30},{8,16},{10,18},{12,20},{14,22},{16,8},... | collective-permute-start | bytes 786440 | tf_op jit(solution)/shard_map/ppermute | solution.py:265
  26.4 51.5 %copy-start = (bf16[4,256,512]{2,1,0:T(8,128)(2,1)}, bf16[4,256,512]{2,1,0:T(8,128)(2,1)S(1)}, u32[]{:S(2)}) copy-start(bf16[4,256,512]{2,1,0:T(8,128)(2,1)S(1)} %pad_maximum_fusion.1.near_0) | copy-start | bytes 3145732
  26.4 30.7 %collective-permute-start.5 = (bf16[4,256,512]{2,1,0:T(8,128)(2,1)S(1)}, bf16[4,256,512]{2,1,0:T(8,128)(2,1)}, u32[]{:S(2)}, u32[]{:S(2)}) collective-permute-start(bf16[4,256,512]{2,1,0:T(8,128)(2,1)S(1)} %pad_maximum_fusion.1.near_0), channel_id=1, source_target_pairs={{0,4},{2,6},{4,0},{6,2},{8,12},{10,14},{12,8},{14,10},{16,20},{18,... | collective-permute-start | bytes 3145736 | tf_op jit(solution)/shard_map/ppermute | solution.py:265
  28.0 29.2 %collective-permute-start = (bf16[128,4096]{1,0:T(8,128)(2,1)}, bf16[128,4096]{1,0:T(8,128)(2,1)}, u32[]{:S(2)}, u32[]{:S(2)}) collective-permute-start(bf16[128,4096]{1,0:T(8,128)(2,1)} %param.10), channel_id=1, source_target_pairs={{0,1},{1,0},{2,3},{3,2},{4,5},{5,4},{6,7},{7,6},{8,9},{9,8},{10,11... | collective-permute-start | bytes 3145736 | tf_op jit(solution)/shard_map/ppermute | solution.py:309
  29.5 48.4 %copy-start.13 = (bf16[256,512]{1,0:T(8,128)(2,1)}, bf16[256,512]{1,0:T(8,128)(2,1)S(1)}, u32[]{:S(2)}) copy-start(bf16[256,512]{1,0:T(8,128)(2,1)S(1)} %get-tuple-element.76.own_ref) | copy-start | bytes 786436
  29.6 13.2 %collective-permute-start.7 = (bf16[256,512]{1,0:T(8,128)(2,1)S(1)}, bf16[256,512]{1,0:T(8,128)(2,1)S(1)}, u32[]{:S(2)}, u32[]{:S(2)}) collective-permute-start(bf16[256,512]{1,0:T(8,128)(2,1)S(1)} %get-tuple-element.76.own_ref), channel_id=1, source_target_pairs={{0,8},{2,10},{4,12},{6,14},{8,0},{10,2},{12,4},{14,6},{16,24},{18,... | collective-permute-start | bytes 786440 | tf_op jit(solution)/shard_map/ppermute | solution.py:265
  34.4 21.1 %collective-permute-start.8 = (bf16[256,512]{1,0:T(8,128)(2,1)S(1)}, bf16[256,512]{1,0:T(8,128)(2,1)S(1)}, u32[]{:S(2)}, u32[]{:S(2)}) collective-permute-start(bf16[256,512]{1,0:T(8,128)(2,1)S(1)} %get-tuple-element.76.own_ref), channel_id=1, source_target_pairs={{0,16},{2,18},{4,20},{6,22},{8,24},{10,26},{12,28},{14,30},{16,0},... | collective-permute-start | bytes 786440 | tf_op jit(solution)/shard_map/ppermute | solution.py:265
  35.5 20.0 %collective-permute-start.9 = (bf16[256,512]{1,0:T(8,128)(2,1)S(1)}, bf16[256,512]{1,0:T(8,128)(2,1)}, u32[]{:S(2)}, u32[]{:S(2)}) collective-permute-start(bf16[256,512]{1,0:T(8,128)(2,1)S(1)} %get-tuple-element.76.own_ref), channel_id=1, source_target_pairs={{0,24},{2,26},{4,28},{6,30},{8,16},{10,18},{12,20},{14,22},{16,8},... | collective-permute-start | bytes 786440 | tf_op jit(solution)/shard_map/ppermute | solution.py:265
  42.7 35.2 %collective-permute-start.4 = (bf16[4,256,512]{2,1,0:T(8,128)(2,1)S(1)}, bf16[4,256,512]{2,1,0:T(8,128)(2,1)}, u32[]{:S(2)}, u32[]{:S(2)}) collective-permute-start(bf16[4,256,512]{2,1,0:T(8,128)(2,1)S(1)} %pad_maximum_fusion.1.near_0), channel_id=1, source_target_pairs={{0,2},{2,0},{4,6},{6,4},{8,10},{10,8},{12,14},{14,12},{16,18},{18,... | collective-permute-start | bytes 3145736 | tf_op jit(solution)/shard_map/ppermute | solution.py:265
  56.5 62.5 %copy-start.1 = (bf16[4,256,512]{2,1,0:T(8,128)(2,1)}, bf16[4,256,512]{2,1,0:T(8,128)(2,1)S(1)}, u32[]{:S(2)}) copy-start(bf16[4,256,512]{2,1,0:T(8,128)(2,1)S(1)} %pad_maximum_fusion.2.near_0) | copy-start | bytes 3145732
  56.5 63.0 %collective-permute-start.11 = (bf16[4,256,512]{2,1,0:T(8,128)(2,1)S(1)}, bf16[4,256,512]{2,1,0:T(8,128)(2,1)}, u32[]{:S(2)}, u32[]{:S(2)}) collective-permute-start(bf16[4,256,512]{2,1,0:T(8,128)(2,1)S(1)} %pad_maximum_fusion.2.near_0), channel_id=1, source_target_pairs={{0,4},{2,6},{4,0},{6,2},{8,12},{10,14},{12,8},{14,10},{16,20},{18,... | collective-permute-start | bytes 3145736 | tf_op jit(solution)/shard_map/ppermute | solution.py:265
  57.1 20.8 %collective-permute-start.6 = (bf16[4,256,512]{2,1,0:T(8,128)(2,1)}, bf16[4,256,512]{2,1,0:T(8,128)(2,1)S(1)}, u32[]{:S(2)}, u32[]{:S(2)}) collective-permute-start(bf16[4,256,512]{2,1,0:T(8,128)(2,1)} %collective-permute-done.5.near_2), channel_id=1, source_target_pairs={{0,2},{2,0},{4,6},{6,4},{8,10},{10,8},{12,14},{14,12},{16,18},{18,... | collective-permute-start | bytes 3145736 | tf_op jit(solution)/shard_map/ppermute | solution.py:265
  78.0 1.0 copy-start.17
  119.0 31.7 %collective-permute-start.13 = (bf16[2,4,2,256,256]{4,3,2,1,0:T(8,128)(2,1)}, bf16[2,4,2,256,256]{4,3,2,1,0:T(8,128)(2,1)S(1)}, u32[]{:S(2)}, u32[]{:S(2)}) collective-permute-start(bf16[2,4,2,256,256]{4,3,2,1,0:T(8,128)(2,1)} %get-tuple-element.25.rest_0_), channel_id=1, source_target_pairs={{0,2},{2,0},{4,6},{6,4},{8,10},{10,8},{12,14},{14,12},{16,18},{18,... | collective-permute-start | bytes 6291464 | tf_op jit(solution)/shard_map/ppermute | solution.py:265
  119.1 6.9 %collective-permute-start.10 = (bf16[4,256,512]{2,1,0:T(8,128)(2,1)S(1)}, bf16[4,256,512]{2,1,0:T(8,128)(2,1)}, u32[]{:S(2)}, u32[]{:S(2)}) collective-permute-start(bf16[4,256,512]{2,1,0:T(8,128)(2,1)S(1)} %pad_maximum_fusion.2.near_0), channel_id=1, source_target_pairs={{0,2},{2,0},{4,6},{6,4},{8,10},{10,8},{12,14},{14,12},{16,18},{18,... | collective-permute-start | bytes 3145736 | tf_op jit(solution)/shard_map/ppermute | solution.py:265
  119.6 7.0 %collective-permute-start.12 = (bf16[4,256,512]{2,1,0:T(8,128)(2,1)}, bf16[4,256,512]{2,1,0:T(8,128)(2,1)}, u32[]{:S(2)}, u32[]{:S(2)}) collective-permute-start(bf16[4,256,512]{2,1,0:T(8,128)(2,1)} %collective-permute-done.11.near_2), channel_id=1, source_target_pairs={{0,2},{2,0},{4,6},{6,4},{8,10},{10,8},{12,14},{14,12},{16,18},{18,... | collective-permute-start | bytes 3145736 | tf_op jit(solution)/shard_map/ppermute | solution.py:265
  119.6 29.0 %copy-start.7 = (f32[256,512]{1,0:T(8,128)S(1)}, f32[256,512]{1,0:T(8,128)}, u32[]{:S(2)}) copy-start(f32[256,512]{1,0:T(8,128)} %get-tuple-element.34) | copy-start | bytes 1572868
  148.5 54.2 %collective-permute-start.19 = (bf16[2,4,1,256,256]{4,3,1,2,0:T(8,128)(2,1)}, bf16[2,4,1,256,256]{4,3,1,2,0:T(8,128)(2,1)}, u32[]{:S(2)}, u32[]{:S(2)}) collective-permute-start(bf16[2,4,1,256,256]{4,3,1,2,0:T(8,128)(2,1)} %bitcast.167), channel_id=1, source_target_pairs={{0,2},{2,0},{4,6},{6,4},{8,10},{10,8},{12,14},{14,12},{16,18},{18,... | collective-permute-start | bytes 3145736 | tf_op jit(solution)/shard_map/ppermute | solution.py:265
  152.9 26.6 %copy-start.2 = (bf16[4,2,256,256]{3,2,1,0:T(8,128)(2,1)}, bf16[4,2,256,256]{3,2,1,0:T(8,128)(2,1)S(1)}, u32[]{:S(2)}) copy-start(bf16[4,2,256,256]{3,2,1,0:T(8,128)(2,1)S(1)} %fusion.11.rest_0_) | copy-start | bytes 3145732
  152.9 49.9 %copy-start.8 = (bf16[4,1,256,256]{3,2,1,0:T(8,128)(2,1)S(1)}, bf16[4,1,256,256]{3,2,1,0:T(8,128)(2,1)}, u32[]{:S(2)}) copy-start(bf16[4,1,256,256]{3,2,1,0:T(8,128)(2,1)} %get-tuple-element.39) | copy-start | bytes 1572868
  152.9 97.8 %collective-permute-start.15 = (bf16[4,2,256,256]{3,2,1,0:T(8,128)(2,1)S(1)}, bf16[4,2,256,256]{3,2,1,0:T(8,128)(2,1)}, u32[]{:S(2)}, u32[]{:S(2)}) collective-permute-start(bf16[4,2,256,256]{3,2,1,0:T(8,128)(2,1)S(1)} %fusion.11.rest_0_), channel_id=1, source_target_pairs={{0,4},{2,6},{4,0},{6,2},{8,12},{10,14},{12,8},{14,10},{16,20},{18,... | collective-permute-start | bytes 3145736 | tf_op jit(solution)/shard_map/ppermute | solution.py:265
  204.6 26.6 %collective-permute-start.20 = (bf16[4,1,256,256]{3,2,0,1:T(8,128)(2,1)S(1)}, bf16[4,1,256,256]{3,2,0,1:T(8,128)(2,1)}, u32[]{:S(2)}, u32[]{:S(2)}) collective-permute-start(bf16[4,1,256,256]{3,2,0,1:T(8,128)(2,1)S(1)} %fusion.16), channel_id=1, source_target_pairs={{0,4},{2,6},{4,0},{6,2},{8,12},{10,14},{12,8},{14,10},{16,20},{18,... | collective-permute-start | bytes 1572872 | tf_op jit(solution)/shard_map/ppermute | solution.py:265
  213.9 45.6 %collective-permute-start.24 = (bf16[2,4,1,256,256]{4,3,1,2,0:T(8,128)(2,1)}, bf16[2,4,1,256,256]{4,3,1,2,0:T(8,128)(2,1)}, u32[]{:S(2)}, u32[]{:S(2)}) collective-permute-start(bf16[2,4,1,256,256]{4,3,1,2,0:T(8,128)(2,1)} %bitcast.166), channel_id=1, source_target_pairs={{0,2},{2,0},{4,6},{6,4},{8,10},{10,8},{12,14},{14,12},{16,18},{18,... | collective-permute-start | bytes 3145736 | tf_op jit(solution)/shard_map/ppermute | solution.py:265
  213.9 15.8 %copy-start.5 = (bf16[256,2048]{1,0:T(8,128)(2,1)S(1)}, bf16[256,2048]{1,0:T(8,128)(2,1)}, u32[]{:S(2)}) copy-start(bf16[256,2048]{1,0:T(8,128)(2,1)} %get-tuple-element.31) | copy-start | bytes 3145732
  213.9 15.8 %copy-start.11 = (bf16[256,1024]{1,0:T(8,128)(2,1)S(1)}, bf16[256,1024]{1,0:T(8,128)(2,1)}, u32[]{:S(2)}) copy-start(bf16[256,1024]{1,0:T(8,128)(2,1)} %get-tuple-element.32) | copy-start | bytes 1572868
  213.9 15.8 %copy-start.12 = (bf16[256,1024]{1,0:T(8,128)(2,1)S(1)}, bf16[256,1024]{1,0:T(8,128)(2,1)}, u32[]{:S(2)}) copy-start(bf16[256,1024]{1,0:T(8,128)(2,1)} %get-tuple-element.33) | copy-start | bytes 1572868
  229.8 1.5 copy-start.10
  233.4 16.5 %copy-start.16 = (f32[256,256]{1,0:T(8,128)S(1)}, f32[256,256]{1,0:T(8,128)}, u32[]{:S(2)}) copy-start(f32[256,256]{1,0:T(8,128)} %get-tuple-element.37) | copy-start | bytes 786436
  233.4 17.3 %copy-start.4 = (bf16[4,2,256,256]{3,2,1,0:T(8,128)(2,1)S(1)}, bf16[4,2,256,256]{3,2,1,0:T(8,128)(2,1)}, u32[]{:S(2)}) copy-start(bf16[4,2,256,256]{3,2,1,0:T(8,128)(2,1)} %get-tuple-element.35) | copy-start | bytes 3145732
  233.4 10.1 %collective-permute-start.21 = (bf16[1,256,256]{2,1,0:T(8,128)(2,1)S(1)}, bf16[1,256,256]{2,1,0:T(8,128)(2,1)S(1)}, u32[]{:S(2)}, u32[]{:S(2)}) collective-permute-start(bf16[1,256,256]{2,1,0:T(8,128)(2,1)S(1)} %get-tuple-element.55), channel_id=1, source_target_pairs={{0,8},{2,10},{4,12},{6,14},{8,0},{10,2},{12,4},{14,6},{16,24},{18,... | collective-permute-start | bytes 393224 | tf_op jit(solution)/shard_map/ppermute | solution.py:265
  237.0 12.9 %collective-permute-start.22 = (bf16[1,256,256]{2,1,0:T(8,128)(2,1)S(1)}, bf16[1,256,256]{2,1,0:T(8,128)(2,1)S(1)}, u32[]{:S(2)}, u32[]{:S(2)}) collective-permute-start(bf16[1,256,256]{2,1,0:T(8,128)(2,1)S(1)} %get-tuple-element.57), channel_id=1, source_target_pairs={{0,16},{2,18},{4,20},{6,22},{8,24},{10,26},{12,28},{14,30},{16,0},... | collective-permute-start | bytes 393224 | tf_op jit(solution)/shard_map/ppermute | solution.py:265
  238.5 11.4 %collective-permute-start.23 = (bf16[1,256,256]{2,1,0:T(8,128)(2,1)S(1)}, bf16[1,256,256]{2,1,0:T(8,128)(2,1)S(1)}, u32[]{:S(2)}, u32[]{:S(2)}) collective-permute-start(bf16[1,256,256]{2,1,0:T(8,128)(2,1)S(1)} %get-tuple-element.56), channel_id=1, source_target_pairs={{0,24},{2,26},{4,28},{6,30},{8,16},{10,18},{12,20},{14,22},{16,8},... | collective-permute-start | bytes 393224 | tf_op jit(solution)/shard_map/ppermute | solution.py:265
  243.5 24.9 %collective-permute-start.14 = (bf16[128,4096]{1,0:T(8,128)(2,1)S(1)}, bf16[128,4096]{1,0:T(8,128)(2,1)S(1)}, u32[]{:S(2)}, u32[]{:S(2)}) collective-permute-start(bf16[128,4096]{1,0:T(8,128)(2,1)S(1)} %constant_dynamic-slice_fusion), channel_id=1, source_target_pairs={{0,1},{1,0},{2,3},{3,2},{4,5},{5,4},{6,7},{7,6},{8,9},{9,8},{10,11... | collective-permute-start | bytes 3145736 | tf_op jit(solution)/shard_map/ppermute | solution.py:301
  250.7 8.8 %copy-start.6 = (bf16[4,1,256,256]{3,2,1,0:T(8,128)(2,1)S(1)}, bf16[4,1,256,256]{3,2,1,0:T(8,128)(2,1)}, u32[]{:S(2)}) copy-start(bf16[4,1,256,256]{3,2,1,0:T(8,128)(2,1)} %get-tuple-element.43) | copy-start | bytes 1572868
  253.9 15.7 %collective-permute-start.16 = (bf16[2,256,256]{2,1,0:T(8,128)(2,1)S(1)}, bf16[2,256,256]{2,1,0:T(8,128)(2,1)S(1)}, u32[]{:S(2)}, u32[]{:S(2)}) collective-permute-start(bf16[2,256,256]{2,1,0:T(8,128)(2,1)S(1)} %get-tuple-element.50), channel_id=1, source_target_pairs={{0,8},{2,10},{4,12},{6,14},{8,0},{10,2},{12,4},{14,6},{16,24},{18,... | collective-permute-start | bytes 786440 | tf_op jit(solution)/shard_map/ppermute | solution.py:265
  256.6 21.4 %collective-permute-start.17 = (bf16[2,256,256]{2,1,0:T(8,128)(2,1)S(1)}, bf16[2,256,256]{2,1,0:T(8,128)(2,1)S(1)}, u32[]{:S(2)}, u32[]{:S(2)}) collective-permute-start(bf16[2,256,256]{2,1,0:T(8,128)(2,1)S(1)} %get-tuple-element.52), channel_id=1, source_target_pairs={{0,16},{2,18},{4,20},{6,22},{8,24},{10,26},{12,28},{14,30},{16,0},... | collective-permute-start | bytes 786440 | tf_op jit(solution)/shard_map/ppermute | solution.py:265
  258.1 19.9 %collective-permute-start.18 = (bf16[2,256,256]{2,1,0:T(8,128)(2,1)S(1)}, bf16[2,256,256]{2,1,0:T(8,128)(2,1)S(1)}, u32[]{:S(2)}, u32[]{:S(2)}) collective-permute-start(bf16[2,256,256]{2,1,0:T(8,128)(2,1)S(1)} %get-tuple-element.51), channel_id=1, source_target_pairs={{0,24},{2,26},{4,28},{6,30},{8,16},{10,18},{12,20},{14,22},{16,8},... | collective-permute-start | bytes 786440 | tf_op jit(solution)/shard_map/ppermute | solution.py:265
  259.5 18.5 %copy-start.3 = (f32[1,256,256]{2,1,0:T(8,128)S(1)}, f32[1,256,256]{2,1,0:T(8,128)}, u32[]{:S(2)}) copy-start(f32[1,256,256]{2,1,0:T(8,128)} %get-tuple-element.54) | copy-start | bytes 786436
  261.4 17.5 %copy-start.9 = (bf16[4,1,256,256]{3,2,1,0:T(8,128)(2,1)S(1)}, bf16[4,1,256,256]{3,2,1,0:T(8,128)(2,1)}, u32[]{:S(2)}) copy-start(bf16[4,1,256,256]{3,2,1,0:T(8,128)(2,1)} %get-tuple-element.41) | copy-start | bytes 1572868
  261.4 17.5 %collective-permute-start.25 = (bf16[4,1,256,256]{3,2,0,1:T(8,128)(2,1)S(1)}, bf16[4,1,256,256]{3,2,0,1:T(8,128)(2,1)S(1)}, u32[]{:S(2)}, u32[]{:S(2)}) collective-permute-start(bf16[4,1,256,256]{3,2,0,1:T(8,128)(2,1)S(1)} %fusion.15), channel_id=1, source_target_pairs={{0,4},{2,6},{4,0},{6,2},{8,12},{10,14},{12,8},{14,10},{16,20},{18,... | collective-permute-start | bytes 1572872 | tf_op jit(solution)/shard_map/ppermute | solution.py:265
  278.9 17.9 %copy-start.15 = (f32[256,256]{1,0:T(8,128)S(1)}, f32[256,256]{1,0:T(8,128)}, u32[]{:S(2)}) copy-start(f32[256,256]{1,0:T(8,128)} %get-tuple-element.40) | copy-start | bytes 786436
  280.9 8.6 %collective-permute-start.26 = (bf16[1,256,256]{2,1,0:T(8,128)(2,1)S(1)}, bf16[1,256,256]{2,1,0:T(8,128)(2,1)S(1)}, u32[]{:S(2)}, u32[]{:S(2)}) collective-permute-start(bf16[1,256,256]{2,1,0:T(8,128)(2,1)S(1)} %get-tuple-element.58), channel_id=1, source_target_pairs={{0,8},{2,10},{4,12},{6,14},{8,0},{10,2},{12,4},{14,6},{16,24},{18,... | collective-permute-start | bytes 393224 | tf_op jit(solution)/shard_map/ppermute | solution.py:265
  285.3 11.5 %collective-permute-start.27 = (bf16[1,256,256]{2,1,0:T(8,128)(2,1)S(1)}, bf16[1,256,256]{2,1,0:T(8,128)(2,1)S(1)}, u32[]{:S(2)}, u32[]{:S(2)}) collective-permute-start(bf16[1,256,256]{2,1,0:T(8,128)(2,1)S(1)} %get-tuple-element.60), channel_id=1, source_target_pairs={{0,16},{2,18},{4,20},{6,22},{8,24},{10,26},{12,28},{14,30},{16,0},... | collective-permute-start | bytes 393224 | tf_op jit(solution)/shard_map/ppermute | solution.py:265
  286.8 10.1 %collective-permute-start.28 = (bf16[1,256,256]{2,1,0:T(8,128)(2,1)S(1)}, bf16[1,256,256]{2,1,0:T(8,128)(2,1)S(1)}, u32[]{:S(2)}, u32[]{:S(2)}) collective-permute-start(bf16[1,256,256]{2,1,0:T(8,128)(2,1)S(1)} %get-tuple-element.59), channel_id=1, source_target_pairs={{0,24},{2,26},{4,28},{6,30},{8,16},{10,18},{12,20},{14,22},{16,8},... | collective-permute-start | bytes 393224 | tf_op jit(solution)/shard_map/ppermute | solution.py:265

commit v3 on v2

--- a/solution.py
+++ b/solution.py
@@ -11,7 +11,7 @@
 NODE_LEN = 256
 CHAIN = 8
 LEAVES = 8
-GROUP = 4
+GROUP = 8
 
 masked_score = -1e30
 score_scale = HEAD_DIM ** (-0.5)
@@ -26,13 +26,14 @@
     return lax.dot_general(a, b, (((1,), (1,)), ((), ())), preferred_element_type=jnp.float32)
 
 
-def attend(
-    lineage, place, q_ref, up_ref, own_ref, near_0, near_1, near_2, near_3, *rest,
-):
+def attend(near_count, part_count, lineage, place, q_ref, up_ref, own_ref, *refs):
+    near = refs[:near_count]
+    tail = refs[len(refs) - 16 - part_count :]
+    att_ref, dq_ref, own_grad, token = tail[:4]
+    parts = tail[4 : 4 + part_count]
     (
-    att_ref, dq_ref, keep_ref, cross_ref, away_ref, own_grad, token,
-    far_ref, s_ref, p_ref, qs, ups, q_t, up_t, m_ref, l_ref, acc_ref, corr_ref, grad_t,
-    ) = rest[-19:]
+        far_ref, s_ref, p_ref, qs, ups, q_t, up_t, m_ref, l_ref, acc_ref, corr_ref, grad_t,
+    ) = tail[4 + part_count :]
     step = pl.program_id(1)
     depth = place[0]
     me = place[1]
@@ -56,12 +57,15 @@
         grad_t[...] = jnp.zeros_like(grad_t)
 
         def fetch(b, carry):
+            if near_count == 1:
+                far_ref[b] = near[0][lineage[b]]
+                return carry
             away = lineage[b] ^ me
-            for kind, ref in enumerate((near_0, near_1, near_2, near_3)):
+            for kind in range(near_count):
 
                 @pl.when(away % 4 == kind)
                 def _():
-                    far_ref[b] = ref[away // 4]
+                    far_ref[b] = near[kind][away // 4]
 
             return carry
 
@@ -116,8 +120,8 @@
     for h in range(heads):
         att_ref[:, head_columns(h)] = attended[h * NODE_LEN : (h + 1) * NODE_LEN, :]
     q_scaled = qs[...].astype(jnp.float32) * (inverse * score_scale)
-    q_t[...] = q_scaled.T.astype(jnp.bfloat16)
-    up_t[...] = (upstream * inverse).T.astype(jnp.bfloat16)
+    q_t[...] = q_scaled.astype(jnp.bfloat16).T
+    up_t[...] = (upstream * inverse).astype(jnp.bfloat16).T
 
     def backward(b, keys, values):
         corr = corr_ref[...]
@@ -142,15 +146,18 @@
 
     @pl.when(step == pl.num_programs(1) - 1)
     def _():
-        keep_ref[...] = jnp.zeros_like(keep_ref)
-        cross_ref[...] = jnp.zeros_like(cross_ref)
-        away_ref[...] = jnp.zeros_like(away_ref)
+        for part in parts:
+            part[...] = jnp.zeros_like(part)
         own_grad[...] = grad_t[CHAIN].T
         token[...] = jnp.zeros_like(token)
 
         def emit(b, carry):
+            block = grad_t[b].astype(jnp.bfloat16).T
+            if part_count == 1:
+                parts[0][lineage[b], 0] = block
+                return carry
+            keep_ref, cross_ref, away_ref = parts
             away = lineage[b] ^ me
-            block = grad_t[b].T.astype(jnp.bfloat16)
             kind = away % 4
             place_z = away // 4
 
@@ -172,17 +179,21 @@
 
 
 def attention(
-    first_head, chunk_head, heads, head_group, lineage, place, query_rows, upstream, own, near, after
+    first_head, chunk_head, heads, head_group, nodes, by_slot,
+    lineage, place, query_rows, upstream, own, near, after,
 ):
     group = min(GROUP, head_group)
     steps = head_group // group
-    stride = near[0].shape[0]
+    stride = nodes // 4
     width = group * HEAD_DIM
     rows = group * NODE_LEN
     pair = 2 * HEAD_DIM
 
-    def heads_in(i, j, *_):
+    def query_in(i, j, *_):
         return (0, (first_head + i) * steps + j)
+
+    def upstream_in(i, j, *_):
+        return (0, (chunk_head + i) * steps + j)
 
     def heads_out(i, j, *_):
         return (0, i * steps + j)
@@ -202,30 +213,44 @@
     def away_block(i, j, *_):
         return (0, 0, i, 0, 0)
 
+    def token_block(i, j, *_):
+        return (0, 0)
+
+    def part(count):
+        return (
+            pl.BlockSpec((count, 1, NODE_LEN, pair), part_block),
+            jax.ShapeDtypeStruct((count, heads, NODE_LEN, pair), jnp.bfloat16),
+        )
+
+    if by_slot:
+        parts = [part(nodes)]
+    else:
+        away = (
+            pl.BlockSpec((2, stride, 1, NODE_LEN, pair), away_block),
+            jax.ShapeDtypeStruct((2, stride, heads, NODE_LEN, pair), jnp.bfloat16),
+        )
+        parts = [part(stride), part(stride), away]
     blocks = (CHAIN + 1) * head_group * heads
     out_rows = jax.ShapeDtypeStruct((NODE_LEN, heads * head_group * HEAD_DIM), jnp.bfloat16)
-    part = jax.ShapeDtypeStruct((stride, heads, NODE_LEN, pair), jnp.bfloat16)
     return pl.pallas_call(
-        attend,
+        functools.partial(attend, len(near), len(parts)),
         grid_spec=pltpu.PrefetchScalarGridSpec(
             num_scalar_prefetch=2,
             grid=(heads, steps),
             in_specs=[
-                pl.BlockSpec((NODE_LEN, width), heads_in),
-                pl.BlockSpec((NODE_LEN, width), heads_in),
+                pl.BlockSpec((NODE_LEN, width), query_in),
+                pl.BlockSpec((NODE_LEN, width), upstream_in),
                 pl.BlockSpec((NODE_LEN, pair), own_in),
             ]
-            + [pl.BlockSpec((stride, NODE_LEN, pair), near_block)] * 4
+            + [pl.BlockSpec((block.shape[0], NODE_LEN, pair), near_block) for block in near]
             + [pl.BlockSpec(memory_space=pl.ANY)] * len(after),
             out_specs=[
                 pl.BlockSpec((NODE_LEN, width), heads_out),
                 pl.BlockSpec((NODE_LEN, width), heads_out),
-                pl.BlockSpec((stride, 1, NODE_LEN, pair), part_block),
-                pl.BlockSpec((stride, 1, NODE_LEN, pair), part_block),
-                pl.BlockSpec((2, stride, 1, NODE_LEN, pair), away_block),
                 pl.BlockSpec((NODE_LEN, pair), own_out),
-                pl.BlockSpec((8, HEAD_DIM), lambda i, j, *_: (0, 0)),
-            ],
+                pl.BlockSpec((8, HEAD_DIM), token_block),
+            ]
+            + [spec for spec, _ in parts],
             scratch_shapes=[
                 pltpu.VMEM((CHAIN, NODE_LEN, pair), jnp.bfloat16),
                 pltpu.VMEM((CHAIN + 1, rows, NODE_LEN), jnp.float32),
@@ -244,12 +269,10 @@
         out_shape=[
             out_rows,
             out_rows,
-            part,
-            part,
-            jax.ShapeDtypeStruct((2, stride, heads, NODE_LEN, pair), jnp.bfloat16),
             jax.ShapeDtypeStruct((NODE_LEN, heads * pair), jnp.float32),
             jax.ShapeDtypeStruct((8, HEAD_DIM), jnp.float32),
-        ],
+        ]
+        + [shape for _, shape in parts],
         compiler_params=pltpu.CompilerParams(
             dimension_semantics=("arbitrary", "arbitrary"), vmem_limit_bytes=60 * 1024 * 1024
         ),
@@ -261,13 +284,24 @@
     )(lineage, place, query_rows, upstream, own, *near, *after)
 
 
+def zero_of(value):
+    return jnp.minimum(jnp.abs(value.astype(jnp.float32)), 0.0)
+
+
 def swap(block, mask, nodes):
     return lax.ppermute(block, "node", [(i, i ^ mask) for i in range(nodes)])
 
 
-def gather_near(own, nodes):
+def when_there(value, parts):
+    for part in parts:
+        value = value + zero_of(part[(0,) * part.ndim]).astype(value.dtype)
+    return value
+
+
+def gather_near(own, nodes, zero):
     stride = nodes // 4
     line = jnp.stack([own] + [swap(own, 4 * d, nodes) for d in range(1, stride)])
+    line = line + zero.astype(line.dtype)
     cross = swap(line, 2, nodes)
     return line, swap(line, 1, nodes), cross, swap(cross, 1, nodes)
 
@@ -288,31 +322,25 @@
     total = own_part + (keep[0] + zero)
     for part in came:
         total = total + part.astype(f32)
-    yield [total.astype(jnp.bfloat16)]
-
-
-def exchange_sum(part, tp):
-    rows = part.shape[0] // tp
+    return total.astype(jnp.bfloat16)
+
+
+def other_rows(block, tp):
     if tp != 2:
-        return lax.psum_scatter(part, "tp", scatter_dimension=0, tiled=True)
-    me = lax.axis_index("tp")
-    away = lax.dynamic_slice_in_dim(part, (1 - me) * rows, rows, 0)
-    here = lax.dynamic_slice_in_dim(part, me * rows, rows, 0)
-    came = lax.ppermute(away, "tp", [(0, 1), (1, 0)])
-    return (here.astype(jnp.float32) + came.astype(jnp.float32)).astype(jnp.bfloat16)
-
-
-def gather_rows(block, tp):
-    if tp != 2:
-        return lax.all_gather(block, "tp", axis=0, tiled=True)
+        whole = lax.all_gather(block, "tp", axis=0, tiled=True)
+        return whole, whole
     me = lax.axis_index("tp")
     came = lax.ppermute(block, "tp", [(0, 1), (1, 0)])
-    return jnp.where(
-        me == 0, jnp.concatenate([block, came], axis=0), jnp.concatenate([came, block], axis=0)
+    return (
+        jnp.where(
+            me == 0, jnp.concatenate([block, came], axis=0), jnp.concatenate([came, block], axis=0)
+        ),
+        came,
     )
 
 
 def local(tp, nodes, query_rows, key_rows, value_rows, out_weight, out_grad, owner_slot):
+    bf16, f32 = jnp.bfloat16, jnp.float32
     node_count = owner_slot.shape[0]
     tree_nodes = CHAIN + LEAVES
     kv_width = key_rows.shape[1]
@@ -326,47 +354,79 @@
     place = jnp.stack([depth, my_slot]).astype(jnp.int32)
     lineage = lax.dynamic_slice_in_dim(owner_slot, tree_node // tree_nodes * tree_nodes, CHAIN)
 
-    out_grad_rows = gather_rows(out_grad, tp)
     wide = min(2, kv_heads)
-    own, near = [], []
-    for c in range(kv_heads // wide):
-        parts = []
-        for k in range(c * wide, (c + 1) * wide):
+    chunks = [(0, wide)] + ([(wide, kv_heads - wide)] if kv_heads > wide else [])
+    calls = [(0, 0, wide)] + [(1, k, 1) for k in range(wide, kv_heads)]
+
+    out_grad_rows, came = other_rows(out_grad, tp)
+    own, near, upstream = [], [], []
+    for first, heads in chunks:
+        packed = []
+        for k in range(first, first + heads):
             columns = slice(k * HEAD_DIM, (k + 1) * HEAD_DIM)
-            parts += [key_rows[:, columns], value_rows[:, columns]]
-        own.append(jnp.concatenate(parts, axis=1))
-        near.append(gather_near(own[c], nodes))
-    upstream = dot_nt(out_grad_rows, out_weight).astype(jnp.bfloat16)
-
-    calls = [(0, wide)] + [(k, 1) for k in range(wide, kv_heads)]
+            packed += [key_rows[:, columns], value_rows[:, columns]]
+        packed = jnp.concatenate(packed, axis=1)
+        own.append(packed)
+        if first == 0:
+            near.append(gather_near(packed, nodes, zero_of(came[0, 0])))
+        else:
+            packed = packed + zero_of(near[0][0][0, 0, 0]).astype(bf16)
+            near.append([lax.all_gather(packed, "node", axis=0, tiled=False)])
+        width = head_group * HEAD_DIM
+        weight_rows = out_weight[first * width : (first + heads) * width]
+        upstream.append(dot_nt(out_grad_rows, weight_rows).astype(bf16))
+
     attended, query_grad, sums, sent = [], [], [], []
-    for first, heads in calls:
-        c = first // wide
-        att, dq, keep, cross, away, own_part, token = attention(
-            first, first % wide, heads, head_group, lineage, place,
-            query_rows, upstream, own[c], near[c], sent,
+    first_sum = None
+    for n, (c, first, heads) in enumerate(calls):
+        by_slot = n == 0 and len(calls) > 1
+        att, dq, own_part, token, *parts = attention(
+            first, first - chunks[c][0], heads, head_group, nodes, by_slot,
+            lineage, place, query_rows, upstream[c], own[c], near[c], sent,
         )
         attended.append(att)
         query_grad.append(dq)
         own_part = jnp.stack([own_part[:, i * pair : (i + 1) * pair] for i in range(heads)])
         zero = token[0, 0]
         sent = [part for chain in sums for part in chain.send(zero)]
-        sums.append(scatter_sum(keep, cross, away, own_part, nodes))
-        sent += next(sums[-1])
-
-    projected = dot(jnp.concatenate(attended, axis=1), out_weight).astype(jnp.bfloat16)
-    projected = exchange_sum(projected, tp)
-    totals = [None] * len(sums)
-    left = [max(1, 3 - (len(sums) - 1 - n)) for n in range(len(sums))]
-    for turn in range(3):
-        for n in range(len(sums)):
-            if turn < left[n]:
-                totals[n] = sums[n].send(zero)[0]
-    key_grad, value_grad = [], []
-    for (first, heads), total in zip(calls, totals):
-        for i in range(heads):
-            key_grad.append(total[i, :, :HEAD_DIM])
-            value_grad.append(total[i, :, HEAD_DIM:])
+        if by_slot:
+            first_sum = (own_part, lax.psum_scatter(parts[0], "node", scatter_dimension=0, tiled=False))
+            sent = [token]
+        else:
+            sums.append(scatter_sum(*parts, own_part, nodes))
+            sent += next(sums[-1])
+
+    attended = jnp.concatenate(attended, axis=1)
+    if tp == 2:
+        rows = attended.shape[0] // tp
+        me = lax.axis_index("tp")
+        away_rows = when_there(lax.dynamic_slice_in_dim(attended, (1 - me) * rows, rows, 0), sent)
+        away = dot(away_rows, out_weight).astype(bf16)
+        came = lax.ppermute(away, "tp", [(0, 1), (1, 0)])
+        zero = zero_of(away[0, 0])
+        sent = [part for chain in sums for part in chain.send(zero)]
+        here_rows = when_there(lax.dynamic_slice_in_dim(attended, me * rows, rows, 0), sent)
+        here = lax.optimization_barrier(dot(here_rows, out_weight))
+        zero = zero_of(here[0, 0])
+        projected = (here + came.astype(f32)).astype(bf16)
+    else:
+        projected = dot(attended, out_weight).astype(bf16)
+        projected = lax.psum_scatter(projected, "tp", scatter_dimension=0, tiled=True)
+    totals = {}
+    while len(totals) < len(sums):
+        for n, chain in enumerate(sums):
+            if n not in totals:
+                try:
+                    chain.send(zero)
+                except StopIteration as end:
+                    totals[n] = end.value
+    totals = [totals[n] for n in range(len(sums))]
+    if first_sum is not None:
+        own_part, came = first_sum
+        zero = zero_of(totals[-1][0, 0, 0])
+        totals = [(own_part + (came.astype(f32) + zero)).astype(bf16)] + totals
+    key_grad = [total[i, :, :HEAD_DIM] for total in totals for i in range(total.shape[0])]
+    value_grad = [total[i, :, HEAD_DIM:] for total in totals for i in range(total.shape[0])]
     return (
         projected,
         jnp.concatenate(query_grad, axis=1),

time: 299 us -> 267 us (0.89)
  starting transfers between devices: 74.2 us -> 20.1 us
  waiting for transfers between devices: 72.1 us -> 44.9 us
  between operations: 3.64 us -> 24.3 us
  matrix products: 36.6 us -> 50.4 us
  local copies, waits for them, and re-layouts: 6.24 us -> 17.6 us
  Pallas kernels: 84.1 us -> 93.2 us
  other arithmetic: 22.2 us -> 15.8 us
    ppermute x27 -> x16, starting transfers between devices: 72.1 us -> 17 us  [swap(): return lax.ppermute(block, 'node', [(i, i ^ mask) for i in range(nodes)])]
    ppermute x27 -> x16, waiting for transfers between devices: 66.2 us -> 27.2 us  [swap(): return lax.ppermute(block, 'node', [(i, i ^ mask) for i in range(nodes)])]
    ppermute x2, waiting for transfers between devices: 5.89 us -> 17.6 us  [the longest x1 17.6 us: other_rows(): came = lax.ppermute(block, 'tp', [(0, 1), (1, 0)])]
    dot_general x1 -> x2, matrix products: 15.8 us -> 26.3 us  [dot(): return jnp.dot(a, b, preferred_element_type=jnp.float32)]
    pallas_call x3, Pallas kernels: 84.1 us -> 93.2 us  [attention(): pl.pallas_call(functools.partial(attend, len(near), len(parts)), grid_spe...]
    slice x1 -> x11, local copies, waits for them, and re-layouts: 1.12 us -> 8.02 us  [the longest x6 5.38 us: when_there(): value = value + zero_of(part[(0,) * part.ndim]).astype(value.dtype)]
    convert_element_type x3 -> x2, other arithmetic: 5.98 us -> 0.9 us  [scatter_sum(): (cross.astype(f32) + (came[1].astype(f32) + zero)).astype(jnp.bfloat16)]
    another operation x3 -> x2, other arithmetic: 7.29 us -> 3.4 us
  transfers between devices with their start and end apart: 29 -> 20, of which waited for: 12 -> 6; matrix products, arithmetic and copies ran while one was open for 20% -> 30% of each run, Pallas kernels for 28% -> 35%
where the time goes in v3:
time: 267 us; the launch traced here: 266 us
  Pallas kernels  93.2 us (35%)
  matrix products  50.4 us (19%)
  waiting for transfers between devices  44.9 us (17%)
  between operations  24.3 us (9%)
  starting transfers between devices  20.1 us (8%)
  local copies, waits for them, and re-layouts  17.6 us (7%)
  other arithmetic  15.8 us (6%)
    pallas_call x3, Pallas kernels, attention(): pl.pallas_call(functools.partial(attend, len(near), len(parts)), grid_spe...  93.2 us
    ppermute x16, waiting for transfers between devices, swap(): return lax.ppermute(block, 'node', [(i, i ^ mask) for i in range(nodes)])  27.2 us
    dot_general x2, matrix products, dot(): return jnp.dot(a, b, preferred_element_type=jnp.float32)  26.3 us
    dot_general x2, matrix products, dot_nt(): lax.dot_general(a, b, (((1,), (1,)), ((), ())), preferred_element_type=jn...  24 us
    ppermute x1, waiting for transfers between devices, other_rows(): came = lax.ppermute(block, 'tp', [(0, 1), (1, 0)])  17.6 us
    ppermute x16, starting transfers between devices, swap(): return lax.ppermute(block, 'node', [(i, i ^ mask) for i in range(nodes)])  17 us
    slice x6, local copies, waits for them, and re-layouts, when_there(): value = value + zero_of(part[(0,) * part.ndim]).astype(value.dtype)  5.38 us
  transfers between devices with their start and end apart: 20, of which 6 were waited for; matrix products, arithmetic and copies ran while one was open for 30% of the time, Pallas kernels for 35%

profile of v3, /device:TPU:0, one launch (start us, length us, event | category | flops | bytes accessed | tf_op | source)
XLA Modules:
  0.0 266.3 jit_solution(5590553496950824056)
XLA Ops:
  7.2 0.0 all-gather.2.cloned.1.call-start
  7.2 3.0 %collective-permute-start = (bf16[128,4096]{1,0:T(8,128)(2,1)}, bf16[128,4096]{1,0:T(8,128)(2,1)S(1)}, u32[]{:S(2)}, u32[]{:S(2)}) collective-permute-start(bf16[128,4096]{1,0:T(8,128)(2,1)} %param.10), channel_id=1, source_target_pairs={{0,1},{1,0},{2,3},{3,2},{4,5},{5,4},{6,7},{7,6},{8,9},{9,8},{10,11... | collective-permute-start | bytes 3145736 | tf_op jit(solution)/shard_map/ppermute | solution.py:333
  10.2 1.2 slice_bitcast_fusion.18
  11.5 3.7 %collective-permute-start.3 = (bf16[256,512]{1,0:T(8,128)(2,1)S(1)}, bf16[256,512]{1,0:T(8,128)(2,1)S(1)}, u32[]{:S(2)}, u32[]{:S(2)}) collective-permute-start(bf16[256,512]{1,0:T(8,128)(2,1)S(1)} %get-tuple-element.68.own_ref), channel_id=1, source_target_pairs={{0,24},{2,26},{4,28},{6,30},{8,16},{10,18},{12,20},{14,22},{16,8},... | collective-permute-start | bytes 786440 | tf_op jit(solution)/shard_map/ppermute | solution.py:292
  15.2 0.8 collective-permute-start.1
  16.0 17.6 %collective-permute-done = bf16[128,4096]{1,0:T(8,128)(2,1)S(1)} collective-permute-done((bf16[128,4096]{1,0:T(8,128)(2,1)}, bf16[128,4096]{1,0:T(8,128)(2,1)S(1)}, u32[]{:S(2)}, u32[]{:S(2)}) %collective-permute-start) | collective-permute-done | bytes 1048608 | tf_op jit(solution)/shard_map/ppermute | solution.py:333
  33.6 0.5 slice.182
  34.8 2.4 collective-permute-done.2
  37.2 0.1 maximum_add_fusion.refs_0_
  37.4 0.5 slice.183
  38.6 0.8 maximum_add_fusion.2
  39.4 0.0 all-gather.2.cloned.1.call-update
  39.4 0.0 reduce-scatter.2.cloned.1.call-start
  39.5 0.6 fusion.44
  42.7 0.6 dynamic_slice.9.lineage
  43.3 0.7 pad_add_fusion.place
  44.0 0.7 pad_maximum_fusion.2.own_ref
  44.7 1.5 collective-permute-start.5
  46.2 12.0 %fusion.7.up_ref = bf16[256,2048]{1,0:T(8,128)(2,1)} fusion(bf16[4096,4096]{1,0:T(8,128)(2,1)} %param.9, bf16[128,4096]{1,0:T(8,128)(2,1)} %copy-done.18, bf16[128,4096]{1,0:T(8,128)(2,1)S(1)} %copy-done.17, pred[]{:T(512)S(6)} %eq.13), kind=kOutput, calls=%fused_computation.6 | convolution fusion | flops 4304928768 | bytes 19922944 | tf_op jit(solution)/shard_map/dot_general | solution.py:26
  58.3 17.1 %collective-permute-done.5.refs_2_ = bf16[4,256,512]{2,1,0:T(8,128)(2,1)} collective-permute-done((bf16[4,256,512]{2,1,0:T(8,128)(2,1)S(1)}, bf16[4,256,512]{2,1,0:T(8,128)(2,1)}, u32[]{:S(2)}, u32[]{:S(2)}) %collective-permute-start.5) | collective-permute-done | bytes 1048608 | tf_op jit(solution)/shard_map/ppermute | solution.py:292
  75.3 12.0 %fusion.4.up_ref = bf16[256,2048]{1,0:T(8,128)(2,1)} fusion(bf16[4096,4096]{1,0:T(8,128)(2,1)} %param.9, bf16[128,4096]{1,0:T(8,128)(2,1)} %copy-done.18, bf16[128,4096]{1,0:T(8,128)(2,1)S(1)} %copy-done.17, pred[]{:T(512)S(6)} %eq.13), kind=kOutput, calls=%fused_computation.5 | convolution fusion | flops 4304928768 | bytes 19922944 | tf_op jit(solution)/shard_map/dot_general | solution.py:26
  87.3 44.5 %shard_map.93 = (bf16[256,2048]{1,0:T(8,128)(2,1)}, bf16[256,2048]{1,0:T(8,128)(2,1)}, f32[256,512]{1,0:T(8,128)}, f32[8,128]{1,0:T(8,128)}, bf16[16,2,256,256]{3,2,1,0:T(8,128)(2,1)}) custom-call(s32[8]{0:T(128)} %dynamic_slice.9.lineage, s32[2]{0:T(128)} %pad_add_fusion.place, bf16[256,4096]{1,0:T(8,128)(2,1)} %q_ref.5, bf16[256,2048]{1,0:T(8,128)(2,1)} %fusion.4.up_ref, ...), custom_call_target="tpu_custom_call" | custom-call | flops 14495514624 | bytes 33554432 | tf_op jit(solution)/shard_map/pallas_call | solution.py:235
  131.8 1.8 slice_bitcast_fusion.1
  133.6 1.3 constant_dynamic-update-slice_fusion.2
  134.9 0.0 reduce-scatter.2.cloned.1.call-update
  134.9 0.0 all-gather.2.cloned.1.call-done.refs_0_
  134.9 24.2 %shard_map.94 = (bf16[256,1024]{1,0:T(8,128)(2,1)}, bf16[256,1024]{1,0:T(8,128)(2,1)}, f32[256,256]{1,0:T(8,128)}, f32[8,128]{1,0:T(8,128)}, bf16[4,1,256,256]{3...) custom-call(s32[8]{0:T(128)} %dynamic_slice.9.lineage, s32[2]{0:T(128)} %pad_add_fusion.place, ...), custom_call_target="tpu_custom_call" | custom-call | flops 7247757312 | bytes 16777216 | tf_op jit(solution)/shard_map/pallas_call | solution.py:235
  159.1 24.5 %shard_map.95 = (bf16[256,1024]{1,0:T(8,128)(2,1)}, bf16[256,1024]{1,0:T(8,128)(2,1)}, f32[256,256]{1,0:T(8,128)}, f32[8,128]{1,0:T(8,128)}, bf16[4,1,256,256]{3...) custom-call(s32[8]{0:T(128)} %dynamic_slice.9.lineage, s32[2]{0:T(128)} %pad_add_fusion.place, ...), custom_call_target="tpu_custom_call" | custom-call | flops 7247757312 | bytes 16777216 | tf_op jit(solution)/shard_map/pallas_call | solution.py:235
  183.7 1.3 slice.154
  185.7 1.2 slice.151
  186.9 1.1 constant_dynamic-update-slice_fusion
  188.0 1.5 pad_maximum_fusion
  189.6 0.7 fusion.11
  190.3 0.5 slice.186
  190.8 3.1 %collective-permute-start.8 = (bf16[4,1,256,256]{3,2,1,0:T(8,128)(2,1)S(1)}, bf16[4,1,256,256]{3,2,1,0:T(8,128)(2,1)S(1)}, u32[]{:S(2)}, u32[]{:S(2)}) collective-permute-start(bf16[4,1,256,256]{3,2,1,0:T(8,128)(2,1)S(1)} %fusion.11), channel_id=1, source_target_pairs={{0,4},{2,6},{4,0},{6,2},{8,12},{10,14},{12,8},{14,10},{16,20},{18,... | collective-permute-start | bytes 1572872 | tf_op jit(solution)/shard_map/ppermute | solution.py:292
  194.6 13.3 %convolution_convert_fusion = bf16[128,4096]{1,0:T(8,128)(2,1)S(1)} fusion(bf16[4096,4096]{1,0:T(8,128)(2,1)} %param.9, bf16[256,4096]{1,0:T(8,128)(2,1)S(1)} %constant_dynamic-update-slice_fusion, s32[]{:T(128)S(6)} %select_n.39, bf16[]{:T(256)} %bitcast.19, bf16[]{:T(256)} %bitcast.18), kind=kOutput, calls=%fused_computation.4 | convolution fusion | flops 4298637312 | bytes 35651592 | tf_op jit(solution)/shard_map/dot_general | solution.py:22
  207.9 0.5 slice.187
  209.1 0.2 fusion.10
  209.3 0.5 slice.195
  210.6 0.8 copy-done.10
  211.4 2.0 fusion.50
  213.5 0.7 slice_bitcast_fusion.7
  214.2 1.2 slice.189
  215.4 1.3 slice.193
  216.7 0.1 collective-permute-start.17
  216.8 0.5 slice.191
  217.3 3.4 %collective-permute-start.16 = (bf16[1,256,256]{2,1,0:T(8,128)(2,1)S(1)}, bf16[1,256,256]{2,1,0:T(8,128)(2,1)}, u32[]{:S(2)}, u32[]{:S(2)}) collective-permute-start(bf16[1,256,256]{2,1,0:T(8,128)(2,1)S(1)} %get-tuple-element.50), channel_id=1, source_target_pairs={{0,16},{2,18},{4,20},{6,22},{8,24},{10,26},{12,28},{14,30},{16,0},... | collective-permute-start | bytes 393224 | tf_op jit(solution)/shard_map/ppermute | solution.py:292
  222.6 13.0 %fusion.12 = f32[128,4096]{1,0:T(8,128)S(1)} fusion(bf16[4096,4096]{1,0:T(8,128)(2,1)} %param.9, bf16[256,4096]{1,0:T(8,128)(2,1)S(1)} %copy-done.1, s32[]{:T(128)S(6)} %select_n.38, bf16[]{:T(256)} %bitcast.29, bf16[]{:T(256)} %bitcast.26, bf16[]{:T(256)} %bitcast.24, bf16[]{:T(256)} %bitcast.22), kind=kOutput, calls=%fused_computation.20 | convolution fusion | flops 4300210176 | bytes 36700172 | tf_op jit(solution)/shard_map/dot_general | solution.py:22
  235.6 0.5 slice.197
  236.9 1.4 fusion.21
  238.2 1.0 collective-permute-start.14
  239.2 0.1 collective-permute-start.12
  239.3 3.5 %collective-permute-start.13 = (bf16[1,256,256]{2,1,0:T(8,128)(2,1)S(1)}, bf16[1,256,256]{2,1,0:T(8,128)(2,1)S(1)}, u32[]{:S(2)}, u32[]{:S(2)}) collective-permute-start(bf16[1,256,256]{2,1,0:T(8,128)(2,1)S(1)} %get-tuple-element.47), channel_id=1, source_target_pairs={{0,16},{2,18},{4,20},{6,22},{8,24},{10,26},{12,28},{14,30},{16,0},... | collective-permute-start | bytes 393224 | tf_op jit(solution)/shard_map/ppermute | solution.py:292
  242.8 1.1 fusion.36
  243.9 2.7 %collective-permute-done.14 = bf16[1,256,256]{2,1,0:T(8,128)(2,1)S(1)} collective-permute-done((bf16[1,256,256]{2,1,0:T(8,128)(2,1)S(1)}, bf16[1,256,256]{2,1,0:T(8,128)(2,1)S(1)}, u32[]{:S(2)}, u32[]{:S(2)}) %collective-permute-start.14) | collective-permute-done | bytes 131104 | tf_op jit(solution)/shard_map/ppermute | solution.py:292
  246.6 0.5 collective-permute-done.12
  247.2 4.5 %collective-permute-done.13 = bf16[1,256,256]{2,1,0:T(8,128)(2,1)S(1)} collective-permute-done((bf16[1,256,256]{2,1,0:T(8,128)(2,1)S(1)}, bf16[1,256,256]{2,1,0:T(8,128)(2,1)S(1)}, u32[]{:S(2)}, u32[]{:S(2)}) %collective-permute-start.13) | collective-permute-done | bytes 131104 | tf_op jit(solution)/shard_map/ppermute | solution.py:292
  251.6 0.1 fusion.43
  251.8 0.5 slice.202
  252.9 0.7 slice_bitcast_fusion.9
  253.6 1.1 fusion.23
  254.8 1.6 pad_maximum_fusion.4
  256.3 0.7 pad_maximum_fusion.3
  257.1 2.4 add_convert_fusion
  (66 shorter events, 0.3 us)
Async XLA Ops:
  7.2 127.8 %all-gather.2.cloned.1.call-start = ((), (), s32[]{:S(2)}) async-start(), calls=%async_computation.1 | async-start | bytes 4456448 | tf_op jit(solution)/shard_map/all_gather | solution.py:374
  7.2 26.4 %collective-permute-start = (bf16[128,4096]{1,0:T(8,128)(2,1)}, bf16[128,4096]{1,0:T(8,128)(2,1)S(1)}, u32[]{:S(2)}, u32[]{:S(2)}) collective-permute-start(bf16[128,4096]{1,0:T(8,128)(2,1)} %param.10), channel_id=1, source_target_pairs={{0,1},{1,0},{2,3},{3,2},{4,5},{5,4},{6,7},{7,6},{8,9},{9,8},{10,11... | collective-permute-start | bytes 3145736 | tf_op jit(solution)/shard_map/ppermute | solution.py:333
  11.4 28.0 %copy-start.19 = (s32[16]{0:T(128)S(1)}, s32[16]{0:T(128)}, u32[]{:S(2)}) copy-start(s32[16]{0:T(128)} %param.11) | copy-start | bytes 196
  11.4 34.8 %copy-start.17 = (bf16[128,4096]{1,0:T(8,128)(2,1)S(1)}, bf16[128,4096]{1,0:T(8,128)(2,1)}, u32[]{:S(2)}) copy-start(bf16[128,4096]{1,0:T(8,128)(2,1)} %param.10) | copy-start | bytes 3145732
  11.5 46.7 %copy-start.13 = (bf16[256,512]{1,0:T(8,128)(2,1)}, bf16[256,512]{1,0:T(8,128)(2,1)S(1)}, u32[]{:S(2)}) copy-start(bf16[256,512]{1,0:T(8,128)(2,1)S(1)} %get-tuple-element.68.own_ref) | copy-start | bytes 786436
  11.5 23.3 %collective-permute-start.3 = (bf16[256,512]{1,0:T(8,128)(2,1)S(1)}, bf16[256,512]{1,0:T(8,128)(2,1)S(1)}, u32[]{:S(2)}, u32[]{:S(2)}) collective-permute-start(bf16[256,512]{1,0:T(8,128)(2,1)S(1)} %get-tuple-element.68.own_ref), channel_id=1, source_target_pairs={{0,24},{2,26},{4,28},{6,30},{8,16},{10,18},{12,20},{14,22},{16,8},... | collective-permute-start | bytes 786440 | tf_op jit(solution)/shard_map/ppermute | solution.py:292
  15.2 22.0 %collective-permute-start.2 = (bf16[256,512]{1,0:T(8,128)(2,1)S(1)}, bf16[256,512]{1,0:T(8,128)(2,1)S(1)}, u32[]{:S(2)}, u32[]{:S(2)}) collective-permute-start(bf16[256,512]{1,0:T(8,128)(2,1)S(1)} %get-tuple-element.68.own_ref), channel_id=1, source_target_pairs={{0,16},{2,18},{4,20},{6,22},{8,24},{10,26},{12,28},{14,30},{16,0},... | collective-permute-start | bytes 786440 | tf_op jit(solution)/shard_map/ppermute | solution.py:292
  15.2 22.0 %collective-permute-start.1 = (bf16[256,512]{1,0:T(8,128)(2,1)S(1)}, bf16[256,512]{1,0:T(8,128)(2,1)S(1)}, u32[]{:S(2)}, u32[]{:S(2)}) collective-permute-start(bf16[256,512]{1,0:T(8,128)(2,1)S(1)} %get-tuple-element.68.own_ref), channel_id=1, source_target_pairs={{0,8},{2,10},{4,12},{6,14},{8,0},{10,2},{12,4},{14,6},{16,24},{18,... | collective-permute-start | bytes 786440 | tf_op jit(solution)/shard_map/ppermute | solution.py:292
  33.6 3.6 %copy-start.18 = (bf16[128,4096]{1,0:T(8,128)(2,1)}, bf16[128,4096]{1,0:T(8,128)(2,1)S(1)}, u32[]{:S(2)}) copy-start(bf16[128,4096]{1,0:T(8,128)(2,1)S(1)} %collective-permute-done) | copy-start | bytes 3145732
  37.4 20.9 %copy-start.2 = (bf16[4,256,512]{2,1,0:T(8,128)(2,1)}, bf16[4,256,512]{2,1,0:T(8,128)(2,1)S(1)}, u32[]{:S(2)}) copy-start(bf16[4,256,512]{2,1,0:T(8,128)(2,1)S(1)} %maximum_add_fusion.refs_0_) | copy-start | bytes 3145732
  39.4 214.2 %reduce-scatter.2.cloned.1.call-start = ((), (), s32[]{:S(2)}) async-start(), calls=%async_computation.2 | async-start | bytes 4456448 | tf_op jit(solution)/shard_map/reduce_scatter | solution.py:393
  44.7 30.6 %collective-permute-start.5 = (bf16[4,256,512]{2,1,0:T(8,128)(2,1)S(1)}, bf16[4,256,512]{2,1,0:T(8,128)(2,1)}, u32[]{:S(2)}, u32[]{:S(2)}) collective-permute-start(bf16[4,256,512]{2,1,0:T(8,128)(2,1)S(1)} %maximum_add_fusion.refs_0_), channel_id=1, source_target_pairs={{0,4},{2,6},{4,0},{6,2},{8,12},{10,14},{12,8},{14,10},{16,20},{18,... | collective-permute-start | bytes 3145736 | tf_op jit(solution)/shard_map/ppermute | solution.py:292
  46.2 41.1 %collective-permute-start.4 = (bf16[4,256,512]{2,1,0:T(8,128)(2,1)S(1)}, bf16[4,256,512]{2,1,0:T(8,128)(2,1)}, u32[]{:S(2)}, u32[]{:S(2)}) collective-permute-start(bf16[4,256,512]{2,1,0:T(8,128)(2,1)S(1)} %maximum_add_fusion.refs_0_), channel_id=1, source_target_pairs={{0,2},{2,0},{4,6},{6,4},{8,10},{10,8},{12,14},{14,12},{16,18},{18,... | collective-permute-start | bytes 3145736 | tf_op jit(solution)/shard_map/ppermute | solution.py:292
  75.3 12.0 %collective-permute-start.6 = (bf16[4,256,512]{2,1,0:T(8,128)(2,1)}, bf16[4,256,512]{2,1,0:T(8,128)(2,1)}, u32[]{:S(2)}, u32[]{:S(2)}) collective-permute-start(bf16[4,256,512]{2,1,0:T(8,128)(2,1)} %collective-permute-done.5.refs_2_), channel_id=1, source_target_pairs={{0,2},{2,0},{4,6},{6,4},{8,10},{10,8},{12,14},{14,12},{16,18},{18,... | collective-permute-start | bytes 3145736 | tf_op jit(solution)/shard_map/ppermute | solution.py:292
  159.1 27.7 %copy-start.8 = (bf16[256,1024]{1,0:T(8,128)(2,1)S(1)}, bf16[256,1024]{1,0:T(8,128)(2,1)}, u32[]{:S(2)}) copy-start(bf16[256,1024]{1,0:T(8,128)(2,1)} %get-tuple-element.24) | copy-start | bytes 1572868
  159.1 30.4 %collective-permute-start.7 = (bf16[2,4,1,256,256]{4,3,1,2,0:T(8,128)(2,1)}, bf16[2,4,1,256,256]{4,3,1,2,0:T(8,128)(2,1)S(1)}, u32[]{:S(2)}, u32[]{:S(2)}) collective-permute-start(bf16[2,4,1,256,256]{4,3,1,2,0:T(8,128)(2,1)} %bitcast.166), channel_id=1, source_target_pairs={{0,2},{2,0},{4,6},{6,4},{8,10},{10,8},{12,14},{14,12},{16,18},{18,... | collective-permute-start | bytes 3145736 | tf_op jit(solution)/shard_map/ppermute | solution.py:292
  183.7 4.3 %copy-start.5 = (bf16[256,2048]{1,0:T(8,128)(2,1)S(1)}, bf16[256,2048]{1,0:T(8,128)(2,1)}, u32[]{:S(2)}) copy-start(bf16[256,2048]{1,0:T(8,128)(2,1)} %get-tuple-element.32) | copy-start | bytes 3145732
  183.7 4.3 %copy-start.11 = (bf16[256,1024]{1,0:T(8,128)(2,1)S(1)}, bf16[256,1024]{1,0:T(8,128)(2,1)}, u32[]{:S(2)}) copy-start(bf16[256,1024]{1,0:T(8,128)(2,1)} %get-tuple-element.33) | copy-start | bytes 1572868
  183.7 4.4 %copy-start.12 = (bf16[256,1024]{1,0:T(8,128)(2,1)S(1)}, bf16[256,1024]{1,0:T(8,128)(2,1)}, u32[]{:S(2)}) copy-start(bf16[256,1024]{1,0:T(8,128)(2,1)} %get-tuple-element.34) | copy-start | bytes 1572868
  185.0 24.1 %collective-permute-start.9 = (bf16[2,4,1,256,256]{4,3,2,1,0:T(8,128)(2,1)}, bf16[2,4,1,256,256]{4,3,2,1,0:T(8,128)(2,1)S(1)}, u32[]{:S(2)}, u32[]{:S(2)}) collective-permute-start(bf16[2,4,1,256,256]{4,3,2,1,0:T(8,128)(2,1)} %get-tuple-element.30), channel_id=1, source_target_pairs={{0,2},{2,0},{4,6},{6,4},{8,10},{10,8},{12,14},{14,12},{16,18},{18,... | collective-permute-start | bytes 3145736 | tf_op jit(solution)/shard_map/ppermute | solution.py:292
  188.0 6.6 %copy-start = (bf16[256,4096]{1,0:T(8,128)(2,1)}, bf16[256,4096]{1,0:T(8,128)(2,1)S(1)}, u32[]{:S(2)}) copy-start(bf16[256,4096]{1,0:T(8,128)(2,1)S(1)} %constant_dynamic-update-slice_fusion) | copy-start | bytes 6291460
  188.0 1.5 copy-start.7
  189.6 5.0 %copy-start.3 = (bf16[2,4,1,256,256]{4,3,1,2,0:T(8,128)(2,1)}, bf16[2,4,1,256,256]{4,3,1,2,0:T(8,128)(2,1)S(1)}, u32[]{:S(2)}) copy-start(bf16[2,4,1,256,256]{4,3,1,2,0:T(8,128)(2,1)S(1)} %collective-permute-done.7) | copy-start | bytes 3145732
  190.8 19.7 %collective-permute-start.8 = (bf16[4,1,256,256]{3,2,1,0:T(8,128)(2,1)S(1)}, bf16[4,1,256,256]{3,2,1,0:T(8,128)(2,1)S(1)}, u32[]{:S(2)}, u32[]{:S(2)}) collective-permute-start(bf16[4,1,256,256]{3,2,1,0:T(8,128)(2,1)S(1)} %fusion.11), channel_id=1, source_target_pairs={{0,4},{2,6},{4,0},{6,2},{8,12},{10,14},{12,8},{14,10},{16,20},{18,... | collective-permute-start | bytes 1572872 | tf_op jit(solution)/shard_map/ppermute | solution.py:292
  194.6 14.5 %copy-start.6 = (bf16[4,1,256,256]{3,2,1,0:T(8,128)(2,1)S(1)}, bf16[4,1,256,256]{3,2,1,0:T(8,128)(2,1)}, u32[]{:S(2)}) copy-start(bf16[4,1,256,256]{3,2,1,0:T(8,128)(2,1)} %get-tuple-element.31) | copy-start | bytes 1572868
  194.6 16.9 %copy-start.4 = (bf16[2,4,1,256,256]{4,3,1,2,0:T(8,128)(2,1)S(1)}, bf16[2,4,1,256,256]{4,3,1,2,0:T(8,128)(2,1)}, u32[]{:S(2)}) copy-start(bf16[2,4,1,256,256]{4,3,1,2,0:T(8,128)(2,1)} %copy-done.3) | copy-start | bytes 3145732
  208.4 48.6 %collective-permute-start.10 = (bf16[128,4096]{1,0:T(8,128)(2,1)S(1)}, bf16[128,4096]{1,0:T(8,128)(2,1)}, u32[]{:S(2)}, u32[]{:S(2)}) collective-permute-start(bf16[128,4096]{1,0:T(8,128)(2,1)S(1)} %convolution_convert_fusion), channel_id=1, source_target_pairs={{0,1},{1,0},{2,3},{3,2},{4,5},{5,4},{6,7},{7,6},{8,9},{9,8},{10,11... | collective-permute-start | bytes 3145736 | tf_op jit(solution)/shard_map/ppermute | solution.py:405
  209.3 13.3 %copy-start.1 = (bf16[256,4096]{1,0:T(8,128)(2,1)S(1)}, bf16[256,4096]{1,0:T(8,128)(2,1)}, u32[]{:S(2)}) copy-start(bf16[256,4096]{1,0:T(8,128)(2,1)} %copy-done) | copy-start | bytes 6291460
  209.8 27.0 %collective-permute-start.11 = (bf16[4,1,256,256]{3,2,1,0:T(8,128)(2,1)S(1)}, bf16[4,1,256,256]{3,2,1,0:T(8,128)(2,1)}, u32[]{:S(2)}, u32[]{:S(2)}) collective-permute-start(bf16[4,1,256,256]{3,2,1,0:T(8,128)(2,1)S(1)} %fusion.10), channel_id=1, source_target_pairs={{0,4},{2,6},{4,0},{6,2},{8,12},{10,14},{12,8},{14,10},{16,20},{18,... | collective-permute-start | bytes 1572872 | tf_op jit(solution)/shard_map/ppermute | solution.py:292
  210.6 0.8 copy-start.10
  215.4 23.8 %collective-permute-start.15 = (bf16[1,256,256]{2,1,0:T(8,128)(2,1)}, bf16[1,256,256]{2,1,0:T(8,128)(2,1)}, u32[]{:S(2)}, u32[]{:S(2)}) collective-permute-start(bf16[1,256,256]{2,1,0:T(8,128)(2,1)} %get-tuple-element.48), channel_id=1, source_target_pairs={{0,8},{2,10},{4,12},{6,14},{8,0},{10,2},{12,4},{14,6},{16,24},{18,... | collective-permute-start | bytes 393224 | tf_op jit(solution)/shard_map/ppermute | solution.py:292
  216.7 22.6 %collective-permute-start.17 = (bf16[1,256,256]{2,1,0:T(8,128)(2,1)}, bf16[1,256,256]{2,1,0:T(8,128)(2,1)}, u32[]{:S(2)}, u32[]{:S(2)}) collective-permute-start(bf16[1,256,256]{2,1,0:T(8,128)(2,1)} %get-tuple-element.49), channel_id=1, source_target_pairs={{0,24},{2,26},{4,28},{6,30},{8,16},{10,18},{12,20},{14,22},{16,8},... | collective-permute-start | bytes 393224 | tf_op jit(solution)/shard_map/ppermute | solution.py:292
  217.3 25.5 %collective-permute-start.16 = (bf16[1,256,256]{2,1,0:T(8,128)(2,1)S(1)}, bf16[1,256,256]{2,1,0:T(8,128)(2,1)}, u32[]{:S(2)}, u32[]{:S(2)}) collective-permute-start(bf16[1,256,256]{2,1,0:T(8,128)(2,1)S(1)} %get-tuple-element.50), channel_id=1, source_target_pairs={{0,16},{2,18},{4,20},{6,22},{8,24},{10,26},{12,28},{14,30},{16,0},... | collective-permute-start | bytes 393224 | tf_op jit(solution)/shard_map/ppermute | solution.py:292
  222.6 14.2 %copy-start.9 = (bf16[4,1,256,256]{3,2,1,0:T(8,128)(2,1)S(1)}, bf16[4,1,256,256]{3,2,1,0:T(8,128)(2,1)}, u32[]{:S(2)}) copy-start(bf16[4,1,256,256]{3,2,1,0:T(8,128)(2,1)} %get-tuple-element.38) | copy-start | bytes 1572868
  235.6 7.2 %copy-start.15 = (f32[256,256]{1,0:T(8,128)S(1)}, f32[256,256]{1,0:T(8,128)}, u32[]{:S(2)}) copy-start(f32[256,256]{1,0:T(8,128)} %get-tuple-element.39) | copy-start | bytes 786436
  236.8 14.8 %copy-start.14 = (f32[256,256]{1,0:T(8,128)S(1)}, f32[256,256]{1,0:T(8,128)}, u32[]{:S(2)}) copy-start(f32[256,256]{1,0:T(8,128)} %get-tuple-element.37) | copy-start | bytes 786436
  238.2 8.4 %collective-permute-start.14 = (bf16[1,256,256]{2,1,0:T(8,128)(2,1)S(1)}, bf16[1,256,256]{2,1,0:T(8,128)(2,1)S(1)}, u32[]{:S(2)}, u32[]{:S(2)}) collective-permute-start(bf16[1,256,256]{2,1,0:T(8,128)(2,1)S(1)} %slice_bitcast_fusion.2), channel_id=1, source_target_pairs={{0,24},{2,26},{4,28},{6,30},{8,16},{10,18},{12,20},{14,22},{16,8},... | collective-permute-start | bytes 393224 | tf_op jit(solution)/shard_map/ppermute | solution.py:292
  239.2 7.9 %collective-permute-start.12 = (bf16[1,256,256]{2,1,0:T(8,128)(2,1)S(1)}, bf16[1,256,256]{2,1,0:T(8,128)(2,1)S(1)}, u32[]{:S(2)}, u32[]{:S(2)}) collective-permute-start(bf16[1,256,256]{2,1,0:T(8,128)(2,1)S(1)} %get-tuple-element.46), channel_id=1, source_target_pairs={{0,8},{2,10},{4,12},{6,14},{8,0},{10,2},{12,4},{14,6},{16,24},{18,... | collective-permute-start | bytes 393224 | tf_op jit(solution)/shard_map/ppermute | solution.py:292
  239.3 12.3 %collective-permute-start.13 = (bf16[1,256,256]{2,1,0:T(8,128)(2,1)S(1)}, bf16[1,256,256]{2,1,0:T(8,128)(2,1)S(1)}, u32[]{:S(2)}, u32[]{:S(2)}) collective-permute-start(bf16[1,256,256]{2,1,0:T(8,128)(2,1)S(1)} %get-tuple-element.47), channel_id=1, source_target_pairs={{0,16},{2,18},{4,20},{6,22},{8,24},{10,26},{12,28},{14,30},{16,0},... | collective-permute-start | bytes 393224 | tf_op jit(solution)/shard_map/ppermute | solution.py:292
  253.6 2.8 %copy-start.16 = (bf16[256,128]{1,0:T(8,128)(2,1)S(1)}, bf16[256,128]{1,0:T(8,128)(2,1)}, u32[]{:S(2)}) copy-start(bf16[256,128]{1,0:T(8,128)(2,1)} %get-tuple-element.70) | copy-start | bytes 196612
Sparse Core Ops, SparseCore 0:
  39.5 51.7 all-gather.1
  135.0 73.8 reduce-scatter.1

commit v4 on v1

v4 whole, which is shorter than its diff:
```python
import functools

import jax
import jax.numpy as jnp
from jax import lax
from jax.experimental import pallas as pl
from jax.experimental.pallas import tpu as pltpu
from jax.sharding import PartitionSpec as P

HEAD_DIM = 128
NODE_LEN = 256
CHAIN = 8
LEAVES = 8
PAIR = 2 * HEAD_DIM
COLUMNS = 512

masked_score = -1e30
score_scale = HEAD_DIM ** (-0.5)
log2_e = 1.4426950408889634


def dot(a, b):
    return jnp.dot(a, b, preferred_element_type=jnp.float32)


def dot_nt(a, b):
    return lax.dot_general(a, b, (((1,), (1,)), ((), ())), preferred_element_type=jnp.float32)


def attend(layout, lineage, place, *refs):
    near_count, after_count, chunk_head, by_slot, old_count, head = layout
    q_any, own_any, out_grad_any, weight_any = refs[:4]
    near = refs[4 : 4 + near_count]
    old = refs[4 + near_count : 4 + near_count + old_count]
    rest = refs[4 + near_count + old_count + after_count :]
    part_count = 1 if by_slot else 3
    dq_any, proj_any, own_any_grad = rest[:3]
    parts = rest[3 : 3 + part_count]
    (
        far_ref, own_ref, out_grad, weight, proj, att, s_ref, p_ref, qs, ups, q_t, up_t,
        m_ref, l_ref, acc_ref, own_grad, slots, far_sem, q_sem, sem,
    ) = rest[3 + part_count :]
    depth = place[0]
    me = place[1]
    rows = qs.shape[0]
    heads = rows // NODE_LEN
    half = HEAD_DIM
    width = heads * HEAD_DIM
    factor = score_scale * log2_e
    stride = slots.shape[0] // 4

    def head_rows(h):
        return pl.ds(h * NODE_LEN, NODE_LEN)

    def head_columns(h, first=0):
        return pl.ds(first + h * HEAD_DIM, HEAD_DIM)

    q_copies = [
        pltpu.make_async_copy(
            q_any.at[:, head_columns(h, head * width)], qs.at[head_rows(h), :], q_sem.at[h]
        )
        for h in range(heads)
    ]
    own_copy = pltpu.make_async_copy(
        own_any.at[:, pl.ds(chunk_head * PAIR, PAIR)], own_ref, sem.at[0]
    )
    weight_copy = pltpu.make_async_copy(
        weight_any.at[pl.ds(head * width, width), :], weight, sem.at[1]
    )
    out_grad_copy = pltpu.make_async_copy(out_grad_any, out_grad, sem.at[2])
    for copy in [own_copy] + q_copies:
        copy.start()

    def far_copy(source, index, b):
        return pltpu.make_async_copy(
            source.at[index, :, pl.ds(chunk_head * PAIR, PAIR)], far_ref.at[b], far_sem.at[b]
        )

    def fetch(b, carry):
        if near_count == 1:
            far_copy(near[0], lineage[b], b).start()
            return carry
        away = lineage[b] ^ me
        for kind in range(near_count):

            @pl.when(away % 4 == kind)
            def _():
                far_copy(near[kind], away // 4, b).start()

        return carry

    lax.fori_loop(0, depth, fetch, 0)
    weight_copy.start()
    out_grad_copy.start()
    if head > 0:
        proj_copy = pltpu.make_async_copy(old[1], proj, sem.at[3])
        proj_copy.start()

    def fold_max(s):
        return jnp.maximum(s[:, :half], s[:, half:])

    for copy in [own_copy] + q_copies:
        copy.wait()
    s = dot_nt(qs[...], own_ref[:, :half])
    row = lax.broadcasted_iota(jnp.int32, (rows, NODE_LEN), 0) % NODE_LEN
    col = lax.broadcasted_iota(jnp.int32, (rows, NODE_LEN), 1)
    s = jnp.where(col <= row, s, masked_score)
    s_ref[CHAIN] = s
    m_ref[...] = fold_max(s)

    def score_block(b, carry):
        far_copy(near[0], 0, b).wait()
        s = dot_nt(qs[...], far_ref[b, :, :half])
        s_ref[b] = s
        m_ref[...] = jnp.maximum(m_ref[...], fold_max(s))
        return carry

    lax.fori_loop(0, depth, score_block, 0)
    m_ref[...] = jnp.broadcast_to(jnp.max(m_ref[...], axis=1, keepdims=True), (rows, half))

    def weigh(b, values):
        top = m_ref[...]
        s = s_ref[b]
        p_low = jnp.exp2((s[:, :half] - top) * factor)
        p_high = jnp.exp2((s[:, half:] - top) * factor)
        p = jnp.concatenate([p_low, p_high], axis=1).astype(jnp.bfloat16)
        p_ref[b] = p
        return p_low + p_high, dot(p, values)

    part_sum, part = weigh(CHAIN, own_ref[:, half:])
    l_ref[...] = part_sum
    acc_ref[...] = part

    def forward_block(b, carry):
        part_sum, part = weigh(b, far_ref[b, :, half:])
        l_ref[...] += part_sum
        acc_ref[...] += part
        return carry

    lax.fori_loop(0, depth, forward_block, 0)
    inverse = 1.0 / jnp.broadcast_to(jnp.sum(l_ref[...], axis=1, keepdims=True), (rows, half))
    l_ref[...] = inverse
    attended = (acc_ref[...] * inverse).astype(jnp.bfloat16)
    for h in range(heads):
        att[:, head_columns(h)] = attended[h * NODE_LEN : (h + 1) * NODE_LEN, :]

    weight_copy.wait()
    out_grad_copy.wait()
    for h in range(0, heads, 2):
        count = min(2, heads - h)
        two = dot_nt(out_grad[...], weight[h * HEAD_DIM : (h + count) * HEAD_DIM, :])
        for i in range(count):
            ups[head_rows(h + i), :] = two[:, i * HEAD_DIM : (i + 1) * HEAD_DIM].astype(jnp.bfloat16)
    if head > 0:
        proj_copy.wait()

    def project(n, carry):
        columns = pl.ds(pl.multiple_of(n * COLUMNS, COLUMNS), COLUMNS)
        share = dot(att[...], weight[:, columns])
        proj[:, columns] = share if head == 0 else proj[:, columns] + share
        return carry

    lax.fori_loop(0, weight.shape[1] // COLUMNS, project, 0)
    proj_out = pltpu.make_async_copy(proj, proj_any, sem.at[4])
    proj_out.start()

    upstream = ups[...].astype(jnp.float32)
    corr_ref = m_ref
    corr_ref[...] = jnp.broadcast_to(
        jnp.sum(upstream * attended.astype(jnp.float32), axis=1, keepdims=True), (rows, half)
    )
    q_t[...] = (qs[...].astype(jnp.float32) * (inverse * score_scale)).astype(jnp.bfloat16).T
    up_t[...] = (upstream * inverse).astype(jnp.bfloat16).T

    def backward(b, keys, values):
        corr = corr_ref[...]
        p = p_ref[b]
        d_prob = dot_nt(ups[...], values)
        centred = jnp.concatenate([d_prob[:, :half] - corr, d_prob[:, half:] - corr], axis=1)
        d_score = (p.astype(jnp.float32) * centred).astype(jnp.bfloat16)
        grad = jnp.concatenate([dot(q_t[...], d_score), dot(up_t[...], p)], axis=0)
        return dot(d_score, keys), grad

    slots[...] = jnp.zeros_like(slots)
    part, grad = backward(CHAIN, own_ref[:, :half], own_ref[:, half:])
    acc_ref[...] = part
    own_grad[...] = grad.T
    own_out = pltpu.make_async_copy(own_grad, own_any_grad, sem.at[3])
    own_out.start()

    def backward_block(b, carry):
        part, grad = backward(b, far_ref[b, :, :half], far_ref[b, :, half:])
        acc_ref[...] += part
        block = grad.astype(jnp.bfloat16).T
        if by_slot:
            slots[lineage[b]] = block
        else:
            away = lineage[b] ^ me
            kind = away % 4
            slots[away // 4 + stride * jnp.where(kind == 0, 0, jnp.where(kind == 2, 1, 2 + kind // 2))] = block
        return carry

    lax.fori_loop(0, depth, backward_block, 0)
    if by_slot:
        part_copies = [pltpu.make_async_copy(slots, parts[0].at[:, head], sem.at[6])]
    else:
        part_copies = [
            pltpu.make_async_copy(slots.at[pl.ds(stride * i, stride)], target, sem.at[6 + i])
            for i, target in enumerate([parts[0], parts[1], parts[2].at[0], parts[2].at[1]])
        ]
    for copy in part_copies:
        copy.start()
    query_grad = (acc_ref[...] * (l_ref[...] * score_scale)).astype(jnp.bfloat16)
    for h in range(heads):
        att[:, head_columns(h)] = query_grad[h * NODE_LEN : (h + 1) * NODE_LEN, :]
    dq_out = pltpu.make_async_copy(att, dq_any.at[:, pl.ds(head * width, width)], sem.at[5])
    dq_out.start()
    for copy in part_copies + [own_out]:
        copy.wait()
    proj_out.wait()
    dq_out.wait()


def attention(
    head, chunk_head, head_group, nodes, slot_heads,
    lineage, place, query_rows, own, out_grad, weight, near, old, after,
):
    bf16, f32 = jnp.bfloat16, jnp.float32
    stride = nodes // 4
    width = head_group * HEAD_DIM
    rows = head_group * NODE_LEN
    d_out = weight.shape[1]
    block = (NODE_LEN, PAIR)
    anywhere = pl.BlockSpec(memory_space=pl.ANY)
    in_smem = pl.BlockSpec(memory_space=pltpu.SMEM)
    if slot_heads:
        parts = [jax.ShapeDtypeStruct((nodes, slot_heads) + block, bf16)]
    else:
        parts = [
            jax.ShapeDtypeStruct((stride,) + block, bf16),
            jax.ShapeDtypeStruct((stride,) + block, bf16),
            jax.ShapeDtypeStruct((2, stride) + block, bf16),
        ]
    first_old = 6 + len(near)
    aliases = {first_old + i: i if i < 2 else 3 for i in range(len(old))}
    layout = (len(near), len(after), chunk_head, bool(slot_heads), len(old), head)
    blocks = (CHAIN + 1) * head_group
    return pl.pallas_call(
        functools.partial(attend, layout),
        in_specs=[in_smem, in_smem] + [anywhere] * (4 + len(near) + len(old) + len(after)),
        out_specs=[anywhere] * (3 + len(parts)),
        out_shape=[
            jax.ShapeDtypeStruct(query_rows.shape, bf16),
            jax.ShapeDtypeStruct((NODE_LEN, d_out), f32),
            jax.ShapeDtypeStruct(block, f32),
        ]
        + parts,
        input_output_aliases=aliases,
        scratch_shapes=[
            pltpu.VMEM((CHAIN,) + block, bf16),
            pltpu.VMEM(block, bf16),
            pltpu.VMEM((NODE_LEN, d_out), bf16),
            pltpu.VMEM((width, d_out), bf16),
            pltpu.VMEM((NODE_LEN, d_out), f32),
            pltpu.VMEM((NODE_LEN, width), bf16),
            pltpu.VMEM((CHAIN + 1, rows, NODE_LEN), f32),
            pltpu.VMEM((CHAIN + 1, rows, NODE_LEN), bf16),
            pltpu.VMEM((rows, HEAD_DIM), bf16),
            pltpu.VMEM((rows, HEAD_DIM), bf16),
            pltpu.VMEM((HEAD_DIM, rows), bf16),
            pltpu.VMEM((HEAD_DIM, rows), bf16),
            pltpu.VMEM((rows, HEAD_DIM), f32),
            pltpu.VMEM((rows, HEAD_DIM), f32),
            pltpu.VMEM((rows, HEAD_DIM), f32),
            pltpu.VMEM(block, f32),
            pltpu.VMEM((nodes,) + block, bf16),
            pltpu.SemaphoreType.DMA((CHAIN,)),
            pltpu.SemaphoreType.DMA((head_group,)),
            pltpu.SemaphoreType.DMA((10,)),
        ],
        compiler_params=pltpu.CompilerParams(vmem_limit_bytes=63 * 1024 * 1024),
        cost_estimate=pl.CostEstimate(
            flops=2 * blocks * NODE_LEN * NODE_LEN * HEAD_DIM,
            bytes_accessed=4 * 1024 * 1024,
            transcendentals=0,
        ),
    )(lineage, place, query_rows, own, out_grad, weight, *near, *old, *after)


def zero_of(value):
    return jnp.minimum(jnp.abs(value.astype(jnp.float32)), 0.0)


def swap(block, mask, nodes):
    return lax.ppermute(block, "node", [(i, i ^ mask) for i in range(nodes)])


def gather_near(own, nodes, zero):
    stride = nodes // 4
    line = jnp.stack([own] + [swap(own, 4 * d, nodes) for d in range(1, stride)])
    line = line + zero.astype(line.dtype)
    cross = swap(line, 2, nodes)
    return line, swap(line, 1, nodes), cross, swap(cross, 1, nodes)


def add_level_1(keep, cross, came, *refs):
    cross_sum, keep_sum = refs[-2:]
    cross_sum[...] = (cross[...].astype(jnp.float32) + came[1].astype(jnp.float32)).astype(
        jnp.bfloat16
    )
    keep_sum[...] = keep[...].astype(jnp.float32) + came[0].astype(jnp.float32)


def add_level_2(keep, came, *refs):
    keep_sum, *sent = refs[1:]
    total = keep[0] + came[0].astype(jnp.float32)
    for d in range(len(sent) + 1):

        @pl.when(pl.program_id(0) == d)
        def _():
            if d == 0:
                keep_sum[...] = total
            else:
                sent[d - 1][...] = total.astype(jnp.bfloat16)


def add_call(kernel, stride, in_specs, out_specs, out_shape, operands):
    return pl.pallas_call(
        kernel,
        grid=(stride,),
        in_specs=in_specs + [pl.BlockSpec(memory_space=pl.ANY)],
        out_specs=out_specs,
        out_shape=out_shape,
        compiler_params=pltpu.CompilerParams(vmem_limit_bytes=16 * 1024 * 1024),
        cost_estimate=pl.CostEstimate(flops=2**20, bytes_accessed=2**22, transcendentals=0),
    )(*operands)


def scatter_sum(keep, cross, away, own_part, nodes):
    bf16, f32 = jnp.bfloat16, jnp.float32
    stride = nodes // 4
    came = swap(away, 1, nodes)
    after = yield [away]
    block = keep.shape[1:]
    one = pl.BlockSpec((1,) + block, lambda d: (d, 0, 0))
    two = pl.BlockSpec((2, 1) + block, lambda d: (0, d, 0, 0))
    whole = pl.BlockSpec(block, lambda d: (0, 0))
    cross, keep = add_call(
        add_level_1,
        stride,
        [one, one, two],
        [one, one],
        [jax.ShapeDtypeStruct(cross.shape, bf16), jax.ShapeDtypeStruct(keep.shape, f32)],
        [keep, cross, came, after],
    )
    came = swap(cross, 2, nodes)
    after = yield [cross]
    keep, *sent = add_call(
        add_level_2,
        stride,
        [one, one],
        [whole] * stride,
        [jax.ShapeDtypeStruct(block, f32)] + [jax.ShapeDtypeStruct(block, bf16)] * (stride - 1),
        [keep, came, after],
    )
    came = [swap(part, 4 * (d + 1), nodes) for d, part in enumerate(sent)]
    yield sent
    total = own_part + keep
    for part in came:
        total = total + part.astype(f32)
    return total.astype(bf16)


def other_rows(block, tp):
    if tp != 2:
        whole = lax.all_gather(block, "tp", axis=0, tiled=True)
        return whole, whole
    me = lax.axis_index("tp")
    came = lax.ppermute(block, "tp", [(0, 1), (1, 0)])
    return (
        jnp.where(
            me == 0, jnp.concatenate([block, came], axis=0), jnp.concatenate([came, block], axis=0)
        ),
        came,
    )


def local(tp, nodes, query_rows, key_rows, value_rows, out_weight, out_grad, owner_slot):
    bf16, f32 = jnp.bfloat16, jnp.float32
    node_count = owner_slot.shape[0]
    tree_nodes = CHAIN + LEAVES
    kv_width = key_rows.shape[1]
    kv_heads = kv_width // HEAD_DIM
    head_group = query_rows.shape[1] // kv_width
    my_slot = lax.axis_index("node")
    numbers = jnp.arange(node_count, dtype=jnp.int32)
    tree_node = jnp.sum(jnp.where(owner_slot == my_slot, numbers, 0))
    depth = jnp.minimum(tree_node % tree_nodes, CHAIN)
    place = jnp.stack([depth, my_slot]).astype(jnp.int32)
    lineage = lax.dynamic_slice_in_dim(owner_slot, tree_node // tree_nodes * tree_nodes, CHAIN)

    out_grad_rows, came = other_rows(out_grad, tp)
    alone = min(2, kv_heads)
    chunks = [(k, 1) for k in range(alone)]
    if kv_heads > alone:
        chunks.append((alone, kv_heads - alone))
    own, near = {}, {}
    zero = zero_of(came[0, 0])
    earlier = None
    for first, heads in chunks:
        packed = []
        for k in range(first, first + heads):
            columns = slice(k * HEAD_DIM, (k + 1) * HEAD_DIM)
            packed += [key_rows[:, columns], value_rows[:, columns]]
        packed = jnp.concatenate(packed, axis=1)
        later = packed if earlier is None else packed + zero_of(earlier[0, 0, 0]).astype(bf16)
        if heads == 1:
            blocks = gather_near(later, nodes, zero)
            earlier, zero = blocks[0], zero_of(blocks[2][0, 0, 0])
        else:
            blocks = [lax.all_gather(later, "node", axis=0, tiled=False)]
        for i in range(heads):
            own[first + i], near[first + i] = (packed, i), blocks

    offloaded = max(0, kv_heads - 2)
    old, sums, own_parts = [], [], []
    sent = [earlier] if kv_heads > 1 else []
    for k in range(kv_heads):
        by_slot = k < offloaded
        dq, proj, own_part, *parts = attention(
            k, own[k][1], head_group, nodes, offloaded if by_slot else 0,
            lineage, place, query_rows, own[k][0], out_grad_rows, out_weight, near[k], old, sent,
        )
        old = [dq, proj] + (parts if k + 1 < offloaded else [])
        moved = [part for chain in sums for part in chain.send(own_part)]
        sent = moved + [own_part]
        if by_slot:
            own_parts.append(own_part)
            if k + 1 == offloaded:
                came = lax.psum_scatter(parts[0], "node", scatter_dimension=0, tiled=False)
        else:
            sums.append(scatter_sum(*parts, own_part, nodes))
            next(sums[-1])

    rows = proj.shape[0] // tp
    if tp == 2:
        me = lax.axis_index("tp")
        away = lax.dynamic_slice_in_dim(proj, (1 - me) * rows, rows, 0)
        for part in moved:
            away = away + zero_of(part[0, 0, 0])
        away = away.astype(bf16)
        here = lax.dynamic_slice_in_dim(proj, me * rows, rows, 0)
        projected = here + lax.ppermute(away, "tp", [(0, 1), (1, 0)]).astype(f32)
        projected = projected.astype(bf16)
    else:
        projected = lax.psum_scatter(proj.astype(bf16), "tp", scatter_dimension=0, tiled=True)
    moved = moved + [own_part]
    totals, steps = {}, []
    while len(totals) < len(sums):
        for n, chain in enumerate(sums):
            if n not in totals:
                try:
                    moved = chain.send(moved[0])
                    steps.append(moved[0])
                except StopIteration as end:
                    totals[n] = end.value
    totals = [totals[n] for n in range(len(sums))]
    if offloaded:
        zero = zero_of(steps[1].reshape(-1)[0])
        came = came.astype(f32) + zero
        totals = [(own_parts[k] + came[k]).astype(bf16) for k in range(offloaded)] + totals
    return (
        projected,
        dq,
        jnp.concatenate([total[:, :HEAD_DIM] for total in totals], axis=1),
        jnp.concatenate([total[:, HEAD_DIM:] for total in totals], axis=1),
    )


def solution(mesh):
    in_specs = (
        P("node", "tp"),
        P("node", "tp"),
        P("node", "tp"),
        P("tp", None),
        P(("node", "tp"), None),
        P(),
    )
    out_specs = (P(("node", "tp"), None), P("node", "tp"), P("node", "tp"), P("node", "tp"))
    return jax.shard_map(
        functools.partial(local, mesh.shape["tp"], mesh.shape["node"]),
        mesh=mesh, in_specs=in_specs, out_specs=out_specs, check_vma=False,
    )
```

time: 451 us -> 250 us (0.55)
  waiting for transfers between devices: 330 us -> 56.7 us
  Pallas kernels: 42.7 us -> 117 us
  matrix products: 33.1 us -> 0 us
  starting transfers between devices: 4.87 us -> 31.1 us
    reduce_scatter x4 -> x1, waiting for transfers between devices: 196 us -> 0.02 us  [local(): came = lax.psum_scatter(parts[0], 'node', scatter_dimension=0, tiled=False)]
    all_gather x4 -> x1, waiting for transfers between devices: 92.8 us -> 0.01 us  [local(): blocks = [lax.all_gather(later, 'node', axis=0, tiled=False)]]
    pallas_call x4 -> x8, Pallas kernels: 42.7 us -> 117 us  [the longest x4 113 us: attention(): pl.pallas_call(functools.partial(attend, layout), in_specs=[in_smem, in_s...]
    dot_general x2 -> x0, matrix products: 33.1 us -> none  [the longest x1 17 us: dot(): return jnp.dot(a, b, preferred_element_type=jnp.float32)]
    ppermute x2 -> x24, starting transfers between devices: 4.35 us -> 31 us  [the longest x22 26.5 us: swap(): return lax.ppermute(block, 'node', [(i, i ^ mask) for i in range(nodes)])]
    ppermute x2 -> x24, waiting for transfers between devices: 40.8 us -> 56.7 us  [the longest x22 38.8 us: swap(): return lax.ppermute(block, 'node', [(i, i ^ mask) for i in range(nodes)])]
  transfers between devices with their start and end apart: 10 -> 26, of which waited for: 10 -> 7; matrix products, arithmetic and copies ran while one was open for 10% -> 7% of each run, Pallas kernels for 9% -> 47%
where the time goes in v4:
time: 250 us; the launch traced here: 249 us
  Pallas kernels  117 us (47%)
  waiting for transfers between devices  56.7 us (23%)
  starting transfers between devices  31.1 us (12%)
  between operations  21 us (8%)
  other arithmetic  16.2 us (6%)
  local copies, waits for them, and re-layouts  7.58 us (3%)
    pallas_call x4, Pallas kernels, attention(): pl.pallas_call(functools.partial(attend, layout), in_specs=[in_smem, in_s...  113 us
    ppermute x22, waiting for transfers between devices, swap(): return lax.ppermute(block, 'node', [(i, i ^ mask) for i in range(nodes)])  38.8 us
    ppermute x22, starting transfers between devices, swap(): return lax.ppermute(block, 'node', [(i, i ^ mask) for i in range(nodes)])  26.5 us
    ppermute x1, waiting for transfers between devices, other_rows(): came = lax.ppermute(block, 'tp', [(0, 1), (1, 0)])  17.9 us
  transfers between devices with their start and end apart: 26, of which 7 were waited for; matrix products, arithmetic and copies ran while one was open for 7% of the time, Pallas kernels for 47%

profile of v4, /device:TPU:0, one launch (start us, length us, event | category | flops | bytes accessed | tf_op | source)
XLA Modules:
  0.0 249.1 jit_solution(17421021786796182448)
XLA Ops:
  7.2 3.0 %collective-permute-start = (bf16[128,4096]{1,0:T(8,128)(2,1)}, bf16[128,4096]{1,0:T(8,128)(2,1)S(1)}, u32[]{:S(2)}, u32[]{:S(2)}) collective-permute-start(bf16[128,4096]{1,0:T(8,128)(2,1)} %param.10), channel_id=1, source_target_pairs={{0,1},{1,0},{2,3},{3,2},{4,5},{5,4},{6,7},{7,6},{8,9},{9,8},{10,11... | collective-permute-start | bytes 3145736 | tf_op jit(solution)/shard_map/ppermute | solution.py:379
  10.2 1.2 slice_bitcast_fusion.2
  11.5 2.7 %collective-permute-start.2 = (bf16[256,256]{1,0:T(8,128)(2,1)S(1)}, bf16[256,256]{1,0:T(8,128)(2,1)S(1)}, u32[]{:S(2)}, u32[]{:S(2)}) collective-permute-start(bf16[256,256]{1,0:T(8,128)(2,1)S(1)} %get-tuple-element.95.refs_1_), channel_id=1, source_target_pairs={{0,16},{2,18},{4,20},{6,22},{8,24},{10,26},{12,28},{14,30},{16,0},... | collective-permute-start | bytes 393224 | tf_op jit(solution)/shard_map/ppermute | solution.py:295
  14.2 1.3 collective-permute-start.3
  15.5 0.2 collective-permute-start.1
  15.7 17.9 %collective-permute-done = bf16[128,4096]{1,0:T(8,128)(2,1)S(1)} collective-permute-done((bf16[128,4096]{1,0:T(8,128)(2,1)}, bf16[128,4096]{1,0:T(8,128)(2,1)S(1)}, u32[]{:S(2)}, u32[]{:S(2)}) %collective-permute-start) | collective-permute-done | bytes 1048608 | tf_op jit(solution)/shard_map/ppermute | solution.py:379
  33.6 0.5 slice.98
  34.9 0.1 maximum_add_fusion.refs_4_
  35.0 1.8 collective-permute-start.7
  36.7 0.5 slice.99
  37.9 0.7 pad_maximum_fusion.4
  38.6 1.6 collective-permute-start.4
  40.2 2.6 %collective-permute-start.5 = (bf16[256,256]{1,0:T(8,128)(2,1)S(1)}, bf16[256,256]{1,0:T(8,128)(2,1)S(1)}, u32[]{:S(2)}, u32[]{:S(2)}) collective-permute-start(bf16[256,256]{1,0:T(8,128)(2,1)S(1)} %get-tuple-element.93), channel_id=1, source_target_pairs={{0,16},{2,18},{4,20},{6,22},{8,24},{10,26},{12,28},{14,30},{16,0},... | collective-permute-start | bytes 393224 | tf_op jit(solution)/shard_map/ppermute | solution.py:295
  42.8 0.2 collective-permute-start.6
  43.0 5.1 %collective-permute-done.7.refs_6_ = bf16[4,256,256]{2,1,0:T(8,128)(2,1)S(1)} collective-permute-done((bf16[4,256,256]{2,1,0:T(8,128)(2,1)S(1)}, bf16[4,256,256]{2,1,0:T(8,128)(2,1)S(1)}, u32[]{:S(2)}, u32[]{:S(2)}) %collective-permute-start.7) | collective-permute-done | bytes 524320 | tf_op jit(solution)/shard_map/ppermute | solution.py:295
  48.1 0.5 slice.100
  49.3 2.6 %collective-permute-done.5 = bf16[256,256]{1,0:T(8,128)(2,1)S(1)} collective-permute-done((bf16[256,256]{1,0:T(8,128)(2,1)S(1)}, bf16[256,256]{1,0:T(8,128)(2,1)S(1)}, u32[]{:S(2)}, u32[]{:S(2)}) %collective-permute-start.5) | collective-permute-done | bytes 131104 | tf_op jit(solution)/shard_map/ppermute | solution.py:295
  51.9 0.1 maximum_add_fusion.1.refs_8_.refs_4_
  52.0 0.6 slice.101
  53.2 0.8 maximum_add_fusion.2
  54.1 0.6 collective-permute-start.9
  54.7 0.7 fusion.4
  57.3 0.1 collective-permute-start.11
  57.4 0.5 collective-permute-start.12
  57.8 0.6 pad_add_fusion.place
  59.1 0.6 dynamic_slice.9.lineage
  59.7 0.1 collective-permute-start.8
  59.8 4.3 %collective-permute-done.9.refs_6_ = bf16[4,256,256]{2,1,0:T(8,128)(2,1)} collective-permute-done((bf16[4,256,256]{2,1,0:T(8,128)(2,1)S(1)}, bf16[4,256,256]{2,1,0:T(8,128)(2,1)}, u32[]{:S(2)}, u32[]{:S(2)}) %collective-permute-start.9) | collective-permute-done | bytes 524320 | tf_op jit(solution)/shard_map/ppermute | solution.py:295
  64.1 3.7 %maximum_select_fusion.refs_2_ = bf16[256,4096]{1,0:T(8,128)(2,1)} fusion(bf16[128,4096]{1,0:T(8,128)(2,1)} %copy-done.17, bf16[128,4096]{1,0:T(8,128)(2,1)S(1)} %copy-done.16, pred[]{:T(512)S(6)} %eq.13), kind=kLoop, calls=%fused_computation | loop fusion | flops 9437184 | bytes 4194305 | tf_op jit(solution)/shard_map/jit(_where)/select_n | solution.py:381
  67.8 28.3 %shard_map.93 = (bf16[256,4096]{1,0:T(8,128)(2,1)}, f32[256,4096]{1,0:T(8,128)}, f32[256,256]{1,0:T(8,128)}, bf16[16,2,256,256]{3,2,1,0:T(8,128)(2,1)}) custom-call(s32[8]{0:T(128)} %dynamic_slice.9.lineage, s32[2]{0:T(128)} %pad_add_fusion.place, bf16[256,4096]{1,0:T(8,128)(2,1)} %refs_0_.7, bf16[256,256]{1,0:T(8,128)(2,1)} %copy-done.19, ...), custom_call_target="tpu_custom_call" | custom-call | flops 1207959552 | bytes 4194304 | tf_op jit(solution)/shard_map/pallas_call | solution.py:248
  96.1 28.5 %shard_map.94 = (bf16[256,4096]{1,0:T(8,128)(2,1)}, f32[256,4096]{1,0:T(8,128)}, f32[256,256]{1,0:T(8,128)}, bf16[16,2,256,256]{3,2,1,0:T(8,128)(2,1)}) custom-call(s32[8]{0:T(128)} %dynamic_slice.9.lineage, s32[2]{0:T(128)} %pad_add_fusion.place, bf16[256,4096]{1,0:T(8,128)(2,1)} %refs_0_.7, ...), custom_call_target="tpu_custom_call", output_to_operand_aliasing={{0}: (10, {}), {1}: (11, {}), {3}: (12, {})} | custom-call | flops 1207959552 | bytes 4194304 | tf_op jit(solution)/shard_map/pallas_call | solution.py:248
  124.6 0.7 pad_maximum_fusion.refs_1_
  125.4 28.3 %shard_map.95 = (bf16[256,4096]{1,0:T(8,128)(2,1)}, f32[256,4096]{1,0:T(8,128)}, f32[256,256]{1,0:T(8,128)}, bf16[4,256,256]{2,1,0:T(8,128)(2,1)}, bf16[4,256,25...) custom-call(s32[8]{0:T(128)} %dynamic_slice.9.lineage, ...), custom_call_target="tpu_custom_call", output_to_operand_aliasing={{0}: (7, {}), {1}: (8, {})} | custom-call | flops 1207959552 | bytes 4194304 | tf_op jit(solution)/shard_map/pallas_call | solution.py:248
  153.7 0.6 collective-permute-start.13
  154.3 28.4 %shard_map.96 = (bf16[256,4096]{1,0:T(8,128)(2,1)}, f32[256,4096]{1,0:T(8,128)}, f32[256,256]{1,0:T(8,128)}, bf16[4,256,256]{2,1,0:T(8,128)(2,1)}, bf16[4,256,25...) custom-call(s32[8]{0:T(128)} %dynamic_slice.9.lineage, ...), custom_call_target="tpu_custom_call", output_to_operand_aliasing={{0}: (7, {}), {1}: (8, {})} | custom-call | flops 1207959552 | bytes 4194304 | tf_op jit(solution)/shard_map/pallas_call | solution.py:248
  182.7 0.1 collective-permute-start.15
  182.8 0.9 copy-done
  183.8 1.0 copy-done.5
  184.8 2.1 shard_map.97
  186.9 0.9 collective-permute-start.16
  187.9 0.5 slice.86
  189.1 2.8 %add_convert_fusion.1 = bf16[128,4096]{1,0:T(8,128)(2,1)} fusion(f32[256,4096]{1,0:T(8,128)} %get-tuple-element.46, s32[]{:T(128)S(6)} %select_n.39, f32[]{:T(128)} %bitcast.19), kind=kLoop, calls=%fused_computation.2 | loop fusion | flops 1048576 | bytes 3145736 | tf_op jit(solution)/shard_map/convert_element_type | solution.py:451
  191.9 1.5 collective-permute-start.14
  193.4 10.5 %collective-permute-done.16.came = bf16[4,256,256]{2,1,0:T(8,128)(2,1)S(1)} collective-permute-done((bf16[4,256,256]{2,1,0:T(8,128)(2,1)S(1)}, bf16[4,256,256]{2,1,0:T(8,128)(2,1)S(1)}, u32[]{:S(2)}, u32[]{:S(2)}) %collective-permute-start.16) | collective-permute-done | bytes 524320 | tf_op jit(solution)/shard_map/ppermute | solution.py:295
  203.9 0.2 shard_map.98
  204.1 4.6 %collective-permute-start.17 = (bf16[256,256]{1,0:T(8,128)(2,1)S(1)}, bf16[256,256]{1,0:T(8,128)(2,1)}, u32[]{:S(2)}, u32[]{:S(2)}) collective-permute-start(bf16[256,256]{1,0:T(8,128)(2,1)S(1)} %get-tuple-element.58.refs_0_), channel_id=1, source_target_pairs={{0,8},{2,10},{4,12},{6,14},{8,0},{10,2},{12,4},{14,6},{16,24},{18,... | collective-permute-start | bytes 393224 | tf_op jit(solution)/shard_map/ppermute | solution.py:295
  208.7 0.4 shard_map.99
  209.2 0.4 collective-permute-start.20
  209.5 0.4 copy.17
  210.0 0.6 slice.102
  211.2 1.0 convert_add_fusion
  212.2 0.1 fusion.3
  212.3 0.4 collective-permute-start.18
  212.8 2.0 collective-permute-start.19
  214.8 8.8 %collective-permute-done.18 = bf16[256,256]{1,0:T(8,128)(2,1)S(1)} collective-permute-done((bf16[256,256]{1,0:T(8,128)(2,1)S(1)}, bf16[256,256]{1,0:T(8,128)(2,1)S(1)}, u32[]{:S(2)}, u32[]{:S(2)}) %collective-permute-start.18) | collective-permute-done | bytes 131104 | tf_op jit(solution)/shard_map/ppermute | solution.py:295
  223.6 1.0 add_convert_fusion.3
  224.6 0.2 shard_map.100
  224.9 3.3 %collective-permute-start.21 = (bf16[256,256]{1,0:T(8,128)(2,1)S(1)}, bf16[256,256]{1,0:T(8,128)(2,1)S(1)}, u32[]{:S(2)}, u32[]{:S(2)}) collective-permute-start(bf16[256,256]{1,0:T(8,128)(2,1)S(1)} %get-tuple-element.65), channel_id=1, source_target_pairs={{0,8},{2,10},{4,12},{6,14},{8,0},{10,2},{12,4},{14,6},{16,24},{18,... | collective-permute-start | bytes 393224 | tf_op jit(solution)/shard_map/ppermute | solution.py:295
  228.2 2.4 collective-permute-start.23
  230.7 2.5 add_convert_fusion
  233.1 7.6 %collective-permute-done.22 = bf16[256,256]{1,0:T(8,128)(2,1)S(1)} collective-permute-done((bf16[256,256]{1,0:T(8,128)(2,1)S(1)}, bf16[256,256]{1,0:T(8,128)(2,1)S(1)}, u32[]{:S(2)}, u32[]{:S(2)}) %collective-permute-start.22) | collective-permute-done | bytes 131104 | tf_op jit(solution)/shard_map/ppermute | solution.py:295
  240.7 0.1 add_convert_fusion.2
  240.8 0.7 pad_maximum_fusion.2
  241.6 0.7 pad_maximum_fusion.1
  (71 shorter events, 0.4 us)
Async XLA Ops:
  7.2 118.2 %all-gather.2.cloned.1.call-start = ((), (), s32[]{:S(2)}) async-start(), calls=%async_computation.1 | async-start | bytes 4456448 | tf_op jit(solution)/shard_map/all_gather | solution.py:421
  7.2 26.4 %collective-permute-start = (bf16[128,4096]{1,0:T(8,128)(2,1)}, bf16[128,4096]{1,0:T(8,128)(2,1)S(1)}, u32[]{:S(2)}, u32[]{:S(2)}) collective-permute-start(bf16[128,4096]{1,0:T(8,128)(2,1)} %param.10), channel_id=1, source_target_pairs={{0,1},{1,0},{2,3},{3,2},{4,5},{5,4},{6,7},{7,6},{8,9},{9,8},{10,11... | collective-permute-start | bytes 3145736 | tf_op jit(solution)/shard_map/ppermute | solution.py:379
  11.4 43.3 %copy-start.20 = (s32[16]{0:T(128)S(1)}, s32[16]{0:T(128)}, u32[]{:S(2)}) copy-start(s32[16]{0:T(128)} %param.11) | copy-start | bytes 196
  11.5 52.6 %copy-start.16 = (bf16[128,4096]{1,0:T(8,128)(2,1)S(1)}, bf16[128,4096]{1,0:T(8,128)(2,1)}, u32[]{:S(2)}) copy-start(bf16[128,4096]{1,0:T(8,128)(2,1)} %param.10) | copy-start | bytes 3145732
  11.5 56.3 %copy-start.19 = (bf16[256,256]{1,0:T(8,128)(2,1)}, bf16[256,256]{1,0:T(8,128)(2,1)S(1)}, u32[]{:S(2)}) copy-start(bf16[256,256]{1,0:T(8,128)(2,1)S(1)} %get-tuple-element.95.refs_1_) | copy-start | bytes 393220
  11.5 23.3 %collective-permute-start.2 = (bf16[256,256]{1,0:T(8,128)(2,1)S(1)}, bf16[256,256]{1,0:T(8,128)(2,1)S(1)}, u32[]{:S(2)}, u32[]{:S(2)}) collective-permute-start(bf16[256,256]{1,0:T(8,128)(2,1)S(1)} %get-tuple-element.95.refs_1_), channel_id=1, source_target_pairs={{0,16},{2,18},{4,20},{6,22},{8,24},{10,26},{12,28},{14,30},{16,0},... | collective-permute-start | bytes 393224 | tf_op jit(solution)/shard_map/ppermute | solution.py:295
  14.2 20.7 %collective-permute-start.3 = (bf16[256,256]{1,0:T(8,128)(2,1)S(1)}, bf16[256,256]{1,0:T(8,128)(2,1)S(1)}, u32[]{:S(2)}, u32[]{:S(2)}) collective-permute-start(bf16[256,256]{1,0:T(8,128)(2,1)S(1)} %get-tuple-element.95.refs_1_), channel_id=1, source_target_pairs={{0,24},{2,26},{4,28},{6,30},{8,16},{10,18},{12,20},{14,22},{16,8},... | collective-permute-start | bytes 393224 | tf_op jit(solution)/shard_map/ppermute | solution.py:295
  15.5 19.3 %collective-permute-start.1 = (bf16[256,256]{1,0:T(8,128)(2,1)S(1)}, bf16[256,256]{1,0:T(8,128)(2,1)S(1)}, u32[]{:S(2)}, u32[]{:S(2)}) collective-permute-start(bf16[256,256]{1,0:T(8,128)(2,1)S(1)} %get-tuple-element.95.refs_1_), channel_id=1, source_target_pairs={{0,8},{2,10},{4,12},{6,14},{8,0},{10,2},{12,4},{14,6},{16,24},{18,... | collective-permute-start | bytes 393224 | tf_op jit(solution)/shard_map/ppermute | solution.py:295
  33.6 18.3 %copy-start.17 = (bf16[128,4096]{1,0:T(8,128)(2,1)}, bf16[128,4096]{1,0:T(8,128)(2,1)S(1)}, u32[]{:S(2)}) copy-start(bf16[128,4096]{1,0:T(8,128)(2,1)S(1)} %collective-permute-done) | copy-start | bytes 3145732
  34.9 32.8 %copy-start.12 = (bf16[4,256,256]{2,1,0:T(8,128)(2,1)}, bf16[4,256,256]{2,1,0:T(8,128)(2,1)S(1)}, u32[]{:S(2)}) copy-start(bf16[4,256,256]{2,1,0:T(8,128)(2,1)S(1)} %maximum_add_fusion.refs_4_) | copy-start | bytes 1572868
  35.0 13.2 %collective-permute-start.7 = (bf16[4,256,256]{2,1,0:T(8,128)(2,1)S(1)}, bf16[4,256,256]{2,1,0:T(8,128)(2,1)S(1)}, u32[]{:S(2)}, u32[]{:S(2)}) collective-permute-start(bf16[4,256,256]{2,1,0:T(8,128)(2,1)S(1)} %maximum_add_fusion.refs_4_), channel_id=1, source_target_pairs={{0,4},{2,6},{4,0},{6,2},{8,12},{10,14},{12,8},{14,10},{16,20},{18,... | collective-permute-start | bytes 1572872 | tf_op jit(solution)/shard_map/ppermute | solution.py:295
  38.6 10.7 %collective-permute-start.4 = (bf16[256,256]{1,0:T(8,128)(2,1)S(1)}, bf16[256,256]{1,0:T(8,128)(2,1)S(1)}, u32[]{:S(2)}, u32[]{:S(2)}) collective-permute-start(bf16[256,256]{1,0:T(8,128)(2,1)S(1)} %get-tuple-element.93), channel_id=1, source_target_pairs={{0,8},{2,10},{4,12},{6,14},{8,0},{10,2},{12,4},{14,6},{16,24},{18,... | collective-permute-start | bytes 393224 | tf_op jit(solution)/shard_map/ppermute | solution.py:295
  40.2 11.7 %collective-permute-start.5 = (bf16[256,256]{1,0:T(8,128)(2,1)S(1)}, bf16[256,256]{1,0:T(8,128)(2,1)S(1)}, u32[]{:S(2)}, u32[]{:S(2)}) collective-permute-start(bf16[256,256]{1,0:T(8,128)(2,1)S(1)} %get-tuple-element.93), channel_id=1, source_target_pairs={{0,16},{2,18},{4,20},{6,22},{8,24},{10,26},{12,28},{14,30},{16,0},... | collective-permute-start | bytes 393224 | tf_op jit(solution)/shard_map/ppermute | solution.py:295
  42.8 9.1 %collective-permute-start.6 = (bf16[256,256]{1,0:T(8,128)(2,1)S(1)}, bf16[256,256]{1,0:T(8,128)(2,1)S(1)}, u32[]{:S(2)}, u32[]{:S(2)}) collective-permute-start(bf16[256,256]{1,0:T(8,128)(2,1)S(1)} %get-tuple-element.93), channel_id=1, source_target_pairs={{0,24},{2,26},{4,28},{6,30},{8,16},{10,18},{12,20},{14,22},{16,8},... | collective-permute-start | bytes 393224 | tf_op jit(solution)/shard_map/ppermute | solution.py:295
  48.1 19.6 %copy-start.18 = (bf16[4,256,256]{2,1,0:T(8,128)(2,1)}, bf16[4,256,256]{2,1,0:T(8,128)(2,1)S(1)}, u32[]{:S(2)}) copy-start(bf16[4,256,256]{2,1,0:T(8,128)(2,1)S(1)} %collective-permute-done.7.refs_6_) | copy-start | bytes 1572868
  52.0 15.8 %copy-start.11 = (bf16[4,256,256]{2,1,0:T(8,128)(2,1)}, bf16[4,256,256]{2,1,0:T(8,128)(2,1)S(1)}, u32[]{:S(2)}) copy-start(bf16[4,256,256]{2,1,0:T(8,128)(2,1)S(1)} %maximum_add_fusion.1.refs_8_.refs_4_) | copy-start | bytes 1572868
  54.0 157.2 %reduce-scatter.2.cloned.1.call-start = ((), (), s32[]{:S(2)}) async-start(), calls=%async_computation.2 | async-start | bytes 4456448 | tf_op jit(solution)/shard_map/reduce_scatter | solution.py:440
  54.1 10.0 %collective-permute-start.9 = (bf16[4,256,256]{2,1,0:T(8,128)(2,1)S(1)}, bf16[4,256,256]{2,1,0:T(8,128)(2,1)}, u32[]{:S(2)}, u32[]{:S(2)}) collective-permute-start(bf16[4,256,256]{2,1,0:T(8,128)(2,1)S(1)} %maximum_add_fusion.1.refs_8_.refs_4_), channel_id=1, source_target_pairs={{0,4},{2,6},{4,0},{6,2},{8,12},{10,14},{12,8},{14,10},{16,20},{18,... | collective-permute-start | bytes 1572872 | tf_op jit(solution)/shard_map/ppermute | solution.py:295
  57.3 10.5 %collective-permute-start.11 = (bf16[4,256,256]{2,1,0:T(8,128)(2,1)S(1)}, bf16[4,256,256]{2,1,0:T(8,128)(2,1)}, u32[]{:S(2)}, u32[]{:S(2)}) collective-permute-start(bf16[4,256,256]{2,1,0:T(8,128)(2,1)S(1)} %maximum_add_fusion.refs_4_), channel_id=1, source_target_pairs={{0,2},{2,0},{4,6},{6,4},{8,10},{10,8},{12,14},{14,12},{16,18},{18,... | collective-permute-start | bytes 1572872 | tf_op jit(solution)/shard_map/ppermute | solution.py:295
  57.4 10.5 %collective-permute-start.12 = (bf16[4,256,256]{2,1,0:T(8,128)(2,1)S(1)}, bf16[4,256,256]{2,1,0:T(8,128)(2,1)}, u32[]{:S(2)}, u32[]{:S(2)}) collective-permute-start(bf16[4,256,256]{2,1,0:T(8,128)(2,1)S(1)} %collective-permute-done.7.refs_6_), channel_id=1, source_target_pairs={{0,2},{2,0},{4,6},{6,4},{8,10},{10,8},{12,14},{14,12},{16,18},{18,... | collective-permute-start | bytes 1572872 | tf_op jit(solution)/shard_map/ppermute | solution.py:295
  59.7 36.4 %collective-permute-start.8 = (bf16[4,256,256]{2,1,0:T(8,128)(2,1)S(1)}, bf16[4,256,256]{2,1,0:T(8,128)(2,1)}, u32[]{:S(2)}, u32[]{:S(2)}) collective-permute-start(bf16[4,256,256]{2,1,0:T(8,128)(2,1)S(1)} %maximum_add_fusion.1.refs_8_.refs_4_), channel_id=1, source_target_pairs={{0,2},{2,0},{4,6},{6,4},{8,10},{10,8},{12,14},{14,12},{16,18},{18,... | collective-permute-start | bytes 1572872 | tf_op jit(solution)/shard_map/ppermute | solution.py:295
  64.1 32.1 %collective-permute-start.10 = (bf16[4,256,256]{2,1,0:T(8,128)(2,1)}, bf16[4,256,256]{2,1,0:T(8,128)(2,1)}, u32[]{:S(2)}, u32[]{:S(2)}) collective-permute-start(bf16[4,256,256]{2,1,0:T(8,128)(2,1)} %collective-permute-done.9.refs_6_), channel_id=1, source_target_pairs={{0,2},{2,0},{4,6},{6,4},{8,10},{10,8},{12,14},{14,12},{16,18},{18,... | collective-permute-start | bytes 1572872 | tf_op jit(solution)/shard_map/ppermute | solution.py:295
  153.7 29.1 %collective-permute-start.13 = (bf16[2,4,256,256]{3,2,1,0:T(8,128)(2,1)}, bf16[2,4,256,256]{3,2,1,0:T(8,128)(2,1)}, u32[]{:S(2)}, u32[]{:S(2)}) collective-permute-start(bf16[2,4,256,256]{3,2,1,0:T(8,128)(2,1)} %get-tuple-element.49), channel_id=1, source_target_pairs={{0,2},{2,0},{4,6},{6,4},{8,10},{10,8},{12,14},{14,12},{16,18},{18,... | collective-permute-start | bytes 3145736 | tf_op jit(solution)/shard_map/ppermute | solution.py:295
  154.3 28.5 %copy-start.4 = (bf16[4,256,256]{2,1,0:T(8,128)(2,1)S(1)}, bf16[4,256,256]{2,1,0:T(8,128)(2,1)}, u32[]{:S(2)}) copy-start(bf16[4,256,256]{2,1,0:T(8,128)(2,1)} %get-tuple-element.47.keep) | copy-start | bytes 1572868
  182.7 26.0 %collective-permute-start.15 = (bf16[2,4,256,256]{3,2,1,0:T(8,128)(2,1)}, bf16[2,4,256,256]{3,2,1,0:T(8,128)(2,1)S(1)}, u32[]{:S(2)}, u32[]{:S(2)}) collective-permute-start(bf16[2,4,256,256]{3,2,1,0:T(8,128)(2,1)} %get-tuple-element.56), channel_id=1, source_target_pairs={{0,2},{2,0},{4,6},{6,4},{8,10},{10,8},{12,14},{14,12},{16,18},{18,... | collective-permute-start | bytes 3145736 | tf_op jit(solution)/shard_map/ppermute | solution.py:295
  182.8 1.0 copy-start
  183.8 1.0 copy-start.5
  186.9 16.9 %collective-permute-start.16 = (bf16[4,256,256]{2,1,0:T(8,128)(2,1)S(1)}, bf16[4,256,256]{2,1,0:T(8,128)(2,1)S(1)}, u32[]{:S(2)}, u32[]{:S(2)}) collective-permute-start(bf16[4,256,256]{2,1,0:T(8,128)(2,1)S(1)} %get-tuple-element.51.refs_0_), channel_id=1, source_target_pairs={{0,4},{2,6},{4,0},{6,2},{8,12},{10,14},{12,8},{14,10},{16,20},{18,... | collective-permute-start | bytes 1572872 | tf_op jit(solution)/shard_map/ppermute | solution.py:295
  189.1 19.7 %copy-start.2 = (bf16[4,256,256]{2,1,0:T(8,128)(2,1)S(1)}, bf16[4,256,256]{2,1,0:T(8,128)(2,1)}, u32[]{:S(2)}) copy-start(bf16[4,256,256]{2,1,0:T(8,128)(2,1)} %get-tuple-element.54.keep) | copy-start | bytes 1572868
  189.1 19.7 %copy-start.3 = (bf16[4,256,256]{2,1,0:T(8,128)(2,1)S(1)}, bf16[4,256,256]{2,1,0:T(8,128)(2,1)}, u32[]{:S(2)}) copy-start(bf16[4,256,256]{2,1,0:T(8,128)(2,1)} %get-tuple-element.55.cross) | copy-start | bytes 1572868
  191.9 38.8 %collective-permute-start.14 = (bf16[128,4096]{1,0:T(8,128)(2,1)}, bf16[128,4096]{1,0:T(8,128)(2,1)}, u32[]{:S(2)}, u32[]{:S(2)}) collective-permute-start(bf16[128,4096]{1,0:T(8,128)(2,1)} %add_convert_fusion.1), channel_id=1, source_target_pairs={{0,1},{1,0},{2,3},{3,2},{4,5},{5,4},{6,7},{7,6},{8,9},{9,8},{10,11... | collective-permute-start | bytes 3145736 | tf_op jit(solution)/shard_map/ppermute | solution.py:453
  204.1 5.1 %copy-start.6 = (bf16[256,256]{1,0:T(8,128)(2,1)}, bf16[256,256]{1,0:T(8,128)(2,1)S(1)}, u32[]{:S(2)}) copy-start(bf16[256,256]{1,0:T(8,128)(2,1)S(1)} %get-tuple-element.62) | copy-start | bytes 393220
  204.1 5.1 %copy-start.8 = (bf16[256,256]{1,0:T(8,128)(2,1)}, bf16[256,256]{1,0:T(8,128)(2,1)S(1)}, u32[]{:S(2)}) copy-start(bf16[256,256]{1,0:T(8,128)(2,1)S(1)} %get-tuple-element.61) | copy-start | bytes 393220
  204.1 8.1 %copy-start.13 = (f32[256,256]{1,0:T(8,128)S(1)}, f32[256,256]{1,0:T(8,128)}, u32[]{:S(2)}) copy-start(f32[256,256]{1,0:T(8,128)} %get-tuple-element.39.refs_11_) | copy-start | bytes 786436
  204.1 8.1 %copy-start.14 = (f32[256,256]{1,0:T(8,128)S(1)}, f32[256,256]{1,0:T(8,128)}, u32[]{:S(2)}) copy-start(f32[256,256]{1,0:T(8,128)} %get-tuple-element.42.refs_7_) | copy-start | bytes 786436
  204.1 10.7 %collective-permute-start.17 = (bf16[256,256]{1,0:T(8,128)(2,1)S(1)}, bf16[256,256]{1,0:T(8,128)(2,1)}, u32[]{:S(2)}, u32[]{:S(2)}) collective-permute-start(bf16[256,256]{1,0:T(8,128)(2,1)S(1)} %get-tuple-element.58.refs_0_), channel_id=1, source_target_pairs={{0,8},{2,10},{4,12},{6,14},{8,0},{10,2},{12,4},{14,6},{16,24},{18,... | collective-permute-start | bytes 393224 | tf_op jit(solution)/shard_map/ppermute | solution.py:295
  209.2 14.4 %copy-start.15 = (f32[256,256]{1,0:T(8,128)S(1)}, f32[256,256]{1,0:T(8,128)}, u32[]{:S(2)}) copy-start(f32[256,256]{1,0:T(8,128)} %get-tuple-element.45.refs_7_) | copy-start | bytes 786436
  209.2 3.6 %copy-start.7 = (bf16[256,256]{1,0:T(8,128)(2,1)S(1)}, bf16[256,256]{1,0:T(8,128)(2,1)}, u32[]{:S(2)}) copy-start(bf16[256,256]{1,0:T(8,128)(2,1)} %copy-done.6) | copy-start | bytes 393220
  209.2 15.4 %collective-permute-start.20 = (bf16[4,256,256]{2,1,0:T(8,128)(2,1)S(1)}, bf16[4,256,256]{2,1,0:T(8,128)(2,1)S(1)}, u32[]{:S(2)}, u32[]{:S(2)}) collective-permute-start(bf16[4,256,256]{2,1,0:T(8,128)(2,1)S(1)} %get-tuple-element.59.refs_0_), channel_id=1, source_target_pairs={{0,4},{2,6},{4,0},{6,2},{8,12},{10,14},{12,8},{14,10},{16,20},{18,... | collective-permute-start | bytes 1572872 | tf_op jit(solution)/shard_map/ppermute | solution.py:295
  209.5 2.8 %copy-start.9 = (bf16[256,256]{1,0:T(8,128)(2,1)S(1)}, bf16[256,256]{1,0:T(8,128)(2,1)}, u32[]{:S(2)}) copy-start(bf16[256,256]{1,0:T(8,128)(2,1)} %copy-done.8) | copy-start | bytes 393220
  212.2 18.4 %copy-start.10 = (f32[256,4096]{1,0:T(8,128)S(1)}, f32[256,4096]{1,0:T(8,128)}, u32[]{:S(2)}) copy-start(f32[256,4096]{1,0:T(8,128)} %get-tuple-element.46) | copy-start | bytes 12582916
  212.3 11.3 %collective-permute-start.18 = (bf16[256,256]{1,0:T(8,128)(2,1)S(1)}, bf16[256,256]{1,0:T(8,128)(2,1)S(1)}, u32[]{:S(2)}, u32[]{:S(2)}) collective-permute-start(bf16[256,256]{1,0:T(8,128)(2,1)S(1)} %copy-done.9), channel_id=1, source_target_pairs={{0,16},{2,18},{4,20},{6,22},{8,24},{10,26},{12,28},{14,30},{16,0},... | collective-permute-start | bytes 393224 | tf_op jit(solution)/shard_map/ppermute | solution.py:295
  212.8 10.8 %collective-permute-start.19 = (bf16[256,256]{1,0:T(8,128)(2,1)S(1)}, bf16[256,256]{1,0:T(8,128)(2,1)S(1)}, u32[]{:S(2)}, u32[]{:S(2)}) collective-permute-start(bf16[256,256]{1,0:T(8,128)(2,1)S(1)} %copy-done.7), channel_id=1, source_target_pairs={{0,24},{2,26},{4,28},{6,30},{8,16},{10,18},{12,20},{14,22},{16,8},... | collective-permute-start | bytes 393224 | tf_op jit(solution)/shard_map/ppermute | solution.py:295
  224.9 8.2 %collective-permute-start.21 = (bf16[256,256]{1,0:T(8,128)(2,1)S(1)}, bf16[256,256]{1,0:T(8,128)(2,1)S(1)}, u32[]{:S(2)}, u32[]{:S(2)}) collective-permute-start(bf16[256,256]{1,0:T(8,128)(2,1)S(1)} %get-tuple-element.65), channel_id=1, source_target_pairs={{0,8},{2,10},{4,12},{6,14},{8,0},{10,2},{12,4},{14,6},{16,24},{18,... | collective-permute-start | bytes 393224 | tf_op jit(solution)/shard_map/ppermute | solution.py:295
  228.2 12.5 %collective-permute-start.22 = (bf16[256,256]{1,0:T(8,128)(2,1)S(1)}, bf16[256,256]{1,0:T(8,128)(2,1)S(1)}, u32[]{:S(2)}, u32[]{:S(2)}) collective-permute-start(bf16[256,256]{1,0:T(8,128)(2,1)S(1)} %get-tuple-element.66), channel_id=1, source_target_pairs={{0,16},{2,18},{4,20},{6,22},{8,24},{10,26},{12,28},{14,30},{16,0},... | collective-permute-start | bytes 393224 | tf_op jit(solution)/shard_map/ppermute | solution.py:295
  228.2 12.5 %copy-start.1 = (f32[256,256]{1,0:T(8,128)S(1)}, f32[256,256]{1,0:T(8,128)}, u32[]{:S(2)}) copy-start(f32[256,256]{1,0:T(8,128)} %get-tuple-element.50.refs_0_) | copy-start | bytes 786436
  228.2 12.5 %collective-permute-start.23 = (bf16[256,256]{1,0:T(8,128)(2,1)S(1)}, bf16[256,256]{1,0:T(8,128)(2,1)S(1)}, u32[]{:S(2)}, u32[]{:S(2)}) collective-permute-start(bf16[256,256]{1,0:T(8,128)(2,1)S(1)} %get-tuple-element.67), channel_id=1, source_target_pairs={{0,24},{2,26},{4,28},{6,30},{8,16},{10,18},{12,20},{14,22},{16,8},... | collective-permute-start | bytes 393224 | tf_op jit(solution)/shard_map/ppermute | solution.py:295
Sparse Core Ops, SparseCore 0:
  54.1 50.3 all-gather.1
  124.8 79.9 reduce-scatter.1
